TPU v7x, 512 devices: a whole 4x8x8 slice. The times are simulated.
512 devices in a mesh: ctx: 64 (over z, x, core), tp: 8 (over y).
Axes of the slice: x: 4, y: 8, z: 8, core: 2. Of those that a mesh axis runs over, the one named last changes fastest.
Arguments:
- inner_input: bfloat16 [8192, 8192], P('ctx', 'tp'), may hold values from -6 to 6
- gate_input: bfloat16 [8192, 8192], P('ctx', 'tp'), may hold values from -6 to 6
- state_inputs: bfloat16 [2, 8192, 1024], P(None, 'ctx', 'tp'), may hold values from -6 to 6
- step_size: float32 [128, 8192], P('tp', 'ctx'), may hold values from 0.5 to 2
- resets: int32 [8192], P('ctx'), may hold values 0 or 1
- decay_rate: float32 [128], P('tp'), may hold values from 0 to 0.04
- skip_gain: float32 [128], P('tp'), may hold values from 0.5 to 1.5
- conv_inner: float32 [4, 8192], P(None, 'tp'), may hold values from -3 to 3
- conv_state: float32 [2, 4, 1024], P(None, None, 'tp'), may hold values from -3 to 3
- norm_gain: float32 [8192], P('tp'), may hold values from 0.5 to 1.5
- out_weight: bfloat16 [8192, 4096], P('tp', 'ctx'), may hold values from -0.0625 to 0.0625
- residual: bfloat16 [8192, 4096], P('ctx', 'tp'), may hold values from -6 to 6
- final_gain: float32 [4096], replicated, may hold values from 0.5 to 1.5
- head_weight: bfloat16 [4096, 65536], P(None, ('ctx', 'tp')), may hold values from -8 to 8
- scored: int32 [512], P('ctx'), may hold values from 0 to 8191, as said below
- targets: int32 [512], replicated, may hold values from 0 to 65535
- policy_logprob: float32 [512], replicated, may hold values from -20 to -10
Outputs:
- ref_logprob: float32 [512], replicated
- token_kl: float32 [512], replicated
Inputs may be any that keep to these rules, and one draw needn't show every extreme that they name: `scored`: entries j * 8 to (j + 1) * 8 - 1 are distinct positions in j * 128 to (j + 1) * 128 - 1.
All inputs are finite; a program needn't handle non-finite values. No bound on the sum of `resets` on one device may be relied on, other than what follows from the above.
Results may differ from a plain program's by a relative error of at most 0.00215.
The roundings to bfloat16 on the way count: a program that leaves them out, or rounds other values in their place, can miss the bound.
Values may be sent and summed in bfloat16 or wider, within the bound.
No kernel may reach another device: no remote copies, remote signals or barrier semaphores. Data moves between devices by JAX's collectives and lax.ppermute only.
A program may use at most 128 MiB of HBM per device.

v0:
```python
import jax
import jax.numpy as jnp
from jax import lax
from jax.sharding import Mesh
from jax.sharding import PartitionSpec as P

HEAD_DIM = 64
STATE = 128
SPAN = 128
CTX = ("ctx_0", "ctx_1", "ctx_2")
CTX_TP = ("ctx_0", "ctx_1", "ctx_2", "tp")


epsilon = 1e-05
precise = lax.Precision.HIGHEST


def passed_along(shard, axis, by):
    count = lax.axis_size(axis)
    pairs = [(i, i + by) for i in range(count) if 0 <= i + by < count]
    return lax.ppermute(shard, axis, pairs)


def filled_with(shard, identity):
    return jax.tree.map(
        lambda a, e: jnp.broadcast_to(jnp.asarray(e, a.dtype), a.shape), shard, identity
    )


def entering_2(shard, axes, combine, identity):
    before = start = filled_with(shard, identity)
    subtotal = shard
    for axis in reversed(axes):
        count, place = (lax.axis_size(axis), lax.axis_index(axis))
        pieces = jax.tree.map(lambda part: lax.all_gather(part, axis), subtotal)
        inside, subtotal = (start, start)
        for k in range(count):
            passed = k < place
            subtotal = combine(subtotal, jax.tree.map(lambda part: part[k], pieces))
            inside = jax.tree.map(lambda new, old: jnp.where(passed, new, old), subtotal, inside)
        before = combine(inside, before)
    return before


def laid_out(blocks, dim):
    lengths = list(blocks.shape[1:])
    lengths[dim] *= blocks.shape[0]
    return jnp.moveaxis(blocks, 0, dim).reshape(lengths)


def from_everyone(shard, axis):
    count = lax.axis_size(axis)
    return lax.all_to_all(
        jnp.broadcast_to(shard[None], (count, *shard.shape)), axis, 0, 0, tiled=True
    )


def collect(shard, axis, dim):
    return laid_out(from_everyone(shard, axis), dim)


def of_everyone(shard, axis):
    return from_everyone(shard, axis).sum(axis=0)


def gather_in_order(shard, axes, order):
    blocks = shard[None]
    for k in order:
        blocks = lax.all_gather(blocks, axes[k], axis=0, tiled=True)
    block = [lax.axis_size(axes[k]) for k in reversed(order)]
    blocks = blocks.reshape(*block, *shard.shape)
    turned = sorted(range(len(order)), key=lambda place: order[len(order) - 1 - place])
    return blocks.transpose(*turned, *range(len(order), blocks.ndim)).reshape(-1, *shard.shape)


def gather_axes(shard, axes, order, dim):
    return laid_out(gather_in_order(shard, axes, order), dim)


def gathered_once(shard, axis):
    leaves = jax.tree.leaves(shard)
    order = sorted(range(len(leaves)), key=lambda k: -leaves[k].size)
    width = (1, *leaves[order[0]].shape)[-1]
    lines = [
        jnp.pad(leaves[k].reshape(-1), (0, -leaves[k].size % width)).reshape(-1, width)
        for k in order
    ]
    both, at, found = (lax.all_gather(jnp.concatenate(lines), axis), 0, {})
    for k, line in zip(order, lines):
        piece = both[:, at : at + len(line)].reshape(len(both), -1)
        found[k] = piece[:, : leaves[k].size].reshape(-1, *leaves[k].shape)
        at += len(line)
    numbers = iter(range(len(leaves)))
    return jax.tree.map(lambda _: found[next(numbers)], shard)


def combined_by_axis(shard, axes, combine):
    for axis in axes:
        pieces = gathered_once(shard, axis)
        shard = jax.tree.map(lambda part: part[0], pieces)
        for k in range(1, lax.axis_size(axis)):
            shard = combine(shard, jax.tree.map(lambda part: part[k], pieces))
    return shard


def causal_filter(stream, tail_rows, kernel, keeping):
    kernel_taps = kernel.shape[0]
    rows_here = stream.shape[0]
    padded = jnp.concatenate([tail_rows, stream], axis=0).astype(jnp.float32)
    summed = jnp.zeros((rows_here, stream.shape[1]), jnp.float32)
    for offset in range(kernel_taps):
        anchor = kernel_taps - 1 - offset
        summed = (
            summed
            + keeping[offset][:, None]
            * kernel[offset][None, :]
            * padded[anchor : anchor + rows_here]
        )
    return jax.nn.silu(summed).astype(jnp.bfloat16)


def join_states(earlier, later):
    return (earlier[0] * later[0], later[0][:, None, None] * earlier[1] + later[1])


def join_partials(former, latter):
    row_top = jnp.maximum(former[0], latter[0])
    weight_former = jnp.exp(former[0] - row_top)
    weight_latter = jnp.exp(latter[0] - row_top)
    return (row_top, former[1] * weight_former + latter[1] * weight_latter, former[2] + latter[2])


def normalize_rows(hidden, squares, gain_part, row_width):
    return (
        hidden.astype(jnp.float32)
        * lax.rsqrt(squares / row_width + epsilon)[:, None]
        * gain_part[None, :]
    ).astype(jnp.bfloat16)


def pick_logit(logits, target_column):
    columns = jnp.arange(logits.shape[1], dtype=jnp.int32)
    return jnp.sum(jnp.where(columns[None, :] == target_column[:, None], logits, 0.0), axis=1)


def summarize_logits(logits, target_column):
    row_top = jnp.max(logits, axis=1)
    summed = jnp.sum(jnp.exp(logits - row_top[:, None]), axis=1)
    return jnp.stack([row_top, summed, pick_logit(logits, target_column)], axis=1)


def body(
    inner_input,
    gate_input,
    state_inputs,
    step_size,
    resets,
    decay_rate,
    skip_gain,
    conv_inner,
    conv_state,
    norm_gain,
    out_weight,
    residual,
    final_gain,
    head_weight,
    scored,
    targets,
    policy_logprob,
):
    kernel_taps = conv_inner.shape[0]
    rows_here = inner_input.shape[0]
    head_count = step_size.shape[0]
    group_count = state_inputs.shape[2] // STATE
    per_group = head_count // group_count
    margin = kernel_taps - 1
    inner_tail, state_tail, reset_tail = passed_along(
        (
            inner_input[rows_here - margin :],
            state_inputs[:, rows_here - margin :],
            resets[rows_here - margin :].astype(jnp.bfloat16),
        ),
        CTX,
        1,
    )
    flags = jnp.concatenate([reset_tail.astype(jnp.float32), resets.astype(jnp.float32)])
    counted = jnp.cumsum(flags)
    keeping = jnp.stack(
        [
            (
                counted[margin:] - counted[margin - offset : margin - offset + rows_here] == 0.0
            ).astype(jnp.float32)
            for offset in range(kernel_taps)
        ]
    )
    inner_conv = causal_filter(inner_input, inner_tail, conv_inner, keeping)
    write_map = causal_filter(state_inputs[0], state_tail[0], conv_state[0], keeping)
    read_map = causal_filter(state_inputs[1], state_tail[1], conv_state[1], keeping)
    spans = rows_here // SPAN
    values = inner_conv.reshape(spans, SPAN, head_count, HEAD_DIM)
    writes = write_map.reshape(spans, SPAN, group_count, STATE)
    reads = read_map.reshape(spans, SPAN, group_count, STATE)
    steps_blocked = step_size.reshape(head_count, spans, SPAN).transpose(1, 0, 2)
    cumulated = jnp.cumsum(-decay_rate[None, :, None] * steps_blocked, axis=2)
    segment = jnp.cumsum(resets.reshape(spans, SPAN), axis=1)
    positions = jnp.arange(SPAN)
    causal = (positions[None, :, None] >= positions[None, None, :]) & (
        segment[:, :, None] == segment[:, None, :]
    )
    gaps = cumulated[:, :, :, None] - cumulated[:, :, None, :]
    decay_matrix = jnp.where(causal[:, None], jnp.exp(jnp.where(causal[:, None], gaps, 0.0)), 0.0)
    scores = jnp.einsum("kign,kjgn->kgij", reads, writes, preferred_element_type=jnp.float32)
    mixing = jnp.repeat(scores, per_group, axis=1) * decay_matrix * steps_blocked[:, :, None, :]
    values_wide = values.astype(jnp.float32)
    within = jnp.einsum("khij,kjhp->kihp", mixing, values_wide, precision=precise)
    writes_heads = jnp.repeat(writes, per_group, axis=2).astype(jnp.float32)
    reads_heads = jnp.repeat(reads, per_group, axis=2).astype(jnp.float32)
    to_end = (
        jnp.exp(cumulated[:, :, -1:] - cumulated)
        * (segment[:, None, :] == segment[:, None, -1:])
        * steps_blocked
    )
    weighted = values_wide * to_end.transpose(0, 2, 1)[:, :, :, None]
    span_states = jnp.einsum("kjhp,kjhn->khpn", weighted, writes_heads, precision=precise)
    span_decay = jnp.exp(cumulated[:, :, -1]) * (segment[:, -1] == 0)[:, None]
    from_start = jnp.exp(cumulated) * (segment == 0)[:, None, :]

    def advance(running, item):
        return (item[0][:, None, None] * running + item[1], running)

    empty_state = jnp.zeros((head_count, HEAD_DIM, STATE), jnp.float32)
    device_state, entering = lax.scan(advance, empty_state, (span_decay, span_states))
    decay_prefix = jnp.cumprod(span_decay, axis=0)
    before = jnp.concatenate([jnp.ones((1, head_count), jnp.float32), decay_prefix[:-1]], axis=0)
    incoming = entering_2(
        (decay_prefix[-1], device_state),
        CTX,
        join_states,
        (jnp.ones((head_count,), jnp.float32), empty_state),
    )
    entering = entering + before[:, :, None, None] * incoming[1][None]
    across = (
        jnp.einsum("kihn,khpn->kihp", reads_heads, entering, precision=precise)
        * from_start.transpose(0, 2, 1)[:, :, :, None]
    )
    mixed_out = (within + across).reshape(rows_here, head_count * HEAD_DIM) + jnp.repeat(
        skip_gain, HEAD_DIM
    )[None, :] * values_wide.reshape(rows_here, head_count * HEAD_DIM)
    gated = mixed_out * jax.nn.silu(gate_input.astype(jnp.float32))
    grouped = gated.reshape(rows_here, group_count, -1)
    inverse_rms = lax.rsqrt(jnp.mean(grouped * grouped, axis=2, keepdims=True) + epsilon)
    normed = ((grouped * inverse_rms).reshape(rows_here, -1) * norm_gain[None, :]).astype(
        jnp.bfloat16
    )
    local_rows = scored - lax.axis_index(CTX) * rows_here
    every_normed = collect(normed[local_rows], CTX, 0)
    partial_rows = jnp.dot(every_normed, out_weight, preferred_element_type=jnp.float32)
    summed_rows = of_everyone(partial_rows, "tp")
    returned = lax.all_to_all(summed_rows, CTX, split_axis=0, concat_axis=1, tiled=True)
    width_part = residual.shape[1]
    own_columns = lax.dynamic_slice_in_dim(
        returned, lax.axis_index("tp") * width_part, width_part, 1
    )
    hidden = (residual[local_rows].astype(jnp.float32) + own_columns).astype(jnp.bfloat16)
    model_width = final_gain.shape[0]
    vocab_part = head_weight.shape[1]
    vocab_start = (lax.axis_index(CTX) * lax.axis_size("tp") + lax.axis_index("tp")) * vocab_part
    target_column = targets - vocab_start
    features = collect(hidden, "tp", 1)
    features = normalize_rows(
        features, jnp.sum(jnp.square(features.astype(jnp.float32)), axis=1), final_gain, model_width
    )
    outcome = summarize_logits(
        jnp.dot(
            gather_axes(features, CTX, (1, 0, 2), 0),
            head_weight,
            preferred_element_type=jnp.float32,
        ),
        target_column,
    )
    row_top, summed, picked = combined_by_axis(
        (outcome[:, 0], outcome[:, 1], outcome[:, 2]), CTX_TP, join_partials
    )
    ref_logprob = picked - row_top - jnp.log(summed)
    token_kl = 0.5 * jnp.square(ref_logprob - policy_logprob)
    return (ref_logprob, token_kl)


def solution(mesh):
    finer = Mesh(mesh.devices.reshape(8, 4, 2, mesh.shape["tp"]), ("ctx_0", "ctx_1", "ctx_2", "tp"))
    placed = (
        P(CTX, "tp"),
        P(CTX, "tp"),
        P(None, CTX, "tp"),
        P("tp", CTX),
        P(CTX),
        P("tp"),
        P("tp"),
        P(None, "tp"),
        P(None, None, "tp"),
        P("tp"),
        P("tp", CTX),
        P(CTX, "tp"),
        P(),
        P(None, CTX_TP),
        P(CTX),
        P(),
        P(),
    )
    return jax.shard_map(body, mesh=finer, in_specs=placed, out_specs=(P(), P()), check_vma=False)
```

profile of v0, /device:TPU:1, one launch (start us, length us, event | category | flops | bytes accessed | tf_op | source)
XLA Modules:
  0.0 408.2 jit_solution(529203863400693494)
XLA Ops:
  7.2 0.8 fusion.164
  8.1 4.5 %collective-permute-start = (bf16[3]{0:T(256)(128)(2,1)S(1)}, bf16[3]{0:T(256)(128)(2,1)S(1)}, u32[]{:S(2)}, u32[]{:S(2)}) collective-permute-start(bf16[3]{0:T(256)(128)(2,1)S(1)} %slice.577), channel_id=1, source_target_pairs={{0,8},{8,16},{16,24},{24,32},{32,40},{40,48},{48,56},{56,64},{64,7... | collective-permute-start | bytes 26 | tf_op jit(solution)/shard_map/ppermute | solution.py:21
  12.6 0.7 slice.595
  13.3 1.9 collective-permute-start.2
  15.2 0.7 slice.582
  15.9 3.5 collective-permute-start.1
  19.4 0.8 slice_bitcast_fusion.3
  20.2 1.4 slice_bitcast_fusion.48
  21.6 0.9 fusion.163
  22.5 1.0 reduce_window_sum.39
  25.3 1.1 compare_convert_fusion
  26.5 0.8 multiply_bitcast_fusion.2
  27.7 0.8 multiply_bitcast_fusion.1
  30.1 1.0 maximum_convert_fusion
  31.9 1.3 convolution_add_fusion
  33.3 2.3 all-gather.5
  35.6 7.9 %all-gather.6 = f32[4,1,16]{2,1,0:T(1,128)S(1)} all-gather(f32[1,1,16]{2,1,0:T(1,128)S(1)} %get-tuple-element.80), channel_id=1, replica_groups=mesh['ctx_0'=8,'ctx_1'=4,'ctx_2'=2,'tp'=8] {'ctx_1'}, dimensions={0}, use_global_device_ids=true | all-gather | bytes 320 | tf_op jit(solution)/shard_map/all_gather | solution.py:35
  44.1 11.7 %all-gather.26.cloned.1.call-done = f32[32,64,128]{2,1,0:T(8,128)} async-done(((f32[16,64,128]{2,1,0:T(8,128)}), f32[32,64,128]{2,1,0:T(8,128)}) %all-gather.26.cloned.1.call-update) | async-done | bytes 1048592 | tf_op jit(solution)/shard_map/all_gather | solution.py:35
  55.8 2.3 fusion.19
  58.7 35.5 %all-gather.18.cloned.1.call-done = f32[4,16,64,128]{3,2,1,0:T(8,128)} async-done(((f32[1,16,64,128]{3,2,1,0:T(8,128)}), f32[4,16,64,128]{3,2,1,0:T(8,128)}) %all-gather.18.cloned.1.call-update) | async-done | bytes 2097168 | tf_op jit(solution)/shard_map/all_gather | solution.py:35
  94.2 2.5 slice_add_fusion.8
  96.8 0.7 broadcast_in_dim.46
  97.6 13.5 %all-gather.7 = f32[8,1,16]{2,1,0:T(1,128)S(1)} all-gather(f32[1,1,16]{2,1,0:T(1,128)} %get-tuple-element.72), channel_id=1, replica_groups=mesh['ctx_0'=8,'ctx_1'=4,'ctx_2'=2,'tp'=8] {'ctx_0'}, dimensions={0}, use_global_device_ids=true | all-gather | bytes 576 | tf_op jit(solution)/shard_map/all_gather | solution.py:35
  112.4 1.2 multiply_bitcast_fusion
  113.5 1.4 fusion.92
  114.9 0.7 maximum_convert_fusion.1
  115.6 0.8 multiply_convert_fusion.4
  116.4 0.8 fusion.166
  117.2 38.1 %all-gather.20.cloned.1.call-done = f32[8,16,64,128]{3,2,1,0:T(8,128)} async-done(((f32[1,16,64,128]{3,2,1,0:T(8,128)}), f32[8,16,64,128]{3,2,1,0:T(8,128)}) %all-gather.20.cloned.1.call-update) | async-done | bytes 4194320 | tf_op jit(solution)/shard_map/all_gather | solution.py:35
  155.3 4.5 %fusion.1 = f32[1,128,16,64]{1,3,2,0:T(8,128)S(1)} fusion(f32[8,16,64,128]{3,2,1,0:T(8,128)} %all-gather.20.cloned.1.call-done, f32[1,16,64,128]{3,2,1,0:T(8,128)S(1)} %copy-done.1, f32[1,16,64,128]{3,2,1,0:T(8,128)} %slice_add_fusion.8, f32[4,16,64,128]{3,2,1,0:T(8,128)} %all-gather.18.cloned.1.call-done, f32[32,64,128]{2,1,0:T(8,128)S(1)} %copy-done.2, ...), kind=kOutput, calls=%fused_computation.6 | convolution fusion | flops 206569472 | bytes 7912462 | tf_op jit(solution)/shard_map/kihn,khpn->kihp/dot_general | solution.py:243
  159.8 1.3 fusion
  161.4 1.7 multiply_reduce_fusion
  164.0 35.7 %all_to_all.34 = bf16[64,8,1024]{2,1,0:T(8,128)(2,1)S(1)} all-to-all(bf16[64,8,1024]{2,1,0:T(8,128)(2,1)S(1)} %broadcast_in_dim.47), channel_id=1, replica_groups=mesh['ctx_0'=8,'ctx_1'=4,'ctx_2'=2,'tp'=8] {'ctx_0','ctx_1','ctx_2'}, dimensions={0} | all-to-all | bytes 2097152 | tf_op jit(solution)/shard_map/all_to_all | solution.py:53
  200.3 32.6 %all_to_all.35 = f32[8,512,64]{1,2,0:T(8,128)S(1)} all-to-all(f32[8,512,64]{1,2,0:T(8,128)S(1)} %broadcast_in_dim.48), channel_id=1, replica_groups=mesh['ctx_0'=8,'ctx_1'=4,'ctx_2'=2,'tp'=8] {'tp'}, dimensions={0} | all-to-all | bytes 2097152 | tf_op jit(solution)/shard_map/all_to_all | solution.py:53
  233.1 0.8 reshape.1464
  233.9 8.9 %all-to-all-start.2 = ((f32[64,1,512]{2,1,0:T(1,128)}), f32[64,1,512]{2,1,0:T(1,128)S(1)}, u32[]{:S(2)}, u32[]{:S(2)}) async-start(f32[64,1,512]{2,1,0:T(1,128)} %reshape.1464), calls=%async_computation.2 | async-start | bytes 262144 | tf_op jit(solution)/shard_map/all_to_all | solution.py:259
  243.5 10.5 %all-to-all-done.2 = f32[64,1,512]{2,1,0:T(1,128)S(1)} async-done(((f32[64,1,512]{2,1,0:T(1,128)}), f32[64,1,512]{2,1,0:T(1,128)S(1)}, u32[]{:S(2)}, u32[]{:S(2)}) %all-to-all-start.2) | async-done | bytes 131104 | tf_op jit(solution)/shard_map/all_to_all | solution.py:259
  254.5 0.9 reduce.10
  255.7 9.5 %all_to_all.36 = bf16[8,8,512]{2,1,0:T(8,128)(2,1)S(1)} all-to-all(bf16[8,8,512]{2,1,0:T(8,128)(2,1)S(1)} %broadcast_in_dim.49), channel_id=1, replica_groups=mesh['ctx_0'=8,'ctx_1'=4,'ctx_2'=2,'tp'=8] {'tp'}, dimensions={0} | all-to-all | bytes 131072 | tf_op jit(solution)/shard_map/all_to_all | solution.py:53
  265.5 10.1 %all_gather.62 = bf16[4,8,4096]{2,1,0:T(8,128)(2,1)} all-gather(bf16[1,8,4096]{2,1,0:T(8,128)(2,1)S(1)} %multiply_convert_fusion.2), channel_id=1, replica_groups=mesh['ctx_0'=8,'ctx_1'=4,'ctx_2'=2,'tp'=8] {'ctx_1'}, dimensions={0}, use_global_device_ids=true | all-gather | bytes 327680 | tf_op jit(solution)/shard_map/all_gather | solution.py:69
  275.7 34.8 %all-gather.22.cloned.1.call-done = bf16[32,8,4096]{2,1,0:T(8,128)(2,1)} async-done(((bf16[4,8,4096]{2,1,0:T(8,128)(2,1)}), bf16[32,8,4096]{2,1,0:T(8,128)(2,1)}) %all-gather.22.cloned.1.call-update) | async-done | bytes 2097168 | tf_op jit(solution)/shard_map/all_gather | solution.py:69
  310.6 27.3 %all-gather.24.cloned.1.call-done = bf16[64,8,4096]{2,1,0:T(8,128)(2,1)} async-done(((bf16[32,8,4096]{2,1,0:T(8,128)(2,1)}), bf16[64,8,4096]{2,1,0:T(8,128)(2,1)}) %all-gather.24.cloned.1.call-update) | async-done | bytes 4194320 | tf_op jit(solution)/shard_map/all_gather | solution.py:69
  337.9 2.5 copy.40
  340.4 1.6 fusion.165
  342.0 19.2 %all-gather.8 = f32[8,3,512]{2,1,0:T(4,128)S(1)} all-gather(f32[1,3,512]{2,1,0:T(4,128)S(1)} %maximum_bitcast_fusion), channel_id=3, replica_groups=mesh['ctx_0'=8,'ctx_1'=4,'ctx_2'=2,'tp'=8] {'ctx_0'}, dimensions={0}, use_global_device_ids=true | all-gather | bytes 55296 | tf_op jit(solution)/shard_map/all_gather | solution.py:88
  361.3 9.5 %all-gather.9 = f32[4,3,512]{2,1,0:T(4,128)S(1)} all-gather(f32[1,3,512]{2,1,0:T(4,128)S(1)} %maximum_bitcast_fusion.1), channel_id=4, replica_groups=mesh['ctx_0'=8,'ctx_1'=4,'ctx_2'=2,'tp'=8] {'ctx_1'}, dimensions={0}, use_global_device_ids=true | all-gather | bytes 30720 | tf_op jit(solution)/shard_map/all_gather | solution.py:88
  370.9 10.8 %all-gather.10 = f32[2,3,512]{2,1,0:T(4,128)S(1)} all-gather(f32[1,3,512]{2,1,0:T(4,128)S(1)} %maximum_bitcast_fusion.2), channel_id=5, replica_groups=mesh['ctx_0'=8,'ctx_1'=4,'ctx_2'=2,'tp'=8] {'ctx_2'}, dimensions={0}, use_global_device_ids=true | all-gather | bytes 18432 | tf_op jit(solution)/shard_map/all_gather | solution.py:88
  381.7 19.3 %all-gather.11 = f32[8,3,512]{2,1,0:T(4,128)S(1)} all-gather(f32[1,3,512]{2,1,0:T(4,128)S(1)} %maximum_bitcast_fusion.3), channel_id=6, replica_groups=mesh['ctx_0'=8,'ctx_1'=4,'ctx_2'=2,'tp'=8] {'tp'}, dimensions={0}, use_global_device_ids=true | all-gather | bytes 55296 | tf_op jit(solution)/shard_map/all_gather | solution.py:88
  (112 shorter events, 11.3 us)
Async XLA Ops:
  7.2 333.2 %copy-start = (bf16[4096,128]{1,0:T(8,128)(2,1)S(1)}, bf16[4096,128]{1,0:T(8,128)(2,1)}, u32[]{:S(2)}) copy-start(bf16[4096,128]{1,0:T(8,128)(2,1)} %param.30) | copy-start | bytes 3145732
  7.2 48.6 %all-gather.26.cloned.1.call-start = ((), (), s32[]{:S(2)}) async-start(), calls=%async_computation.8 | async-start | bytes 1572864 | tf_op jit(solution)/shard_map/all_gather | solution.py:35
  8.1 20.5 %collective-permute-start = (bf16[3]{0:T(256)(128)(2,1)S(1)}, bf16[3]{0:T(256)(128)(2,1)S(1)}, u32[]{:S(2)}, u32[]{:S(2)}) collective-permute-start(bf16[3]{0:T(256)(128)(2,1)S(1)} %slice.577), channel_id=1, source_target_pairs={{0,8},{8,16},{16,24},{24,32},{32,40},{40,48},{48,56},{56,64},{64,7... | collective-permute-start | bytes 26 | tf_op jit(solution)/shard_map/ppermute | solution.py:21
  13.3 16.1 %collective-permute-start.2 = (bf16[2,3,128]{2,1,0:T(4,128)(2,1)S(1)}, bf16[2,3,128]{2,1,0:T(4,128)(2,1)S(1)}, u32[]{:S(2)}, u32[]{:S(2)}) collective-permute-start(bf16[2,3,128]{2,1,0:T(4,128)(2,1)S(1)} %slice.595), channel_id=1, source_target_pairs={{0,8},{8,16},{16,24},{24,32},{32,40},{40,48},{48,56},{56,64},{64,7... | collective-permute-start | bytes 4616 | tf_op jit(solution)/shard_map/ppermute | solution.py:21
  15.9 14.2 %collective-permute-start.1 = (bf16[3,1024]{1,0:T(4,128)(2,1)S(1)}, bf16[3,1024]{1,0:T(4,128)(2,1)S(1)}, u32[]{:S(2)}, u32[]{:S(2)}) collective-permute-start(bf16[3,1024]{1,0:T(4,128)(2,1)S(1)} %slice.582), channel_id=1, source_target_pairs={{0,8},{8,16},{16,24},{24,32},{32,40},{40,48},{48,56},{56,64},{64,7... | collective-permute-start | bytes 18440 | tf_op jit(solution)/shard_map/ppermute | solution.py:21
  23.4 3.0 copy-start.11
  29.4 1.8 copy-start.9
  33.2 61.0 %all-gather.18.cloned.1.call-start = ((), (), s32[]{:S(2)}) async-start(), calls=%async_computation.4 | async-start | bytes 2621440 | tf_op jit(solution)/shard_map/all_gather | solution.py:35
  44.1 11.7 %copy-start.14 = (f32[16]{0:T(128)}, f32[16]{0:T(128)S(1)}, u32[]{:S(2)}) copy-start(f32[16]{0:T(128)S(1)} %get-tuple-element.79) | copy-start | bytes 196
  44.1 52.7 %copy-start.13 = (f32[16]{0:T(128)}, f32[16]{0:T(128)S(1)}, u32[]{:S(2)}) copy-start(f32[16]{0:T(128)S(1)} %get-tuple-element.76) | copy-start | bytes 196
  55.8 99.5 %copy-start.2 = (f32[32,64,128]{2,1,0:T(8,128)S(1)}, f32[32,64,128]{2,1,0:T(8,128)}, u32[]{:S(2)}) copy-start(f32[32,64,128]{2,1,0:T(8,128)} %all-gather.26.cloned.1.call-done) | copy-start | bytes 3145732
  58.0 97.3 %copy-start.1 = (f32[1,16,64,128]{3,2,1,0:T(8,128)S(1)}, f32[1,16,64,128]{3,2,1,0:T(8,128)}, u32[]{:S(2)}) copy-start(f32[1,16,64,128]{3,2,1,0:T(8,128)} %fusion.19) | copy-start | bytes 1572868
  58.0 97.2 %all-gather.20.cloned.1.call-start = ((), (), s32[]{:S(2)}) async-start(), calls=%async_computation.5 | async-start | bytes 4718592 | tf_op jit(solution)/shard_map/all_gather | solution.py:35
  58.7 38.1 %copy-start.15 = (f32[16]{0:T(128)}, f32[16]{0:T(128)S(1)}, u32[]{:S(2)}) copy-start(f32[16]{0:T(128)S(1)} %get-tuple-element.74) | copy-start | bytes 196
  117.2 42.6 %copy-start.5 = (f32[16,128]{1,0:T(8,128)S(1)}, f32[16,128]{1,0:T(8,128)}, u32[]{:S(2)}) copy-start(f32[16,128]{1,0:T(8,128)} %param.20) | copy-start | bytes 24580
  155.3 4.6 %copy-start.4 = (f32[128,128]{1,0:T(8,128)S(1)}, f32[128,128]{1,0:T(8,128)}, u32[]{:S(2)}) copy-start(f32[128,128]{1,0:T(8,128)} %fusion.166) | copy-start | bytes 196612
  155.3 4.6 %copy-start.7 = (pred[128,128]{1,0:T(8,128)(4,1)S(1)}, pred[128,128]{1,0:T(8,128)(4,1)}, u32[]{:S(2)}) copy-start(pred[128,128]{1,0:T(8,128)(4,1)} %fusion.92) | copy-start | bytes 49156
  155.3 6.1 %copy-start.10 = (f32[128]{0:T(128)S(1)}, f32[128]{0:T(128)}, u32[]{:S(2)}) copy-start(f32[128]{0:T(128)} %copy-done.9) | copy-start | bytes 1540
  159.8 3.3 copy-start.12
  161.2 38.5 %copy-start.3 = (bf16[1024,64]{0,1:T(8,128)(2,1)S(1)}, bf16[1024,64]{0,1:T(8,128)(2,1)}, u32[]{:S(2)}) copy-start(bf16[1024,64]{0,1:T(8,128)(2,1)} %param.27) | copy-start | bytes 393220
  164.0 78.9 %copy-start.6 = (bf16[128,512]{1,0:T(8,128)(2,1)S(1)}, bf16[128,512]{1,0:T(8,128)(2,1)}, u32[]{:S(2)}) copy-start(bf16[128,512]{1,0:T(8,128)(2,1)} %param.28) | copy-start | bytes 393220
  199.7 65.8 %copy-start.8 = (f32[4096]{0:T(1024)S(1)}, f32[4096]{0:T(1024)}, u32[]{:S(2)}) copy-start(f32[4096]{0:T(1024)} %param.29) | copy-start | bytes 49156
  200.2 110.3 %copy-start.17 = (s32[512]{0:T(512)S(1)}, s32[512]{0:T(512)}, u32[]{:S(2)}) copy-start(s32[512]{0:T(512)} %param.32) | copy-start | bytes 6148
  233.9 20.1 %all-to-all-start.2 = ((f32[64,1,512]{2,1,0:T(1,128)}), f32[64,1,512]{2,1,0:T(1,128)S(1)}, u32[]{:S(2)}, u32[]{:S(2)}) async-start(f32[64,1,512]{2,1,0:T(1,128)} %reshape.1464), calls=%async_computation.2 | async-start | bytes 262144 | tf_op jit(solution)/shard_map/all_to_all | solution.py:259
  242.8 67.7 %all-gather.22.cloned.1.call-start = ((), (), s32[]{:S(2)}) async-start(), calls=%async_computation.6 | async-start | bytes 2359296 | tf_op jit(solution)/shard_map/all_gather | solution.py:69
  275.7 62.2 %all-gather.24.cloned.1.call-start = ((), (), s32[]{:S(2)}) async-start(), calls=%async_computation.7 | async-start | bytes 6291456 | tf_op jit(solution)/shard_map/all_gather | solution.py:69
  340.3 60.7 %copy-start.16 = (f32[512]{0:T(512)S(1)}, f32[512]{0:T(512)}, u32[]{:S(2)}) copy-start(f32[512]{0:T(512)} %param.33) | copy-start | bytes 6148
Sparse Core Ops, SparseCore 0:
  33.3 22.3 all-gather.25
  58.2 35.9 all-gather.17
  96.9 58.3 all-gather.19
  275.8 34.6 all-gather.21
  312.4 25.3 all-gather.23
where the time goes:
time: 414 us; the launch traced here: 408 us
  blocking collectives  170 us (41%)
  waiting for transfers between devices  158 us (38%)
  other arithmetic  23.3 us (6%)
  starting transfers between devices  19 us (5%)
  between operations  15 us (4%)
  local copies, waits for them, and re-layouts  12.8 us (3%)
  matrix products  9.91 us (2%)
    all_gather x3, waiting for transfers between devices, entering_2(): pieces = jax.tree.map(lambda part: lax.all_gather(part, axis), subtotal)  85.3 us
    all_to_all x3, blocking collectives, from_everyone(): lax.all_to_all(jnp.broadcast_to(shard[None], (count, *shard.shape)), axis...  77.8 us
    all_gather x2, waiting for transfers between devices, gather_in_order(): blocks = lax.all_gather(blocks, axes[k], axis=0, tiled=True)  62.1 us
    all_gather x4, blocking collectives, gathered_once(): both, at, found = (lax.all_gather(jnp.concatenate(lines), axis), 0, {})  58.7 us
    all_gather x3, blocking collectives, entering_2(): pieces = jax.tree.map(lambda part: lax.all_gather(part, axis), subtotal)  23.7 us
    all_to_all x1, waiting for transfers between devices, body(): lax.all_to_all(summed_rows, CTX, split_axis=0, concat_axis=1, tiled=True)  10.5 us
    all_gather x1, blocking collectives, gather_in_order(): blocks = lax.all_gather(blocks, axes[k], axis=0, tiled=True)  10.1 us
    ppermute x3, starting transfers between devices, passed_along(): return lax.ppermute(shard, axis, pairs)  9.9 us
  transfers between devices with their start and end apart: 9, of which 6 were waited for; matrix products, arithmetic and copies ran while one was open for 5% of the time, Pallas kernels for 0%

commit v1 on v0

v1 whole, which is shorter than its diff:
```python
import functools

import jax
import jax.numpy as jnp
from jax import lax
from jax.experimental import pallas as pl
from jax.experimental.pallas import tpu as pltpu
from jax.sharding import Mesh
from jax.sharding import PartitionSpec as P

CTX = ("z", "x", "core")
SUB = ("x", "core")
PLANE = ("z", "tp")

epsilon = 1e-05
blocked = -1e9
precise = lax.Precision.HIGHEST
f32 = jnp.float32
bf16 = jnp.bfloat16


def exchange(blocks, axes):
    return lax.all_to_all(blocks, axes, 0, 0, tiled=True)


def to_everyone(shard, axes):
    return exchange(jnp.broadcast_to(shard[None], (lax.axis_size(axes), *shard.shape)), axes)


whole = pl.BlockSpec(memory_space=pltpu.VMEM)


def split(value, count):
    parts = []
    for _ in range(count):
        part = value.astype(bf16)
        parts.append(part)
        value = value - part.astype(f32)
    return parts


def exponent(value, axis):
    top = jnp.max(jnp.abs(value), axis=axis, keepdims=True)
    return jnp.floor(jnp.log2(jnp.maximum(top, 1e-30))) + 1.0


def coded(value, power):
    return jnp.clip(jnp.round(value * jnp.exp2(15.0 - power)), -32767.0, 32767.0)


def coded_log(value, free):
    high = jnp.round(value * 2048.0)
    low = jnp.round((value - high / 2048.0) * 2.0**26)
    return jnp.where(free, high, -32768.0), jnp.where(free, low, 0.0)


def decoded_log(high, low):
    return jnp.where(high < -32767.5, blocked, high / 2048.0 + low * 2.0**-26)


def local_kernel(
    place_ref, stream_ref, state_ref, tail_ref, gate_ref, step_ref, reset_ref, head_ref, taps_ref, state_taps_ref, out_ref, pad_ref
):
    rows, channels = stream_ref.shape
    states = state_ref.shape[2]
    heads = step_ref.shape[0]
    margin = tail_ref.shape[0]
    width = tail_ref.shape[1] - 128
    count = place_ref.shape[0]
    lane = lax.broadcasted_iota(jnp.int32, (8, 128), 1)
    line = lax.broadcasted_iota(jnp.int32, (8, 128), 0)

    flag = jnp.broadcast_to(reset_ref[...].astype(f32), (8, rows))
    free = 1.0 - flag
    earlier = 1.0 - tail_ref[:, width:].astype(f32)
    one, two = earlier[margin - 1 :], earlier[margin - 2 : margin - 1]
    second = free * jnp.where(lane == 0, one, pltpu.roll(free, 1, 1))
    third = second * jnp.where(lane == 0, two, jnp.where(lane == 1, one, pltpu.roll(free, 2, 1)))
    turned = jnp.where(line == 0, free, jnp.where(line == 1, second, third)).T
    keeping = [jnp.broadcast_to(turned[:, k : k + 1], (rows, 128)) for k in range(3)]

    def filtered(block, tail, taps):
        pad_ref[:margin] = tail.astype(f32)
        pad_ref[margin:] = block.astype(f32)
        summed = taps[0:1] * pad_ref[margin:]
        for k in range(1, 4):
            summed = summed + keeping[k - 1] * taps[k : k + 1] * pad_ref[margin - k : margin - k + rows]
        return (summed * jax.nn.sigmoid(summed)).astype(bf16)

    writes = filtered(state_ref[0], tail_ref[:, channels : channels + states], state_taps_ref[0])
    reads = filtered(state_ref[1], tail_ref[:, channels + states : width], state_taps_ref[1])

    chosen = lane == place_ref[...]
    pick = chosen.astype(bf16)
    rows_reads = jnp.dot(pick, reads, preferred_element_type=f32)
    first = lax.broadcasted_iota(jnp.int32, (rows, rows), 0)
    upto = (first <= lax.broadcasted_iota(jnp.int32, (rows, rows), 1)).astype(bf16)
    step = step_ref[...]
    drift = jnp.concatenate(split(-head_ref[:, 0:1] * step, 3), axis=0)
    summed = jnp.dot(drift, upto, preferred_element_type=f32)
    cumulated = summed[:heads] + summed[heads : 2 * heads] + summed[2 * heads :]
    segment = jnp.dot(flag.astype(bf16), upto, preferred_element_type=f32)
    rows_segment = jnp.sum(jnp.where(chosen, segment, 0.0), axis=1, keepdims=True)
    rows_log = jnp.sum(jnp.where(chosen[None], cumulated[:, None, :], 0.0), axis=2, keepdims=True)
    causal = (lane <= place_ref[...]) & (segment == rows_segment)
    scores = lax.dot_general(
        rows_reads.astype(bf16), writes, (((1,), (1,)), ((), ())), preferred_element_type=f32
    )
    gaps = jnp.where(causal[None], rows_log - cumulated[:, None, :], 0.0)
    mixing = jnp.where(causal[None], jnp.exp(gaps), 0.0) * scores[None] * step[:, None, :]
    mixing = mixing + jnp.where(chosen[None], head_ref[:, 1:2][:, :, None], 0.0)
    mixing = split(mixing.reshape(heads * count, rows), 3)

    end_segment = segment[0:1, rows - 1 :]
    end_log = cumulated[:, rows - 1 :]
    to_end = jnp.where(segment[0:1] == end_segment, jnp.exp(end_log - cumulated) * step, 0.0)
    end_high, end_low = coded_log(end_log, jnp.broadcast_to(end_segment == 0.0, end_log.shape))
    log_high, log_low = coded_log(rows_log, jnp.broadcast_to((rows_segment == 0.0)[None], rows_log.shape))

    power = exponent(rows_reads, 1)
    rows_reads = coded(rows_reads, power)
    folded = jnp.concatenate([pltpu.roll(rows_reads, 64, 1), rows_reads], axis=0)
    folded = jnp.broadcast_to(folded[None], (8, 16, 128)).reshape(128, 128)
    powers = jnp.broadcast_to(power, (8, 128))
    left = lane < 64
    wide = lax.broadcasted_iota(jnp.int32, (128, 128), 1)
    empty = jnp.zeros((80, 128), f32)
    for b in range(channels // 128):
        span = slice(b * 128, (b + 1) * 128)
        p, q = 2 * b, 2 * b + 1
        values = filtered(stream_ref[:, span], tail_ref[:, span], taps_ref[:, span])
        ends = jnp.concatenate(
            [jnp.broadcast_to(to_end[p : p + 1], (64, rows)), jnp.broadcast_to(to_end[q : q + 1], (64, rows))], axis=0
        )
        high, low = split(values.astype(f32).T * ends, 2)
        state = jnp.dot(high, writes, preferred_element_type=f32) + jnp.dot(low, writes, preferred_element_type=f32)
        both = jnp.concatenate([part[16 * b : 16 * b + 16] for part in mixing], axis=0)
        met = jnp.dot(both, values, preferred_element_type=f32)
        met = met[:16] + met[16:32] + met[32:]
        local = jnp.where(left, met[:8], met[8:])
        gate = jnp.dot(pick, gate_ref[:, span], preferred_element_type=f32)
        local_power, gate_power, state_power = exponent(local, 0), exponent(gate, 0), exponent(state, 1)
        others = jnp.where(line == 2, local_power, jnp.where(line == 3, gate_power, 0.0))
        others = jnp.where(line == 1, jnp.where(left, end_low[p : p + 1], end_low[q : q + 1]), others)
        others = jnp.where(line == 0, jnp.where(left, end_high[p : p + 1], end_high[q : q + 1]), others)
        side = jnp.concatenate(
            [
                coded(local, local_power),
                coded(gate, gate_power),
                jnp.where(left, log_high[p], log_high[q]),
                jnp.where(left, log_low[p], log_low[q]),
                others,
                powers,
                empty,
            ],
            axis=0,
        ).T
        side = jnp.where(wide == 36, state_power, jnp.where(wide < 64, side, folded))
        for at, part in ((0, coded(state, state_power)), (16, side)):
            part = part.astype(jnp.int32).reshape(8, 16, 128)
            out_ref[8 * b : 8 * b + 8, at : at + 16, :] = part.astype(jnp.int16)


def local_part(place, stream, states, tail, gate, step, resets, by_head, taps, state_taps):
    channels = stream.shape[1]
    return pl.pallas_call(
        local_kernel,
        out_shape=jax.ShapeDtypeStruct((channels // 16, 32, 128), jnp.int16),
        in_specs=[whole] * 10,
        out_specs=whole,
        scratch_shapes=[pltpu.VMEM((tail.shape[0] + stream.shape[0], 128), f32)],
        compiler_params=pltpu.CompilerParams(vmem_limit_bytes=16 * 2**20),
        cost_estimate=pl.CostEstimate(flops=1 << 27, bytes_accessed=2 << 20, transcendentals=1 << 18),
    )(place, stream, states, tail, gate, step, resets, by_head, taps, state_taps)


def project_kernel(gated_ref, gain_ref, weight_ref, out_ref):
    gated = gated_ref[...]
    lanes = gated.shape[1]
    half = lanes // 2
    depth = gated.shape[0]
    squares = jnp.broadcast_to(jnp.sum(gated * gated, axis=0, keepdims=True), (8, lanes))
    squares = squares + pltpu.roll(squares, half, 1)
    inverse = lax.rsqrt(squares[:1] / (2 * depth) + epsilon)
    normed = (gated * inverse * gain_ref[...]).T.astype(bf16)
    contract = (((1,), (1,)), ((), ()))
    out_ref[...] = lax.dot_general(
        normed[:half], weight_ref[:, :depth], contract, preferred_element_type=f32
    ) + lax.dot_general(normed[half:], weight_ref[:, depth:], contract, preferred_element_type=f32)


def project(gated, gain, weight):
    return pl.pallas_call(
        project_kernel,
        out_shape=jax.ShapeDtypeStruct((gated.shape[1] // 2, weight.shape[0]), f32),
        in_specs=[whole] * 3,
        out_specs=whole,
        compiler_params=pltpu.CompilerParams(vmem_limit_bytes=8 * 2**20),
        cost_estimate=pl.CostEstimate(flops=2 * 64 * 1024 * 512, bytes_accessed=1 << 21, transcendentals=0),
    )(gated, gain, weight)


def logits_kernel(start_ref, chosen_ref, gain_ref, target_ref, weight_ref, out_ref, total_ref, inverse_ref, *, steps, stride):
    step = pl.program_id(0)
    slabs, group, width = chosen_ref.shape
    subs, _, columns = weight_ref.shape

    @pl.when(step == 0)
    def _():
        squares = jnp.zeros((group, 1), f32)
        for k in range(slabs):
            slab = chosen_ref[k].astype(f32)
            squares = squares + jnp.sum(slab * slab, axis=1, keepdims=True)
        inverse_ref[...] = jnp.broadcast_to(lax.rsqrt(squares / (slabs * width) + epsilon), inverse_ref.shape)
        total_ref[...] = jnp.zeros_like(total_ref)

    features = chosen_ref[step].astype(f32) * inverse_ref[:, :1] * gain_ref[pl.ds(step, 1), :]
    weight = jnp.concatenate([weight_ref[k] for k in range(subs)], axis=1)
    total_ref[...] += jnp.dot(features.astype(bf16), weight, preferred_element_type=f32)

    @pl.when(step == steps - 1)
    def _():
        logits = total_ref[...]
        top = jnp.max(logits, axis=1, keepdims=True)
        summed = jnp.sum(jnp.exp(logits - top), axis=1, keepdims=True)
        picked = jnp.zeros((group, 1), f32)
        lane = lax.broadcasted_iota(jnp.int32, (group, columns), 1)
        for k in range(subs):
            own = lane + (start_ref[0] + k * stride) == target_ref[...]
            picked = picked + jnp.sum(
                jnp.where(own, logits[:, k * columns : (k + 1) * columns], 0.0), axis=1, keepdims=True
            )
        place = lax.broadcasted_iota(jnp.int32, (group, 128), 1)
        found = jnp.where(place == 0, top, jnp.where(place == 1, summed, picked)).T
        pair = jnp.concatenate([found[0:1], found[1:2], found[2:3], found[2:3]], axis=1)
        out_ref[...] = pair


def score(start, chosen, gain, target, weight, stride):
    slabs, group, width = chosen.shape
    subs, _, columns = weight.shape
    fixed = lambda *shape: pl.BlockSpec(shape, lambda k: (0,) * len(shape))
    return pl.pallas_call(
        functools.partial(logits_kernel, steps=slabs, stride=stride),
        grid=(slabs,),
        out_shape=jax.ShapeDtypeStruct((1, 4 * group), f32),
        in_specs=[
            pl.BlockSpec(memory_space=pltpu.SMEM),
            fixed(slabs, group, width),
            fixed(slabs, width),
            fixed(group, 1),
            pl.BlockSpec((subs, width, columns), lambda k: (0, k, 0)),
        ],
        out_specs=fixed(1, 4 * group),
        scratch_shapes=[pltpu.VMEM((group, subs * columns), f32), pltpu.VMEM((group, 128), f32)],
        compiler_params=pltpu.CompilerParams(
            dimension_semantics=("arbitrary",), vmem_limit_bytes=24 * 2**20
        ),
        cost_estimate=pl.CostEstimate(flops=2 * 64 * 4096 * 1024, bytes_accessed=9 << 20, transcendentals=0),
    )(start, chosen, gain, target, weight)


def body(
    inner_input,
    gate_input,
    state_inputs,
    step_size,
    resets,
    decay_rate,
    skip_gain,
    conv_inner,
    conv_state,
    norm_gain,
    out_weight,
    residual,
    final_gain,
    head_weight,
    scored,
    targets,
    policy_logprob,
):
    rows, channels = inner_input.shape
    chunks = lax.axis_size(CTX)
    part = channels // chunks
    planes, subs = lax.axis_size("z"), lax.axis_size(SUB)
    count = scored.shape[0]
    group = planes * count
    total = chunks * count
    local_rows = scored - lax.axis_index(CTX) * rows

    margin = 16
    flags = jnp.broadcast_to(resets[rows - margin :, None].astype(bf16), (margin, 128))
    tail = [inner_input[rows - margin :], state_inputs[0, rows - margin :], state_inputs[1, rows - margin :], flags]
    tail = lax.ppermute(jnp.concatenate(tail, axis=1), CTX, [(i, i + 1) for i in range(chunks - 1)])

    half = part // 2
    by_half = lambda a: jnp.swapaxes(a.reshape(chunks, 2, half, -1), 0, 1).reshape(channels, -1)
    out_full = lax.all_gather(by_half(out_weight).T, SUB, axis=0, tiled=True)
    gain = by_half(norm_gain)
    gain = jnp.repeat(gain.reshape(2, channels // 2), group, axis=0).T
    head_full = lax.all_gather(head_weight, SUB, axis=0)
    pick = (jnp.arange(rows)[None, :] == local_rows[:, None]).astype(bf16)
    rows_residual = jnp.dot(pick, residual, preferred_element_type=f32).astype(bf16)
    swap = [(i * planes + k, k * planes + i) for i in range(planes) for k in range(planes)]
    rows_residual = lax.ppermute(rows_residual, PLANE, swap)
    own = lax.dynamic_index_in_dim(targets.reshape(planes, subs, count), lax.axis_index(SUB), 1, False).reshape(group, 1)

    by_head = jnp.stack([decay_rate, skip_gain], axis=1)
    message = local_part(
        local_rows.reshape(-1, 1), inner_input, state_inputs, tail, gate_input, step_size, resets.reshape(1, rows), by_head, conv_inner, conv_state
    )
    message, rows_residual = lax.optimization_barrier((message, rows_residual))
    came = exchange(message, CTX)

    side = came[:, part:].astype(f32)
    states = (came[:, :part].astype(f32) * jnp.exp2(side[:, :, 36:37] - 15.0)).reshape(channels, -1)
    one = side[:, 0]
    reads = jnp.concatenate([side[:, :count, 64:], side[:, count:, 64:]], axis=2)
    reads = reads * jnp.exp2(one[:, 40:48] - 15.0)[:, :, None]

    def by_group(a):
        return jnp.swapaxes(a.reshape(planes, subs, *a.shape[1:]), 0, 1)

    reads = by_group(reads).reshape(total, -1)
    met = lax.dot_general(states, reads, (((1,), (1,)), ((), ())), precision=lax.Precision.HIGH).reshape(chunks, part, total)
    end_log = decoded_log(one[:, 32], one[:, 33])
    rows_log = by_group(decoded_log(one[:, 16:24], one[:, 24:32])).reshape(1, total)
    lane = jnp.arange(total)
    chunk_of = (lane // count) % planes * subs + lane // group
    index = jnp.arange(chunks)
    before = index[:, None] < chunk_of[None, :]
    between = jnp.dot(
        (index[None, :] > index[:, None]).astype(f32), jnp.where(before, end_log[:, None], 0.0), precision=precise
    )
    weights = jnp.where(before, jnp.exp(between + rows_log), 0.0)
    across = jnp.sum(weights[:, None, :] * met, axis=0)
    local = side[:, :, :8] * jnp.exp2(side[:, :, 34:35] - 15.0)
    gate = side[:, :, 8:16] * jnp.exp2(side[:, :, 35:36] - 15.0)
    pair = jnp.stack([local, gate], axis=0).reshape(2, planes, subs, part, count)
    local, gate = pair.transpose(0, 3, 2, 1, 4).reshape(2, part, total)
    gated = (across + local) * jax.nn.silu(gate)
    gated = gated.reshape(2, half, subs, group).transpose(2, 1, 0, 3).reshape(subs, half, 2 * group)
    gated = jnp.broadcast_to(gated[None], (planes, subs, half, 2 * group)).reshape(chunks, half, 2 * group)

    gated = exchange(gated, CTX).reshape(channels // 2, 2 * group)

    partial = exchange(project(gated, gain, out_full).reshape(planes, count, -1), "tp")
    chosen = (jnp.sum(partial, axis=0) + rows_residual.astype(f32)).astype(bf16)

    chosen = to_everyone(chosen, PLANE).reshape(planes, group, -1)
    columns = head_weight.shape[1]
    ways = lax.axis_size("tp")
    start = (lax.axis_index("z") * subs * ways + lax.axis_index("tp")) * columns
    found = score(start.reshape(1), chosen, final_gain.reshape(planes, -1), own, head_full, ways * columns)

    found = to_everyone(found, PLANE).reshape(chunks, 4, group)
    top = jnp.max(found[:, 0], axis=0)
    summed = jnp.sum(found[:, 1] * jnp.exp(found[:, 0] - top[None, :]), axis=0)
    ref = jnp.sum(found[:, 2], axis=0) - top - jnp.log(summed)
    ref = to_everyone(ref.reshape(planes, count), SUB)
    ref_logprob = ref.swapaxes(0, 1).reshape(total)
    token_kl = 0.5 * jnp.square(ref_logprob - policy_logprob)
    return (ref_logprob, token_kl)


def solution(mesh):
    heads_split = mesh.shape["tp"]
    finer = Mesh(mesh.devices.reshape(heads_split, -1, 2, heads_split), ("z", "x", "core", "tp"))
    placed = (
        P(CTX, "tp"),
        P(CTX, "tp"),
        P(None, CTX, "tp"),
        P("tp", CTX),
        P(CTX),
        P("tp"),
        P("tp"),
        P(None, "tp"),
        P(None, None, "tp"),
        P("tp"),
        P("tp", CTX),
        P(CTX, "tp"),
        P(),
        P(None, (*CTX, "tp")),
        P(CTX),
        P(),
        P(),
    )
    return jax.shard_map(body, mesh=finer, in_specs=placed, out_specs=(P(), P()), check_vma=False)
```

time: 414 us -> 166 us (0.40); the launches traced: 408 us -> 165 us
  blocking collectives: 170 us -> 41.6 us
  waiting for transfers between devices: 158 us -> 50 us
  other arithmetic: 23.3 us -> 2.55 us
  starting transfers between devices: 19 us -> 35.6 us
  matrix products: 9.91 us -> 1.58 us
  Pallas kernels: 0 us -> 6.87 us
    all_gather x5 -> x2, waiting for transfers between devices: 147 us -> 0.01 us  [the longest x1 0.01 us: body(): out_full = lax.all_gather(by_half(out_weight).T, SUB, axis=0, tiled=True)]
    all_gather x8 -> x0, blocking collectives: 92.5 us -> none  [the longest x4 58.7 us: gathered_once(): both, at, found = (lax.all_gather(jnp.concatenate(lines), axis), 0, {})]
    all_to_all x3, blocking collectives: 77.8 us -> 41.6 us  [exchange(): return lax.all_to_all(blocks, axes, 0, 0, tiled=True)]
    all_to_all x1 -> x3, waiting for transfers between devices: 10.5 us -> 46 us  [exchange(): return lax.all_to_all(blocks, axes, 0, 0, tiled=True)]
    all_to_all x1 -> x3, starting transfers between devices: 8.94 us -> 30.3 us  [exchange(): return lax.all_to_all(blocks, axes, 0, 0, tiled=True)]
    dot_general x6 -> x3, matrix products: 9.91 us -> 1.58 us  [the longest x1 1.09 us: body(): lax.dot_general(states, reads, (((1,), (1,)), ((), ())), precision=lax.Pr...]
    pallas_call x0 -> x3, Pallas kernels: none -> 6.87 us  [the longest x1 3.93 us: score(): pl.pallas_call(functools.partial(logits_kernel, steps=slabs, stride=strid...]
    unnamed x38 -> x37, local copies, waits for them, and re-layouts: 1.03 us -> 6.07 us
  transfers between devices with their start and end apart: 9 -> 7, of which waited for: 6 -> 4; matrix products, arithmetic and copies ran while one was open for 5% -> 5% of each run, Pallas kernels for 0% -> 2%
where the time goes in v1:
time: 166 us; the launch traced here: 165 us
  waiting for transfers between devices  50 us (30%)
  blocking collectives  41.6 us (25%)
  starting transfers between devices  35.6 us (21%)
  between operations  14.6 us (9%)
  local copies, waits for them, and re-layouts  12.7 us (8%)
  Pallas kernels  6.87 us (4%)
  other arithmetic  2.55 us (2%)
    all_to_all x3, waiting for transfers between devices, exchange(): return lax.all_to_all(blocks, axes, 0, 0, tiled=True)  46 us
    all_to_all x3, blocking collectives, exchange(): return lax.all_to_all(blocks, axes, 0, 0, tiled=True)  41.6 us
    all_to_all x3, starting transfers between devices, exchange(): return lax.all_to_all(blocks, axes, 0, 0, tiled=True)  30.3 us
    unnamed x37, local copies, waits for them, and re-layouts  6.07 us
    ppermute x1, starting transfers between devices, body(): lax.ppermute(jnp.concatenate(tail, axis=1), CTX, [(i, i + 1) for i in ran...  4.51 us
    pallas_call x1, Pallas kernels, score(): pl.pallas_call(functools.partial(logits_kernel, steps=slabs, stride=strid...  3.93 us
  transfers between devices with their start and end apart: 7, of which 4 were waited for; matrix products, arithmetic and copies ran while one was open for 5% of the time, Pallas kernels for 2%

profile of v1, /device:TPU:1, one launch (start us, length us, event | category | flops | bytes accessed | tf_op | source)
XLA Modules:
  0.0 165.5 jit_solution(5936955515993278471)
XLA Ops:
  7.3 1.3 copy.169
  8.6 0.8 copy.171
  9.5 0.7 all-gather.6.cloned.1.call-update
  10.4 4.5 %collective-permute-start = (bf16[16,1408]{1,0:T(8,128)(2,1)S(1)}, bf16[16,1408]{1,0:T(8,128)(2,1)S(1)}, u32[]{:S(2)}, u32[]{:S(2)}) collective-permute-start(bf16[16,1408]{1,0:T(8,128)(2,1)S(1)} %pad_maximum_fusion), channel_id=1, source_target_pairs={{0,8},{8,16},{16,24},{24,32},{32,40},{40,48},{48,56},{56,64},{64,7... | collective-permute-start | bytes 135176 | tf_op jit(solution)/shard_map/ppermute | solution.py:294
  15.0 0.2 convolution_convert_fusion
  15.1 0.7 collective-permute-start.1
  16.0 3.3 %collective-permute-done.tail_ref = bf16[16,1408]{1,0:T(8,128)(2,1)S(1)} collective-permute-done((bf16[16,1408]{1,0:T(8,128)(2,1)S(1)}, bf16[16,1408]{1,0:T(8,128)(2,1)S(1)}, u32[]{:S(2)}, u32[]{:S(2)}) %collective-permute-start) | collective-permute-done | bytes 45088 | tf_op jit(solution)/shard_map/ppermute | solution.py:294
  19.3 2.3 %shard_map.176 = s16[64,32,128]{2,1,0:T(8,128)(2,1)} custom-call(s32[8,1]{1,0:T(8,128)S(1)} %copy.151.place_ref, bf16[128,1024]{1,0:T(8,128)(2,1)S(1)} %copy-done.3, bf16[2,128,128]{2,1,0:T(8,128)(2,1)S(1)} %copy-done.5, bf16[16,1408]{1,0:T(8,128)(2,1)S(1)} %collective-permute-done.tail_ref, bf16[128,1024]{1,0:T(8,128)(2,1)S(1)} %copy-done.4, ...), custom_call_target="tpu_custom_call" | custom-call | flops 134217728 | bytes 2097152 | tf_op jit(solution)/shard_map/pallas_call | solution.py:166
  21.6 20.0 %all-to-all-start = ((s16[64,32,128]{2,1,0:T(8,128)(2,1)}), s16[64,32,128]{2,1,0:T(8,128)(2,1)S(1)}, u32[]{:S(2)}, u32[]{:S(2)}) async-start(s16[64,32,128]{2,1,0:T(8,128)(2,1)} %shard_map.176), calls=%async_computation | async-start | bytes 1048576 | tf_op jit(solution)/shard_map/all_to_all | solution.py:23
  41.6 17.7 %all-to-all-done = s16[64,32,128]{2,1,0:T(8,128)(2,1)S(1)} async-done(((s16[64,32,128]{2,1,0:T(8,128)(2,1)}), s16[64,32,128]{2,1,0:T(8,128)(2,1)S(1)}, u32[]{:S(2)}, u32[]{:S(2)}) %all-to-all-start) | async-done | bytes 524320 | tf_op jit(solution)/shard_map/all_to_all | solution.py:23
  59.4 0.1 fusion.22
  59.5 0.2 fusion.37
  59.7 0.2 fusion.11
  60.0 0.1 add.85
  60.1 0.5 fusion.7
  60.6 0.4 copy.176
  61.0 0.2 fusion.25
  61.2 0.3 fusion.1
  61.5 1.1 multiply_reduce_fusion
  62.7 0.4 copy.177
  63.1 0.4 copy.178
  63.6 0.5 slice_multiply_fusion.1
  64.1 0.3 copy.164
  64.4 0.3 copy.165
  64.7 0.1 maximum_bitcast_fusion
  64.9 0.2 unstack.13
  65.1 0.2 unstack.15
  65.4 0.1 broadcast_in_dim.75
  65.5 0.7 broadcast_in_dim.76
  66.2 5.7 %all-to-all-start.1 = ((f32[64,8,128]{2,1,0:T(8,128)}), f32[64,8,128]{2,1,0:T(8,128)S(1)}, u32[]{:S(2)}, u32[]{:S(2)}) async-start(f32[64,8,128]{2,1,0:T(8,128)} %bitcast.26), calls=%async_computation.1 | async-start | bytes 524288 | tf_op jit(solution)/shard_map/all_to_all | solution.py:23
  72.0 0.1 reshape.154
  72.1 0.1 reshape_reshape.3
  72.3 0.1 copy.168
  72.4 12.7 %all-to-all-done.1 = f32[64,8,128]{2,1,0:T(8,128)S(1)} async-done(((f32[64,8,128]{2,1,0:T(8,128)}), f32[64,8,128]{2,1,0:T(8,128)S(1)}, u32[]{:S(2)}, u32[]{:S(2)}) %all-to-all-start.1) | async-done | bytes 262176 | tf_op jit(solution)/shard_map/all_to_all | solution.py:23
  85.1 1.3 copy-done.2
  86.4 0.6 shard_map.177
  87.1 12.5 %all_to_all.30 = f32[8,8,512]{2,1,0:T(8,128)S(1)} all-to-all(f32[8,8,512]{2,1,0:T(8,128)S(1)} %bitcast.71), channel_id=1, replica_groups=mesh['z'=8,'x'=4,'core'=2,'tp'=8] {'tp'}, dimensions={0} | all-to-all | bytes 262144 | tf_op jit(solution)/shard_map/all_to_all | solution.py:23
  99.6 0.9 broadcast_in_dim.78
  100.5 4.6 %all-to-all-start.3 = ((bf16[64,8,512]{2,1,0:T(8,128)(2,1)}), bf16[64,8,512]{2,1,0:T(8,128)(2,1)S(1)}, u32[]{:S(2)}, u32[]{:S(2)}) async-start(bf16[64,8,512]{2,1,0:T(8,128)(2,1)} %broadcast_in_dim.78), calls=%async_computation.3 | async-start | bytes 1048576 | tf_op jit(solution)/shard_map/all_to_all | solution.py:23
  105.4 15.6 %all-to-all-done.3 = bf16[64,8,512]{2,1,0:T(8,128)(2,1)S(1)} async-done(((bf16[64,8,512]{2,1,0:T(8,128)(2,1)}), bf16[64,8,512]{2,1,0:T(8,128)(2,1)S(1)}, u32[]{:S(2)}, u32[]{:S(2)}) %all-to-all-start.3) | async-done | bytes 524320 | tf_op jit(solution)/shard_map/all_to_all | solution.py:23
  121.0 3.4 %copy-done.1 = bf16[32768,128]{1,0:T(8,128)(2,1)S(1)} copy-done((bf16[32768,128]{1,0:T(8,128)(2,1)S(1)}, bf16[32768,128]{1,0:T(8,128)(2,1)}, u32[]{:S(2)}) %copy-start.1) | copy-done | bytes 8388632
  124.4 3.9 %shard_map.178 = f32[1,256]{1,0:T(1,128)S(1)} custom-call(s32[1]{0:T(128)} %bitcast.start_ref, bf16[8,64,512]{2,1,0:T(8,128)(2,1)S(1)} %bitcast.68, f32[8,512]{1,0:T(8,128)S(1)} %reshape.160.gain_ref, s32[64,1]{1,0:T(8,128)S(1)} %reshape.167.target_ref, bf16[8,4096,128]{2,1,0:T(8,128)(2,1)S(1)} %bitcast.67), custom_call_target="tpu_custom_call" | custom-call | flops 536870912 | bytes 9437184 | tf_op jit(solution)/shard_map/pallas_call | solution.py:243
  128.3 18.4 %all_to_all.31 = f32[64,1,256]{2,1,0:T(1,128)S(1)} all-to-all(f32[64,1,256]{2,1,0:T(1,128)S(1)} %broadcast_in_dim.80), channel_id=1, replica_groups=mesh['z'=8,'x'=4,'core'=2,'tp'=8] {'z','tp'}, dimensions={0} | all-to-all | bytes 131072 | tf_op jit(solution)/shard_map/all_to_all | solution.py:23
  146.8 0.2 reduce.4
  146.9 0.1 reshape.163
  147.3 10.6 %all_to_all.32 = f32[8,8,8]{2,1,0:T(8,128)S(1)} all-to-all(f32[8,8,8]{2,1,0:T(8,128)S(1)} %broadcast_in_dim.81), channel_id=1, replica_groups=mesh['z'=8,'x'=4,'core'=2,'tp'=8] {'x','core'}, dimensions={0} | all-to-all | bytes 4096 | tf_op jit(solution)/shard_map/all_to_all | solution.py:23
  157.9 0.1 reshape.164
  158.0 0.6 multiply_multiply_fusion
  (79 shorter events, 1.4 us)
Async XLA Ops:
  7.2 7.8 %copy-start = (bf16[128,512]{1,0:T(8,128)(2,1)S(1)}, bf16[128,512]{1,0:T(8,128)(2,1)}, u32[]{:S(2)}) copy-start(bf16[128,512]{1,0:T(8,128)(2,1)} %param.28) | copy-start | bytes 393220
  7.2 3.2 %slice-start = ((bf16[128,1024]{1,0:T(8,128)(2,1)}), bf16[16,1024]{1,0:T(8,128)(2,1)S(1)}, s32[]{:S(2)}) async-start(bf16[128,1024]{1,0:T(8,128)(2,1)} %stream_ref.1), calls=%async_computation.8 | async-start | bytes 65536 | tf_op jit(solution)/shard_map/slice | solution.py:293
  7.2 12.1 %copy-start.3 = (bf16[128,1024]{1,0:T(8,128)(2,1)S(1)}, bf16[128,1024]{1,0:T(8,128)(2,1)}, u32[]{:S(2)}) copy-start(bf16[128,1024]{1,0:T(8,128)(2,1)} %stream_ref.1) | copy-start | bytes 786436
  7.2 3.0 %copy-start.9 = (s32[128]{0:T(128)S(1)}, s32[128]{0:T(128)}, u32[]{:S(2)}) copy-start(s32[128]{0:T(128)} %param.21) | copy-start | bytes 1540
  7.2 3.1 %copy-start.5 = (bf16[2,128,128]{2,1,0:T(8,128)(2,1)S(1)}, bf16[2,128,128]{2,1,0:T(8,128)(2,1)}, u32[]{:S(2)}) copy-start(bf16[2,128,128]{2,1,0:T(8,128)(2,1)} %state_ref.1) | copy-start | bytes 196612
  7.2 7.7 %copy-start.17 = (s32[8]{0:T(128)S(1)}, s32[8]{0:T(128)}, u32[]{:S(2)}) copy-start(s32[8]{0:T(128)} %param.31) | copy-start | bytes 100
  7.2 8.6 %copy-start.16 = (f32[16]{0:T(128)S(1)}, f32[16]{0:T(128)}, u32[]{:S(2)}) copy-start(f32[16]{0:T(128)} %param.22) | copy-start | bytes 196
  7.2 8.6 %copy-start.15 = (f32[16]{0:T(128)S(1)}, f32[16]{0:T(128)}, u32[]{:S(2)}) copy-start(f32[16]{0:T(128)} %param.23) | copy-start | bytes 196
  7.3 12.0 %copy-start.4 = (bf16[128,1024]{1,0:T(8,128)(2,1)S(1)}, bf16[128,1024]{1,0:T(8,128)(2,1)}, u32[]{:S(2)}) copy-start(bf16[128,1024]{1,0:T(8,128)(2,1)} %gate_ref.1) | copy-start | bytes 786436
  7.3 12.0 %copy-start.7 = (f32[16,128]{1,0:T(8,128)S(1)}, f32[16,128]{1,0:T(8,128)}, u32[]{:S(2)}) copy-start(f32[16,128]{1,0:T(8,128)} %step_ref.1) | copy-start | bytes 24580
  7.3 12.0 %copy-start.6 = (f32[4,1024]{1,0:T(4,128)S(1)}, f32[4,1024]{1,0:T(4,128)}, u32[]{:S(2)}) copy-start(f32[4,1024]{1,0:T(4,128)} %taps_ref.1) | copy-start | bytes 49156
  7.3 12.0 %copy-start.8 = (f32[2,4,128]{2,1,0:T(4,128)S(1)}, f32[2,4,128]{2,1,0:T(4,128)}, u32[]{:S(2)}) copy-start(f32[2,4,128]{2,1,0:T(4,128)} %state_taps_ref.1) | copy-start | bytes 12292
  7.3 77.8 %all-gather.4.cloned.1.call-start = ((), (), s32[]{:S(2)}) async-start(), calls=%async_computation.6 | async-start | bytes 1179648 | tf_op jit(solution)/shard_map/all_gather | solution.py:298
  9.5 111.5 %all-gather.6.cloned.1.call-start = ((), (), s32[]{:S(2)}) async-start(), calls=%async_computation.7 | async-start | bytes 9437184 | tf_op jit(solution)/shard_map/all_gather | solution.py:301
  10.4 8.9 %collective-permute-start = (bf16[16,1408]{1,0:T(8,128)(2,1)S(1)}, bf16[16,1408]{1,0:T(8,128)(2,1)S(1)}, u32[]{:S(2)}, u32[]{:S(2)}) collective-permute-start(bf16[16,1408]{1,0:T(8,128)(2,1)S(1)} %pad_maximum_fusion), channel_id=1, source_target_pairs={{0,8},{8,16},{16,24},{24,32},{32,40},{40,48},{48,56},{56,64},{64,7... | collective-permute-start | bytes 135176 | tf_op jit(solution)/shard_map/ppermute | solution.py:294
  15.1 6.5 %collective-permute-start.1 = (bf16[8,512]{1,0:T(8,128)(2,1)S(1)}, bf16[8,512]{1,0:T(8,128)(2,1)S(1)}, u32[]{:S(2)}, u32[]{:S(2)}) collective-permute-start(bf16[8,512]{1,0:T(8,128)(2,1)S(1)} %convolution_convert_fusion), channel_id=1, source_target_pairs={{0,0},{1,64},{2,128},{3,192},{4,256},{5,320},{6,384},{7,448},{64,1... | collective-permute-start | bytes 24584 | tf_op jit(solution)/shard_map/ppermute | solution.py:305
  21.6 37.7 %all-to-all-start = ((s16[64,32,128]{2,1,0:T(8,128)(2,1)}), s16[64,32,128]{2,1,0:T(8,128)(2,1)S(1)}, u32[]{:S(2)}, u32[]{:S(2)}) async-start(s16[64,32,128]{2,1,0:T(8,128)(2,1)} %shard_map.176), calls=%async_computation | async-start | bytes 1048576 | tf_op jit(solution)/shard_map/all_to_all | solution.py:23
  64.8 7.1 %copy-start.12 = (f32[1024]{0:T(1024)S(1)}, f32[1024]{0:T(1024)}, u32[]{:S(2)}) copy-start(f32[1024]{0:T(1024)} %param.26) | copy-start | bytes 12292
  66.2 18.9 %all-to-all-start.1 = ((f32[64,8,128]{2,1,0:T(8,128)}), f32[64,8,128]{2,1,0:T(8,128)S(1)}, u32[]{:S(2)}, u32[]{:S(2)}) async-start(f32[64,8,128]{2,1,0:T(8,128)} %bitcast.26), calls=%async_computation.1 | async-start | bytes 524288 | tf_op jit(solution)/shard_map/all_to_all | solution.py:23
  72.2 32.9 %copy-start.13 = (s32[512]{0:T(512)S(1)}, s32[512]{0:T(512)}, u32[]{:S(2)}) copy-start(s32[512]{0:T(512)} %param.32) | copy-start | bytes 6148
  72.3 33.1 %copy-start.10 = (f32[4096]{0:T(1024)S(1)}, f32[4096]{0:T(1024)}, u32[]{:S(2)}) copy-start(f32[4096]{0:T(1024)} %param.29) | copy-start | bytes 49156
  85.1 1.3 copy-start.2
  100.5 20.5 %all-to-all-start.3 = ((bf16[64,8,512]{2,1,0:T(8,128)(2,1)}), bf16[64,8,512]{2,1,0:T(8,128)(2,1)S(1)}, u32[]{:S(2)}, u32[]{:S(2)}) async-start(bf16[64,8,512]{2,1,0:T(8,128)(2,1)} %broadcast_in_dim.78), calls=%async_computation.3 | async-start | bytes 1048576 | tf_op jit(solution)/shard_map/all_to_all | solution.py:23
  121.0 3.4 %copy-start.1 = (bf16[32768,128]{1,0:T(8,128)(2,1)S(1)}, bf16[32768,128]{1,0:T(8,128)(2,1)}, u32[]{:S(2)}) copy-start(bf16[32768,128]{1,0:T(8,128)(2,1)} %all-gather.6.cloned.1.call-done) | copy-start | bytes 25165828
  124.4 33.7 %copy-start.14 = (f32[512]{0:T(512)S(1)}, f32[512]{0:T(512)}, u32[]{:S(2)}) copy-start(f32[512]{0:T(512)} %param.33) | copy-start | bytes 6148
  158.0 0.6 copy-start.11
Sparse Core Ops, SparseCore 0:
  10.3 34.7 all-gather.3
  47.2 59.4 all-gather.5

commit v2 on v1

--- a/solution.py
+++ b/solution.py
@@ -169,24 +169,117 @@
         in_specs=[whole] * 10,
         out_specs=whole,
         scratch_shapes=[pltpu.VMEM((tail.shape[0] + stream.shape[0], 128), f32)],
-        compiler_params=pltpu.CompilerParams(vmem_limit_bytes=16 * 2**20),
+        compiler_params=pltpu.CompilerParams(vmem_limit_bytes=58 * 2**20),
         cost_estimate=pl.CostEstimate(flops=1 << 27, bytes_accessed=2 << 20, transcendentals=1 << 18),
     )(place, stream, states, tail, gate, step, resets, by_head, taps, state_taps)
 
 
+def carry_kernel(came_ref, out_ref, side_ref, met_ref, weight_ref, *, planes, subs):
+    chunks, _, states = came_ref.shape
+    part = 16
+    count = 8
+    group = planes * count
+    total = chunks * count
+    side = came_ref[:, part:, :].astype(jnp.int32).astype(f32)
+    side_ref[...] = side.reshape(chunks * part, 128)
+    scale = jnp.exp2(side - 15.0)
+    state = came_ref[:, :part, :].astype(jnp.int32).astype(f32) * scale[:, :, 36:37]
+    state_high, state_low = split(state.reshape(chunks * part, states), 2)
+    wide = lax.broadcasted_iota(jnp.int32, (chunks, 8, 128), 2)
+    reads = jnp.where(wide < 64, pltpu.roll(side[:, :8], 64, 2), side[:, 8:])
+    order = [z * subs + k for k in range(subs) for z in range(planes)]
+    reads = jnp.concatenate([reads[c] for c in order], axis=0)
+    reads_high, reads_low = split(reads, 2)
+    contract = (((1,), (1,)), ((), ()))
+    met_ref[...] = (
+        lax.dot_general(state_high, reads_high, contract, preferred_element_type=f32)
+        + lax.dot_general(state_high, reads_low, contract, preferred_element_type=f32)
+        + lax.dot_general(state_low, reads_high, contract, preferred_element_type=f32)
+    )
+
+    lane = lax.broadcasted_iota(jnp.int32, (8, 128), 1)
+
+    def by_lane(block_of, offset):
+        columns = []
+        for j in range(chunks // 16):
+            column = None
+            for i in range(16):
+                block = block_of(order[16 * j + i])
+                tall = block.shape[0]
+                if (8 * i - offset) % 128:
+                    block = pltpu.roll(block, (8 * i - offset) % 128, 1)
+                place = lax.broadcasted_iota(jnp.int32, (tall, 128), 1)
+                column = block if column is None else jnp.where(place >= 8 * i, block, column)
+            columns.append(column)
+        return jnp.concatenate(columns, axis=1)
+
+    local = side * scale[:, :, 34:35]
+    gate = side * scale[:, :, 35:36]
+    local = by_lane(lambda c: local[c], 0)
+    gate = by_lane(lambda c: gate[c], 8)
+    log_high = by_lane(lambda c: side[c, :8], 16)[:1]
+    log_low = by_lane(lambda c: side[c, :8], 24)[:1]
+    power = by_lane(lambda c: side[c, :8], 40)[:1]
+    rows_log = decoded_log(log_high, log_low)
+
+    one = side_ref[pl.ds(0, chunks, stride=part), :]
+    end_log = decoded_log(one[:, 32:33], one[:, 33:34])
+    chunk = lax.broadcasted_iota(jnp.int32, (chunks, total), 0)
+    at = lax.broadcasted_iota(jnp.int32, (chunks, total), 1)
+    before = chunk < ((at // count) % planes) * subs + at // group
+    upper = lax.broadcasted_iota(jnp.int32, (chunks, chunks), 0) < lax.broadcasted_iota(jnp.int32, (chunks, chunks), 1)
+    upper = upper.astype(bf16)
+    between = jnp.zeros((chunks, total), f32)
+    for piece in split(jnp.where(before, end_log, 0.0), 3):
+        between = between + jnp.dot(upper, piece, preferred_element_type=f32)
+    weight_ref[...] = jnp.where(before, jnp.exp(between + rows_log), 0.0) * jnp.exp2(power - 15.0)
+
+    across = jnp.zeros((part, total), f32)
+    for c in range(chunks):
+        across = across + weight_ref[c : c + 1, :] * met_ref[part * c : part * c + part, :]
+    gated = (across + local) * (gate * jax.nn.sigmoid(gate))
+    for k in range(subs):
+        columns = slice(k // 2 * 128, k // 2 * 128 + 128)
+        first, second = gated[:8, columns], gated[8:, columns]
+        if k % 2:
+            first = pltpu.roll(first, 64, 1)
+        else:
+            second = pltpu.roll(second, 64, 1)
+        tile = jnp.where(lane < 64, first, second)
+        for z in range(planes):
+            out_ref[z * subs + k] = tile
+
+
+def carry(came, planes, subs):
+    chunks = came.shape[0]
+    return pl.pallas_call(
+        functools.partial(carry_kernel, planes=planes, subs=subs),
+        out_shape=jax.ShapeDtypeStruct((chunks, 8, 128), f32),
+        in_specs=[whole],
+        out_specs=whole,
+        scratch_shapes=[
+            pltpu.VMEM((chunks * 16, 128), f32),
+            pltpu.VMEM((chunks * 16, chunks * 8), f32),
+            pltpu.VMEM((chunks, chunks * 8), f32),
+        ],
+        compiler_params=pltpu.CompilerParams(vmem_limit_bytes=24 * 2**20),
+        cost_estimate=pl.CostEstimate(flops=1 << 28, bytes_accessed=1 << 20, transcendentals=1 << 16),
+    )(came)
+
+
 def project_kernel(gated_ref, gain_ref, weight_ref, out_ref):
     gated = gated_ref[...]
-    lanes = gated.shape[1]
+    depth, lanes = gated.shape
     half = lanes // 2
-    depth = gated.shape[0]
     squares = jnp.broadcast_to(jnp.sum(gated * gated, axis=0, keepdims=True), (8, lanes))
     squares = squares + pltpu.roll(squares, half, 1)
-    inverse = lax.rsqrt(squares[:1] / (2 * depth) + epsilon)
-    normed = (gated * inverse * gain_ref[...]).T.astype(bf16)
-    contract = (((1,), (1,)), ((), ()))
+    normed = gated * lax.rsqrt(squares[:1] / (2 * depth) + epsilon)
+    pair = [a.reshape(depth // 8, 1, 8, lanes) for a in (normed, pltpu.roll(normed, half, 1))]
+    normed = jnp.concatenate(pair, axis=1).reshape(2 * depth, lanes).T[:half]
+    normed = (normed * gain_ref[...]).astype(bf16)
     out_ref[...] = lax.dot_general(
-        normed[:half], weight_ref[:, :depth], contract, preferred_element_type=f32
-    ) + lax.dot_general(normed[half:], weight_ref[:, depth:], contract, preferred_element_type=f32)
+        normed, weight_ref[...], (((1,), (1,)), ((), ())), preferred_element_type=f32
+    )
 
 
 def project(gated, gain, weight):
@@ -254,7 +347,7 @@
         out_specs=fixed(1, 4 * group),
         scratch_shapes=[pltpu.VMEM((group, subs * columns), f32), pltpu.VMEM((group, 128), f32)],
         compiler_params=pltpu.CompilerParams(
-            dimension_semantics=("arbitrary",), vmem_limit_bytes=24 * 2**20
+            dimension_semantics=("arbitrary",), vmem_limit_bytes=58 * 2**20
         ),
         cost_estimate=pl.CostEstimate(flops=2 * 64 * 4096 * 1024, bytes_accessed=9 << 20, transcendentals=0),
     )(start, chosen, gain, target, weight)
@@ -293,16 +386,10 @@
     tail = [inner_input[rows - margin :], state_inputs[0, rows - margin :], state_inputs[1, rows - margin :], flags]
     tail = lax.ppermute(jnp.concatenate(tail, axis=1), CTX, [(i, i + 1) for i in range(chunks - 1)])
 
-    half = part // 2
-    by_half = lambda a: jnp.swapaxes(a.reshape(chunks, 2, half, -1), 0, 1).reshape(channels, -1)
-    out_full = lax.all_gather(by_half(out_weight).T, SUB, axis=0, tiled=True)
-    gain = by_half(norm_gain)
-    gain = jnp.repeat(gain.reshape(2, channels // 2), group, axis=0).T
+    out_full = lax.all_gather(out_weight.T, SUB, axis=0, tiled=True)
     head_full = lax.all_gather(head_weight, SUB, axis=0)
     pick = (jnp.arange(rows)[None, :] == local_rows[:, None]).astype(bf16)
     rows_residual = jnp.dot(pick, residual, preferred_element_type=f32).astype(bf16)
-    swap = [(i * planes + k, k * planes + i) for i in range(planes) for k in range(planes)]
-    rows_residual = lax.ppermute(rows_residual, PLANE, swap)
     own = lax.dynamic_index_in_dim(targets.reshape(planes, subs, count), lax.axis_index(SUB), 1, False).reshape(group, 1)
 
     by_head = jnp.stack([decay_rate, skip_gain], axis=1)
@@ -311,40 +398,14 @@
     )
     message, rows_residual = lax.optimization_barrier((message, rows_residual))
     came = exchange(message, CTX)
-
-    side = came[:, part:].astype(f32)
-    states = (came[:, :part].astype(f32) * jnp.exp2(side[:, :, 36:37] - 15.0)).reshape(channels, -1)
-    one = side[:, 0]
-    reads = jnp.concatenate([side[:, :count, 64:], side[:, count:, 64:]], axis=2)
-    reads = reads * jnp.exp2(one[:, 40:48] - 15.0)[:, :, None]
-
-    def by_group(a):
-        return jnp.swapaxes(a.reshape(planes, subs, *a.shape[1:]), 0, 1)
-
-    reads = by_group(reads).reshape(total, -1)
-    met = lax.dot_general(states, reads, (((1,), (1,)), ((), ())), precision=lax.Precision.HIGH).reshape(chunks, part, total)
-    end_log = decoded_log(one[:, 32], one[:, 33])
-    rows_log = by_group(decoded_log(one[:, 16:24], one[:, 24:32])).reshape(1, total)
-    lane = jnp.arange(total)
-    chunk_of = (lane // count) % planes * subs + lane // group
-    index = jnp.arange(chunks)
-    before = index[:, None] < chunk_of[None, :]
-    between = jnp.dot(
-        (index[None, :] > index[:, None]).astype(f32), jnp.where(before, end_log[:, None], 0.0), precision=precise
-    )
-    weights = jnp.where(before, jnp.exp(between + rows_log), 0.0)
-    across = jnp.sum(weights[:, None, :] * met, axis=0)
-    local = side[:, :, :8] * jnp.exp2(side[:, :, 34:35] - 15.0)
-    gate = side[:, :, 8:16] * jnp.exp2(side[:, :, 35:36] - 15.0)
-    pair = jnp.stack([local, gate], axis=0).reshape(2, planes, subs, part, count)
-    local, gate = pair.transpose(0, 3, 2, 1, 4).reshape(2, part, total)
-    gated = (across + local) * jax.nn.silu(gate)
-    gated = gated.reshape(2, half, subs, group).transpose(2, 1, 0, 3).reshape(subs, half, 2 * group)
-    gated = jnp.broadcast_to(gated[None], (planes, subs, half, 2 * group)).reshape(chunks, half, 2 * group)
-
+    swap = [(i * planes + k, k * planes + i) for i in range(planes) for k in range(planes)]
+    rows_residual = lax.ppermute(rows_residual, PLANE, swap)
+    came, rows_residual = lax.optimization_barrier((came, rows_residual))
+
+    gated, out_full = lax.optimization_barrier((carry(came, planes, subs), out_full))
     gated = exchange(gated, CTX).reshape(channels // 2, 2 * group)
 
-    partial = exchange(project(gated, gain, out_full).reshape(planes, count, -1), "tp")
+    partial = exchange(project(gated, norm_gain.reshape(1, -1), out_full).reshape(planes, count, -1), "tp")
     chosen = (jnp.sum(partial, axis=0) + rows_residual.astype(f32)).astype(bf16)
 
     chosen = to_everyone(chosen, PLANE).reshape(planes, group, -1)

time: 166 us -> 161 us (0.970)
  blocking collectives: 41.6 us -> 63.1 us
  waiting for transfers between devices: 50 us -> 33.7 us
  starting transfers between devices: 35.6 us -> 22.4 us
  Pallas kernels: 6.87 us -> 13.9 us
  local copies, waits for them, and re-layouts: 12.7 us -> 9.71 us
    all_to_all x3 -> x4, blocking collectives: 41.6 us -> 63.1 us  [exchange(): return lax.all_to_all(blocks, axes, 0, 0, tiled=True)]
    all_to_all x3 -> x2, waiting for transfers between devices: 46 us -> 31.5 us  [exchange(): return lax.all_to_all(blocks, axes, 0, 0, tiled=True)]
    all_to_all x3 -> x2, starting transfers between devices: 30.3 us -> 17.1 us  [exchange(): return lax.all_to_all(blocks, axes, 0, 0, tiled=True)]
    pallas_call x1, Pallas kernels: 3.93 us -> 8.2 us  [score(): pl.pallas_call(functools.partial(logits_kernel, steps=slabs, stride=strid...]
    unnamed x37 -> x18, local copies, waits for them, and re-layouts: 6.07 us -> 3.4 us
    ppermute x1, waiting for transfers between devices: 3.25 us -> 0.8 us  [body(): lax.ppermute(jnp.concatenate(tail, axis=1), CTX, [(i, i + 1) for i in ran...]
  transfers between devices with their start and end apart: 7 -> 6, of which waited for: 4 -> 3; matrix products, arithmetic and copies ran while one was open for 5% -> 5% of each run, Pallas kernels for 2% -> 4%
where the time goes in v2:
time: 161 us
  blocking collectives  63.1 us (39%)
  waiting for transfers between devices  33.7 us (21%)
  starting transfers between devices  22.4 us (14%)
  between operations  14.2 us (9%)
  Pallas kernels  13.9 us (9%)
  local copies, waits for them, and re-layouts  9.71 us (6%)
  other arithmetic  3.52 us (2%)
    all_to_all x4, blocking collectives, exchange(): return lax.all_to_all(blocks, axes, 0, 0, tiled=True)  63.1 us
    all_to_all x2, waiting for transfers between devices, exchange(): return lax.all_to_all(blocks, axes, 0, 0, tiled=True)  31.5 us
    all_to_all x2, starting transfers between devices, exchange(): return lax.all_to_all(blocks, axes, 0, 0, tiled=True)  17.1 us
    pallas_call x1, Pallas kernels, score(): pl.pallas_call(functools.partial(logits_kernel, steps=slabs, stride=strid...  8.2 us
    ppermute x1, starting transfers between devices, body(): lax.ppermute(jnp.concatenate(tail, axis=1), CTX, [(i, i + 1) for i in ran...  4.5 us
    pallas_call x1, Pallas kernels, local_part(): pl.pallas_call(local_kernel, out_shape=jax.ShapeDtypeStruct((channels //...  3.42 us
    unnamed x18, local copies, waits for them, and re-layouts  3.4 us
  transfers between devices with their start and end apart: 6, of which 3 were waited for; matrix products, arithmetic and copies ran while one was open for 5% of the time, Pallas kernels for 4%

profile of v2, /device:TPU:1, one launch (start us, length us, event | category | flops | bytes accessed | tf_op | source)
XLA Modules:
  0.0 160.7 jit_solution(281453821916581010)
XLA Ops:
  7.2 0.0 copy-start
  7.2 0.0 all-gather.4.cloned.1.call-start
  7.2 0.7 all-gather.4.cloned.1.call-update
  7.9 0.0 all-gather.6.cloned.1.call-start
  8.0 0.7 all-gather.6.cloned.1.call-update
  8.7 0.8 slice.23
  9.4 0.7 convert.3
  10.1 0.1 slice.26
  10.2 0.7 slice_bitcast_fusion.1
  10.9 0.1 broadcast_in_dim.10
  11.0 4.5 %collective-permute-start = (bf16[16,1408]{1,0:T(8,128)(2,1)S(1)}, bf16[16,1408]{1,0:T(8,128)(2,1)S(1)}, u32[]{:S(2)}, u32[]{:S(2)}) collective-permute-start(bf16[16,1408]{1,0:T(8,128)(2,1)S(1)} %pad_maximum_fusion), channel_id=1, source_target_pairs={{0,8},{8,16},{16,24},{24,32},{32,40},{40,48},{48,56},{56,64},{64,7... | collective-permute-start | bytes 135176 | tf_op jit(solution)/shard_map/ppermute | solution.py:387
  15.5 0.7 fusion.3
  16.1 0.7 broadcast_subtract_fusion
  16.8 0.2 convolution_convert_fusion
  17.0 0.7 pad_maximum_fusion.1
  17.7 0.7 copy.44.place_ref
  18.3 0.7 copy.45.head_ref
  19.0 0.8 collective-permute-done.tail_ref
  19.8 0.6 copy-done.4
  20.4 3.4 %shard_map.176 = s16[64,32,128]{2,1,0:T(8,128)(2,1)} custom-call(s32[8,1]{1,0:T(8,128)} %copy.44.place_ref, bf16[128,1024]{1,0:T(8,128)(2,1)} %stream_ref.1, bf16[2,128,128]{2,1,0:T(8,128)(2,1)} %state_ref.1, bf16[16,1408]{1,0:T(8,128)(2,1)} %copy-done.4, bf16[128,1024]{1,0:T(8,128)(2,1)} %gate_ref.1, f32[16,128]{1,0:T(8,128)} %step_ref.1, ...), custom_call_target="tpu_custom_call" | custom-call | flops 134217728 | bytes 2097152 | tf_op jit(solution)/shard_map/pallas_call | solution.py:166
  23.9 12.5 %all-to-all-start = ((s16[64,32,128]{2,1,0:T(8,128)(2,1)}), s16[64,32,128]{2,1,0:T(8,128)(2,1)S(1)}, u32[]{:S(2)}, u32[]{:S(2)}) async-start(s16[64,32,128]{2,1,0:T(8,128)(2,1)} %shard_map.176), calls=%async_computation | async-start | bytes 1048576 | tf_op jit(solution)/shard_map/all_to_all | solution.py:23
  36.4 0.7 collective-permute-start.1
  37.0 17.0 %all-to-all-done.came_ref = s16[64,32,128]{2,1,0:T(8,128)(2,1)S(1)} async-done(((s16[64,32,128]{2,1,0:T(8,128)(2,1)}), s16[64,32,128]{2,1,0:T(8,128)(2,1)S(1)}, u32[]{:S(2)}, u32[]{:S(2)}) %all-to-all-start) | async-done | bytes 524320 | tf_op jit(solution)/shard_map/all_to_all | solution.py:23
  54.1 1.5 shard_map.177
  55.6 0.0 all-gather.4.cloned.1.call-done.weight_ref
  55.6 19.9 %all_to_all.30 = f32[64,8,128]{2,1,0:T(8,128)S(1)} all-to-all(f32[64,8,128]{2,1,0:T(8,128)S(1)} %shard_map.177), channel_id=1, replica_groups=mesh['z'=8,'x'=4,'core'=2,'tp'=8] {'z','x','core'}, dimensions={0} | all-to-all | bytes 524288 | tf_op jit(solution)/shard_map/all_to_all | solution.py:23
  75.5 1.2 copy-done.1
  76.8 0.7 copy-done.2
  77.4 0.7 shard_map.178
  78.2 14.2 %all_to_all.31 = f32[8,8,512]{2,1,0:T(8,128)S(1)} all-to-all(f32[8,8,512]{2,1,0:T(8,128)S(1)} %bitcast.25), channel_id=1, replica_groups=mesh['z'=8,'x'=4,'core'=2,'tp'=8] {'tp'}, dimensions={0} | all-to-all | bytes 262144 | tf_op jit(solution)/shard_map/all_to_all | solution.py:23
  92.4 0.9 broadcast_in_dim.11
  93.3 4.6 %all-to-all-start.3 = ((bf16[64,8,512]{2,1,0:T(8,128)(2,1)}), bf16[64,8,512]{2,1,0:T(8,128)(2,1)S(1)}, u32[]{:S(2)}, u32[]{:S(2)}) async-start(bf16[64,8,512]{2,1,0:T(8,128)(2,1)} %broadcast_in_dim.11), calls=%async_computation.3 | async-start | bytes 1048576 | tf_op jit(solution)/shard_map/all_to_all | solution.py:23
  98.0 0.1 reshape.75
  98.1 0.7 reshape.80.target_ref
  98.8 0.6 reshape.74.gain_ref
  99.4 14.4 %all-to-all-done.3 = bf16[64,8,512]{2,1,0:T(8,128)(2,1)S(1)} async-done(((bf16[64,8,512]{2,1,0:T(8,128)(2,1)}), bf16[64,8,512]{2,1,0:T(8,128)(2,1)S(1)}, u32[]{:S(2)}, u32[]{:S(2)}) %all-to-all-start.3) | async-done | bytes 524320 | tf_op jit(solution)/shard_map/all_to_all | solution.py:23
  113.8 0.8 copy-done.3
  114.6 8.2 %shard_map.179 = f32[1,256]{1,0:T(1,128)} custom-call(s32[1]{0:T(128)} %bitcast.start_ref, bf16[8,64,512]{2,1,0:T(8,128)(2,1)} %bitcast.28, f32[8,512]{1,0:T(8,128)} %reshape.74.gain_ref, s32[64,1]{1,0:T(8,128)} %reshape.80.target_ref, bf16[8,4096,128]{2,1,0:T(8,128)(2,1)} %bitcast.27), custom_call_target="tpu_custom_call" | custom-call | flops 536870912 | bytes 9437184 | tf_op jit(solution)/shard_map/pallas_call | solution.py:336
  122.8 0.7 broadcast_in_dim.13
  123.5 18.4 %all_to_all.32 = f32[64,1,256]{2,1,0:T(1,128)S(1)} all-to-all(f32[64,1,256]{2,1,0:T(1,128)S(1)} %broadcast_in_dim.13), channel_id=1, replica_groups=mesh['z'=8,'x'=4,'core'=2,'tp'=8] {'z','tp'}, dimensions={0} | all-to-all | bytes 131072 | tf_op jit(solution)/shard_map/all_to_all | solution.py:23
  141.9 0.2 reduce.3
  142.1 0.1 reshape.77
  142.2 0.1 fusion.1
  142.4 0.1 sub.41
  142.5 10.6 %all_to_all.33 = f32[8,8,8]{2,1,0:T(8,128)S(1)} all-to-all(f32[8,8,8]{2,1,0:T(8,128)S(1)} %broadcast_in_dim.14), channel_id=1, replica_groups=mesh['z'=8,'x'=4,'core'=2,'tp'=8] {'x','core'}, dimensions={0} | all-to-all | bytes 4096 | tf_op jit(solution)/shard_map/all_to_all | solution.py:23
  153.1 0.1 reshape.78
  153.2 0.0 copy-start.6
  153.2 0.6 multiply_multiply_fusion
  (24 shorter events, 0.2 us)
Async XLA Ops:
  7.2 9.6 %copy-start = (bf16[128,512]{1,0:T(8,128)(2,1)S(1)}, bf16[128,512]{1,0:T(8,128)(2,1)}, u32[]{:S(2)}) copy-start(bf16[128,512]{1,0:T(8,128)(2,1)} %param.28) | copy-start | bytes 393220
  7.2 90.8 %copy-start.7 = (s32[512]{0:T(512)S(1)}, s32[512]{0:T(512)}, u32[]{:S(2)}) copy-start(s32[512]{0:T(512)} %param.32) | copy-start | bytes 6148
  7.2 91.6 %copy-start.5 = (f32[4096]{0:T(1024)S(1)}, f32[4096]{0:T(1024)}, u32[]{:S(2)}) copy-start(f32[4096]{0:T(1024)} %param.29) | copy-start | bytes 49156
  7.2 48.4 %all-gather.4.cloned.1.call-start = ((), (), s32[]{:S(2)}) async-start(), calls=%async_computation.6 | async-start | bytes 1179648 | tf_op jit(solution)/shard_map/all_gather | solution.py:389
  7.9 105.9 %all-gather.6.cloned.1.call-start = ((), (), s32[]{:S(2)}) async-start(), calls=%async_computation.7 | async-start | bytes 9437184 | tf_op jit(solution)/shard_map/all_gather | solution.py:390
  11.0 8.9 %collective-permute-start = (bf16[16,1408]{1,0:T(8,128)(2,1)S(1)}, bf16[16,1408]{1,0:T(8,128)(2,1)S(1)}, u32[]{:S(2)}, u32[]{:S(2)}) collective-permute-start(bf16[16,1408]{1,0:T(8,128)(2,1)S(1)} %pad_maximum_fusion), channel_id=1, source_target_pairs={{0,8},{8,16},{16,24},{24,32},{32,40},{40,48},{48,56},{56,64},{64,7... | collective-permute-start | bytes 135176 | tf_op jit(solution)/shard_map/ppermute | solution.py:387
  19.8 0.6 copy-start.4
  23.9 129.3 %copy-start.8 = (f32[512]{0:T(512)S(1)}, f32[512]{0:T(512)}, u32[]{:S(2)}) copy-start(f32[512]{0:T(512)} %param.33) | copy-start | bytes 6148
  23.9 30.2 %all-to-all-start = ((s16[64,32,128]{2,1,0:T(8,128)(2,1)}), s16[64,32,128]{2,1,0:T(8,128)(2,1)S(1)}, u32[]{:S(2)}, u32[]{:S(2)}) async-start(s16[64,32,128]{2,1,0:T(8,128)(2,1)} %shard_map.176), calls=%async_computation | async-start | bytes 1048576 | tf_op jit(solution)/shard_map/all_to_all | solution.py:23
  36.4 0.7 collective-permute-start.1
  75.5 1.2 copy-start.1
  76.8 0.7 copy-start.2
  93.3 20.5 %all-to-all-start.3 = ((bf16[64,8,512]{2,1,0:T(8,128)(2,1)}), bf16[64,8,512]{2,1,0:T(8,128)(2,1)S(1)}, u32[]{:S(2)}, u32[]{:S(2)}) async-start(bf16[64,8,512]{2,1,0:T(8,128)(2,1)} %broadcast_in_dim.11), calls=%async_computation.3 | async-start | bytes 1048576 | tf_op jit(solution)/shard_map/all_to_all | solution.py:23
  113.8 0.8 copy-start.3
  153.2 0.6 copy-start.6
Sparse Core Ops, SparseCore 0:
  10.2 35.7 all-gather.3
  48.1 58.9 all-gather.5

commit v3 on v2

--- a/solution.py
+++ b/solution.py
@@ -267,7 +267,8 @@
     )(came)
 
 
-def project_kernel(gated_ref, gain_ref, weight_ref, out_ref):
+def project_kernel(place_ref, gated_ref, gain_ref, *refs):
+    weights, out_ref = refs[:-1], refs[-1]
     gated = gated_ref[...]
     depth, lanes = gated.shape
     half = lanes // 2
@@ -277,26 +278,31 @@
     pair = [a.reshape(depth // 8, 1, 8, lanes) for a in (normed, pltpu.roll(normed, half, 1))]
     normed = jnp.concatenate(pair, axis=1).reshape(2 * depth, lanes).T[:half]
     normed = (normed * gain_ref[...]).astype(bf16)
-    out_ref[...] = lax.dot_general(
-        normed, weight_ref[...], (((1,), (1,)), ((), ())), preferred_element_type=f32
-    )
-
-
-def project(gated, gain, weight):
+    for k, weight_ref in enumerate(weights):
+        width = weight_ref.shape[0]
+        columns = pl.ds(pl.multiple_of(place_ref[k] * width, width), width)
+        out_ref[:, columns] = lax.dot_general(
+            normed, weight_ref[...], (((1,), (1,)), ((), ())), preferred_element_type=f32
+        )
+
+
+def project(place, gated, gain, weights):
+    columns = sum(weight.shape[0] for weight in weights)
     return pl.pallas_call(
         project_kernel,
-        out_shape=jax.ShapeDtypeStruct((gated.shape[1] // 2, weight.shape[0]), f32),
-        in_specs=[whole] * 3,
+        out_shape=jax.ShapeDtypeStruct((gated.shape[1] // 2, columns), f32),
+        in_specs=[pl.BlockSpec(memory_space=pltpu.SMEM)] + [whole] * (2 + len(weights)),
         out_specs=whole,
         compiler_params=pltpu.CompilerParams(vmem_limit_bytes=8 * 2**20),
         cost_estimate=pl.CostEstimate(flops=2 * 64 * 1024 * 512, bytes_accessed=1 << 21, transcendentals=0),
-    )(gated, gain, weight)
-
-
-def logits_kernel(start_ref, chosen_ref, gain_ref, target_ref, weight_ref, out_ref, total_ref, inverse_ref, *, steps, stride):
+    )(place, gated, gain, *weights)
+
+
+def logits_kernel(start_ref, chosen_ref, gain_ref, target_ref, *refs, steps):
+    weights, (out_ref, total_ref, inverse_ref) = refs[:-3], refs[-3:]
     step = pl.program_id(0)
     slabs, group, width = chosen_ref.shape
-    subs, _, columns = weight_ref.shape
+    columns = weights[0].shape[1]
 
     @pl.when(step == 0)
     def _():
@@ -308,7 +314,7 @@
         total_ref[...] = jnp.zeros_like(total_ref)
 
     features = chosen_ref[step].astype(f32) * inverse_ref[:, :1] * gain_ref[pl.ds(step, 1), :]
-    weight = jnp.concatenate([weight_ref[k] for k in range(subs)], axis=1)
+    weight = jnp.concatenate([weight_ref[...] for weight_ref in weights], axis=1)
     total_ref[...] += jnp.dot(features.astype(bf16), weight, preferred_element_type=f32)
 
     @pl.when(step == steps - 1)
@@ -318,8 +324,8 @@
         summed = jnp.sum(jnp.exp(logits - top), axis=1, keepdims=True)
         picked = jnp.zeros((group, 1), f32)
         lane = lax.broadcasted_iota(jnp.int32, (group, columns), 1)
-        for k in range(subs):
-            own = lane + (start_ref[0] + k * stride) == target_ref[...]
+        for k in range(len(weights)):
+            own = lane + start_ref[k] == target_ref[...]
             picked = picked + jnp.sum(
                 jnp.where(own, logits[:, k * columns : (k + 1) * columns], 0.0), axis=1, keepdims=True
             )
@@ -329,12 +335,12 @@
         out_ref[...] = pair
 
 
-def score(start, chosen, gain, target, weight, stride):
+def score(starts, chosen, gain, target, weights):
     slabs, group, width = chosen.shape
-    subs, _, columns = weight.shape
+    columns = weights[0].shape[1]
     fixed = lambda *shape: pl.BlockSpec(shape, lambda k: (0,) * len(shape))
     return pl.pallas_call(
-        functools.partial(logits_kernel, steps=slabs, stride=stride),
+        functools.partial(logits_kernel, steps=slabs),
         grid=(slabs,),
         out_shape=jax.ShapeDtypeStruct((1, 4 * group), f32),
         in_specs=[
@@ -342,15 +348,23 @@
             fixed(slabs, group, width),
             fixed(slabs, width),
             fixed(group, 1),
-            pl.BlockSpec((subs, width, columns), lambda k: (0, k, 0)),
+            *[pl.BlockSpec((width, columns), lambda k: (k, 0)) for _ in weights],
         ],
         out_specs=fixed(1, 4 * group),
-        scratch_shapes=[pltpu.VMEM((group, subs * columns), f32), pltpu.VMEM((group, 128), f32)],
+        scratch_shapes=[pltpu.VMEM((group, len(weights) * columns), f32), pltpu.VMEM((group, 128), f32)],
         compiler_params=pltpu.CompilerParams(
-            dimension_semantics=("arbitrary",), vmem_limit_bytes=58 * 2**20
+            dimension_semantics=("arbitrary",), vmem_limit_bytes=24 * 2**20
         ),
         cost_estimate=pl.CostEstimate(flops=2 * 64 * 4096 * 1024, bytes_accessed=9 << 20, transcendentals=0),
-    )(start, chosen, gain, target, weight)
+    )(starts, chosen, gain, target, *weights)
+
+
+def shifted(shard, axis, by):
+    size = lax.axis_size(axis)
+    return lax.ppermute(shard, axis, [(i, (i + by) % size) for i in range(size)])
+
+
+together = lambda *arrays: lax.optimization_barrier(arrays)
 
 
 def body(
@@ -386,8 +400,6 @@
     tail = [inner_input[rows - margin :], state_inputs[0, rows - margin :], state_inputs[1, rows - margin :], flags]
     tail = lax.ppermute(jnp.concatenate(tail, axis=1), CTX, [(i, i + 1) for i in range(chunks - 1)])
 
-    out_full = lax.all_gather(out_weight.T, SUB, axis=0, tiled=True)
-    head_full = lax.all_gather(head_weight, SUB, axis=0)
     pick = (jnp.arange(rows)[None, :] == local_rows[:, None]).astype(bf16)
     rows_residual = jnp.dot(pick, residual, preferred_element_type=f32).astype(bf16)
     own = lax.dynamic_index_in_dim(targets.reshape(planes, subs, count), lax.axis_index(SUB), 1, False).reshape(group, 1)
@@ -396,23 +408,43 @@
     message = local_part(
         local_rows.reshape(-1, 1), inner_input, state_inputs, tail, gate_input, step_size, resets.reshape(1, rows), by_head, conv_inner, conv_state
     )
-    message, rows_residual = lax.optimization_barrier((message, rows_residual))
+    across = lax.axis_index("x")
+    core = lax.axis_index("core")
+    message, rows_residual, own_out = together(message, rows_residual, out_weight.T)
+    heads = head_weight
     came = exchange(message, CTX)
     swap = [(i * planes + k, k * planes + i) for i in range(planes) for k in range(planes)]
     rows_residual = lax.ppermute(rows_residual, PLANE, swap)
-    came, rows_residual = lax.optimization_barrier((came, rows_residual))
-
-    gated, out_full = lax.optimization_barrier((carry(came, planes, subs), out_full))
+    other_out = shifted(own_out, "core", 1)
+    heads_left = shifted(heads, "x", 1)
+    heads_right = shifted(heads, "x", -1)
+    pair = jnp.concatenate([jnp.where(core == 0, own_out, other_out), jnp.where(core == 0, other_out, own_out)], axis=0)
+    came, rows_residual, pair, heads_left, heads_right = together(came, rows_residual, pair, heads_left, heads_right)
+
+    gated, pair = together(carry(came, planes, subs), pair)
     gated = exchange(gated, CTX).reshape(channels // 2, 2 * group)
-
-    partial = exchange(project(gated, norm_gain.reshape(1, -1), out_full).reshape(planes, count, -1), "tp")
+    pairs = [pair, *(shifted(pair, "x", by) for by in (1, -1, 2))]
+    heads_far = shifted(heads, "x", 2)
+    gated, pairs, heads_far = together(gated, pairs, heads_far)
+
+    width = lax.axis_size("x")
+    places = [(across - by) % width for by in (0, 1, -1, 2)]
+    partial = project(jnp.stack(places), gated, norm_gain.reshape(1, -1), pairs)
+    partial, heads_left = together(partial, heads_left)
+    partial = exchange(partial.reshape(planes, count, -1), "tp")
+    others = [shifted(heads, "core", 1), shifted(heads_left, "core", 1)]
+    partial, others = together(partial, others)
     chosen = (jnp.sum(partial, axis=0) + rows_residual.astype(f32)).astype(bf16)
 
+    chosen, heads_right, heads_far = together(chosen, heads_right, heads_far)
     chosen = to_everyone(chosen, PLANE).reshape(planes, group, -1)
+    others = [*others, shifted(heads_right, "core", 1), shifted(heads_far, "core", 1)]
+    chosen, others = together(chosen, others)
     columns = head_weight.shape[1]
-    ways = lax.axis_size("tp")
-    start = (lax.axis_index("z") * subs * ways + lax.axis_index("tp")) * columns
-    found = score(start.reshape(1), chosen, final_gain.reshape(planes, -1), own, head_full, ways * columns)
+    starts = jnp.stack([lax.axis_index("z") * subs + x * 2 + c for c in (core, 1 - core) for x in places])
+    starts = (starts * lax.axis_size("tp") + lax.axis_index("tp")) * columns
+    weights = [heads, heads_left, heads_right, heads_far, *others]
+    found = score(starts, chosen, final_gain.reshape(planes, -1), own, weights)
 
     found = to_everyone(found, PLANE).reshape(chunks, 4, group)
     top = jnp.max(found[:, 0], axis=0)

time: 161 us -> 184 us (1.14)
  starting transfers between devices: 22.4 us -> 83.5 us
  blocking collectives: 63.1 us -> 28.7 us
  between operations: 14.2 us -> 1.04 us
  waiting for transfers between devices: 33.7 us -> 44.8 us
  other arithmetic: 3.52 us -> 1.67 us
    ppermute x0 -> x11, starting transfers between devices: none -> 35.1 us  [shifted(): lax.ppermute(shard, axis, [(i, (i + by) % size) for i in range(size)])]
    all_to_all x4 -> x2, blocking collectives: 63.1 us -> 28.7 us  [exchange(): return lax.all_to_all(blocks, axes, 0, 0, tiled=True)]
    all_to_all x2 -> x4, starting transfers between devices: 17.1 us -> 40.6 us  [exchange(): return lax.all_to_all(blocks, axes, 0, 0, tiled=True)]
    ppermute x0 -> x11, waiting for transfers between devices: none -> 6.5 us  [shifted(): lax.ppermute(shard, axis, [(i, (i + by) % size) for i in range(size)])]
    all_to_all x2 -> x4, waiting for transfers between devices: 31.5 us -> 34.6 us  [exchange(): return lax.all_to_all(blocks, axes, 0, 0, tiled=True)]
    ppermute x1, waiting for transfers between devices: 0.8 us -> 3.63 us  [body(): lax.ppermute(jnp.concatenate(tail, axis=1), CTX, [(i, i + 1) for i in ran...]
    ppermute x1, starting transfers between devices: 4.5 us -> 7.1 us  [body(): lax.ppermute(jnp.concatenate(tail, axis=1), CTX, [(i, i + 1) for i in ran...]
    unnamed x18 -> x24, local copies, waits for them, and re-layouts: 3.4 us -> 3.93 us
  transfers between devices with their start and end apart: 6 -> 17, of which waited for: 3 -> 7; matrix products, arithmetic and copies ran while one was open for 5% -> 2% of each run, Pallas kernels for 4% -> 4%
where the time goes in v3:
time: 184 us; the launch traced here: 183 us
  starting transfers between devices  83.5 us (45%)
  waiting for transfers between devices  44.8 us (24%)
  blocking collectives  28.7 us (16%)
  Pallas kernels  14.9 us (8%)
  local copies, waits for them, and re-layouts  8.31 us (5%)
    all_to_all x4, starting transfers between devices, exchange(): return lax.all_to_all(blocks, axes, 0, 0, tiled=True)  40.6 us
    ppermute x11, starting transfers between devices, shifted(): lax.ppermute(shard, axis, [(i, (i + by) % size) for i in range(size)])  35.1 us
    all_to_all x4, waiting for transfers between devices, exchange(): return lax.all_to_all(blocks, axes, 0, 0, tiled=True)  34.6 us
    all_to_all x2, blocking collectives, exchange(): return lax.all_to_all(blocks, axes, 0, 0, tiled=True)  28.7 us
    pallas_call x1, Pallas kernels, score(): pl.pallas_call(functools.partial(logits_kernel, steps=slabs), grid=(slabs...  7.2 us
    ppermute x1, starting transfers between devices, body(): lax.ppermute(jnp.concatenate(tail, axis=1), CTX, [(i, i + 1) for i in ran...  7.1 us
    ppermute x11, waiting for transfers between devices, shifted(): lax.ppermute(shard, axis, [(i, (i + by) % size) for i in range(size)])  6.5 us
    unnamed x24, local copies, waits for them, and re-layouts  3.93 us
  transfers between devices with their start and end apart: 17, of which 7 were waited for; matrix products, arithmetic and copies ran while one was open for 2% of the time, Pallas kernels for 4%

profile of v3, /device:TPU:1, one launch (start us, length us, event | category | flops | bytes accessed | tf_op | source)
XLA Modules:
  0.0 183.1 jit_solution(9434570357172485739)
XLA Ops:
  0.6 4.1 %collective-permute-start.3 = (bf16[4096,128]{1,0:T(8,128)(2,1)}, bf16[4096,128]{1,0:T(8,128)(2,1)S(1)}, u32[]{:S(2)}, u32[]{:S(2)}) collective-permute-start(bf16[4096,128]{1,0:T(8,128)(2,1)} %refs_0_.1), channel_id=1, source_target_pairs={{0,16},{16,32},{32,48},{48,0},{1,17},{17,33},{33,49},{49,1},{2,18}... | collective-permute-start | bytes 3145736 | tf_op jit(solution)/shard_map/ppermute | solution.py:364
  4.7 3.2 %collective-permute-start.4 = (bf16[4096,128]{1,0:T(8,128)(2,1)}, bf16[4096,128]{1,0:T(8,128)(2,1)}, u32[]{:S(2)}, u32[]{:S(2)}) collective-permute-start(bf16[4096,128]{1,0:T(8,128)(2,1)} %refs_0_.1), channel_id=1, source_target_pairs={{0,48},{16,0},{32,16},{48,32},{1,49},{17,1},{33,17},{49,33},{2,50}... | collective-permute-start | bytes 3145736 | tf_op jit(solution)/shard_map/ppermute | solution.py:364
  7.9 0.7 convert.3
  8.7 0.7 slice_bitcast_fusion.1
  9.5 0.7 slice-done
  10.1 7.1 %collective-permute-start = (bf16[16,1408]{1,0:T(8,128)(2,1)S(1)}, bf16[16,1408]{1,0:T(8,128)(2,1)S(1)}, u32[]{:S(2)}, u32[]{:S(2)}) collective-permute-start(bf16[16,1408]{1,0:T(8,128)(2,1)S(1)} %pad_maximum_fusion.1), channel_id=1, source_target_pairs={{0,8},{8,16},{16,24},{24,32},{32,40},{40,48},{48,56},{56,64},{64,7... | collective-permute-start | bytes 135176 | tf_op jit(solution)/shard_map/ppermute | solution.py:401
  17.3 0.6 copy-done.11
  17.9 0.2 convolution_convert_fusion
  18.1 0.7 copy-done.9
  18.8 0.7 copy.44.place_ref
  19.5 0.7 copy.45.head_ref
  20.1 3.6 %collective-permute-done.tail_ref = bf16[16,1408]{1,0:T(8,128)(2,1)S(1)} collective-permute-done((bf16[16,1408]{1,0:T(8,128)(2,1)S(1)}, bf16[16,1408]{1,0:T(8,128)(2,1)S(1)}, u32[]{:S(2)}, u32[]{:S(2)}) %collective-permute-start) | collective-permute-done | bytes 45088 | tf_op jit(solution)/shard_map/ppermute | solution.py:401
  23.8 0.6 copy-done.4
  24.4 3.5 %shard_map.176 = s16[64,32,128]{2,1,0:T(8,128)(2,1)} custom-call(s32[8,1]{1,0:T(8,128)} %copy.44.place_ref, bf16[128,1024]{1,0:T(8,128)(2,1)} %stream_ref.1, bf16[2,128,128]{2,1,0:T(8,128)(2,1)} %state_ref.1, bf16[16,1408]{1,0:T(8,128)(2,1)} %copy-done.4, bf16[128,1024]{1,0:T(8,128)(2,1)} %gate_ref.1, f32[16,128]{1,0:T(8,128)} %step_ref.1, ...), custom_call_target="tpu_custom_call" | custom-call | flops 134217728 | bytes 2097152 | tf_op jit(solution)/shard_map/pallas_call | solution.py:166
  27.9 18.8 %all-to-all-start = ((s16[64,32,128]{2,1,0:T(8,128)(2,1)}), s16[64,32,128]{2,1,0:T(8,128)(2,1)S(1)}, u32[]{:S(2)}, u32[]{:S(2)}) async-start(s16[64,32,128]{2,1,0:T(8,128)(2,1)} %shard_map.176), calls=%async_computation | async-start | bytes 1048576 | tf_op jit(solution)/shard_map/all_to_all | solution.py:23
  46.7 4.8 %collective-permute-start.8 = (bf16[4096,128]{1,0:T(8,128)(2,1)S(1)}, bf16[4096,128]{1,0:T(8,128)(2,1)}, u32[]{:S(2)}, u32[]{:S(2)}) collective-permute-start(bf16[4096,128]{1,0:T(8,128)(2,1)S(1)} %copy-done.1), channel_id=1, source_target_pairs={{0,32},{16,48},{32,0},{48,16},{1,33},{17,49},{33,1},{49,17},{2,34}... | collective-permute-start | bytes 3145736 | tf_op jit(solution)/shard_map/ppermute | solution.py:364
  51.5 2.5 %collective-permute-start.2 = (bf16[64,1024]{1,0:T(8,128)(2,1)S(1)}, bf16[64,1024]{1,0:T(8,128)(2,1)S(1)}, u32[]{:S(2)}, u32[]{:S(2)}) collective-permute-start(bf16[64,1024]{1,0:T(8,128)(2,1)S(1)} %bitcast.40), channel_id=1, source_target_pairs={{0,8},{8,0},{1,9},{9,1},{2,10},{10,2},{3,11},{11,3},{4,12},{12,4},... | collective-permute-start | bytes 393224 | tf_op jit(solution)/shard_map/ppermute | solution.py:364
  54.1 0.7 collective-permute-start.1
  54.8 0.3 collective-permute-done.2
  55.1 9.4 %all-to-all-done.came_ref = s16[64,32,128]{2,1,0:T(8,128)(2,1)S(1)} async-done(((s16[64,32,128]{2,1,0:T(8,128)(2,1)}), s16[64,32,128]{2,1,0:T(8,128)(2,1)S(1)}, u32[]{:S(2)}, u32[]{:S(2)}) %all-to-all-start) | async-done | bytes 524320 | tf_op jit(solution)/shard_map/all_to_all | solution.py:23
  64.5 2.2 %shard_map.177 = f32[64,8,128]{2,1,0:T(8,128)} custom-call(s16[64,32,128]{2,1,0:T(8,128)(2,1)S(1)} %all-to-all-done.came_ref), custom_call_target="tpu_custom_call" | custom-call | flops 268435456 | bytes 1048576 | tf_op jit(solution)/shard_map/pallas_call | solution.py:255
  66.8 11.8 %all-to-all-start.1 = ((f32[64,8,128]{2,1,0:T(8,128)}), f32[64,8,128]{2,1,0:T(8,128)S(1)}, u32[]{:S(2)}, u32[]{:S(2)}) async-start(f32[64,8,128]{2,1,0:T(8,128)} %shard_map.177), calls=%async_computation.1 | async-start | bytes 524288 | tf_op jit(solution)/shard_map/all_to_all | solution.py:23
  78.5 3.3 %collective-permute-start.5 = (bf16[128,1024]{1,0:T(8,128)(2,1)S(1)}, bf16[128,1024]{1,0:T(8,128)(2,1)S(1)}, u32[]{:S(2)}, u32[]{:S(2)}) collective-permute-start(bf16[128,1024]{1,0:T(8,128)(2,1)S(1)} %pad_maximum_fusion.refs_0_), channel_id=1, source_target_pairs={{0,16},{16,32},{32,48},{48,0},{1,17},{17,33},{33,49},{49,1},{2,18}... | collective-permute-start | bytes 786440 | tf_op jit(solution)/shard_map/ppermute | solution.py:364
  81.9 3.2 %collective-permute-start.6 = (bf16[128,1024]{1,0:T(8,128)(2,1)S(1)}, bf16[128,1024]{1,0:T(8,128)(2,1)S(1)}, u32[]{:S(2)}, u32[]{:S(2)}) collective-permute-start(bf16[128,1024]{1,0:T(8,128)(2,1)S(1)} %pad_maximum_fusion.refs_0_), channel_id=1, source_target_pairs={{0,48},{16,0},{32,16},{48,32},{1,49},{17,1},{33,17},{49,33},{2,50}... | collective-permute-start | bytes 786440 | tf_op jit(solution)/shard_map/ppermute | solution.py:364
  85.1 3.6 %collective-permute-start.7 = (bf16[128,1024]{1,0:T(8,128)(2,1)S(1)}, bf16[128,1024]{1,0:T(8,128)(2,1)S(1)}, u32[]{:S(2)}, u32[]{:S(2)}) collective-permute-start(bf16[128,1024]{1,0:T(8,128)(2,1)S(1)} %pad_maximum_fusion.refs_0_), channel_id=1, source_target_pairs={{0,32},{16,48},{32,0},{48,16},{1,33},{17,49},{33,1},{49,17},{2,34}... | collective-permute-start | bytes 786440 | tf_op jit(solution)/shard_map/ppermute | solution.py:364
  88.7 3.1 %collective-permute-start.9 = (bf16[4096,128]{1,0:T(8,128)(2,1)S(1)}, bf16[4096,128]{1,0:T(8,128)(2,1)}, u32[]{:S(2)}, u32[]{:S(2)}) collective-permute-start(bf16[4096,128]{1,0:T(8,128)(2,1)S(1)} %copy-done.1), channel_id=1, source_target_pairs={{0,8},{8,0},{1,9},{9,1},{2,10},{10,2},{3,11},{11,3},{4,12},{12,4},... | collective-permute-start | bytes 3145736 | tf_op jit(solution)/shard_map/ppermute | solution.py:364
  91.9 0.2 collective-permute-done.6.refs_2_
  92.2 5.9 %collective-permute-done.7.refs_3_ = bf16[128,1024]{1,0:T(8,128)(2,1)S(1)} collective-permute-done((bf16[128,1024]{1,0:T(8,128)(2,1)S(1)}, bf16[128,1024]{1,0:T(8,128)(2,1)S(1)}, u32[]{:S(2)}, u32[]{:S(2)}) %collective-permute-start.7) | collective-permute-done | bytes 262176 | tf_op jit(solution)/shard_map/ppermute | solution.py:364
  98.1 2.0 %shard_map.178 = f32[64,512]{1,0:T(8,128)} custom-call(s32[4]{0:T(128)S(1)} %pad_add_fusion.place_ref, f32[512,128]{1,0:T(8,128)S(1)} %bitcast.35, f32[1,1024]{1,0:T(1,128)S(1)} %bitcast.36, bf16[128,1024]{1,0:T(8,128)(2,1)S(1)} %pad_maximum_fusion.refs_0_, bf16[128,1024]{1,0:T(8,128)(2,1)S(1)} %collective-permute-done.5.refs_1_, ...), custom_call_target="tpu_custom_call" | custom-call | flops 67108864 | bytes 2097152 | tf_op jit(solution)/shard_map/pallas_call | solution.py:291
  100.1 2.9 %collective-permute-start.10 = (bf16[4096,128]{1,0:T(8,128)(2,1)S(1)}, bf16[4096,128]{1,0:T(8,128)(2,1)}, u32[]{:S(2)}, u32[]{:S(2)}) collective-permute-start(bf16[4096,128]{1,0:T(8,128)(2,1)S(1)} %collective-permute-done.3.refs_1_), channel_id=1, source_target_pairs={{0,8},{8,0},{1,9},{9,1},{2,10},{10,2},{3,11},{11,3},{4,12},{12,4},... | collective-permute-start | bytes 3145736 | tf_op jit(solution)/shard_map/ppermute | solution.py:364
  103.0 3.4 %all-to-all-start.2 = ((f32[8,8,512]{2,1,0:T(8,128)}), f32[8,8,512]{2,1,0:T(8,128)S(1)}, u32[]{:S(2)}, u32[]{:S(2)}) async-start(f32[8,8,512]{2,1,0:T(8,128)} %bitcast.21), calls=%async_computation.2 | async-start | bytes 262144 | tf_op jit(solution)/shard_map/all_to_all | solution.py:23
  106.4 9.4 %all-to-all-done.2 = f32[8,8,512]{2,1,0:T(8,128)S(1)} async-done(((f32[8,8,512]{2,1,0:T(8,128)}), f32[8,8,512]{2,1,0:T(8,128)S(1)}, u32[]{:S(2)}, u32[]{:S(2)}) %all-to-all-start.2) | async-done | bytes 131104 | tf_op jit(solution)/shard_map/all_to_all | solution.py:23
  115.8 2.5 %collective-permute-start.11 = (bf16[4096,128]{1,0:T(8,128)(2,1)}, bf16[4096,128]{1,0:T(8,128)(2,1)}, u32[]{:S(2)}, u32[]{:S(2)}) collective-permute-start(bf16[4096,128]{1,0:T(8,128)(2,1)} %collective-permute-done.4.refs_2_), channel_id=1, source_target_pairs={{0,8},{8,0},{1,9},{9,1},{2,10},{10,2},{3,11},{11,3},{4,12},{12,4},... | collective-permute-start | bytes 3145736 | tf_op jit(solution)/shard_map/ppermute | solution.py:364
  118.2 1.9 %collective-permute-start.12 = (bf16[4096,128]{1,0:T(8,128)(2,1)}, bf16[4096,128]{1,0:T(8,128)(2,1)}, u32[]{:S(2)}, u32[]{:S(2)}) collective-permute-start(bf16[4096,128]{1,0:T(8,128)(2,1)} %collective-permute-done.8.refs_3_), channel_id=1, source_target_pairs={{0,8},{8,0},{1,9},{9,1},{2,10},{10,2},{3,11},{11,3},{4,12},{12,4},... | collective-permute-start | bytes 3145736 | tf_op jit(solution)/shard_map/ppermute | solution.py:364
  120.2 0.8 broadcast_in_dim.11
  121.0 6.7 %all-to-all-start.3 = ((bf16[64,8,512]{2,1,0:T(8,128)(2,1)}), bf16[64,8,512]{2,1,0:T(8,128)(2,1)S(1)}, u32[]{:S(2)}, u32[]{:S(2)}) async-start(bf16[64,8,512]{2,1,0:T(8,128)(2,1)} %broadcast_in_dim.11), calls=%async_computation.3 | async-start | bytes 1048576 | tf_op jit(solution)/shard_map/all_to_all | solution.py:23
  127.7 0.7 copy-done.5
  128.4 0.7 copy-done.7
  129.3 0.1 stack.59
  129.4 15.9 %all-to-all-done.3 = bf16[64,8,512]{2,1,0:T(8,128)(2,1)S(1)} async-done(((bf16[64,8,512]{2,1,0:T(8,128)(2,1)}), bf16[64,8,512]{2,1,0:T(8,128)(2,1)S(1)}, u32[]{:S(2)}, u32[]{:S(2)}) %all-to-all-start.3) | async-done | bytes 524320 | tf_op jit(solution)/shard_map/all_to_all | solution.py:23
  145.3 7.2 %shard_map.179 = f32[1,256]{1,0:T(1,128)S(1)} custom-call(s32[8]{0:T(128)S(1)} %add_multiply_fusion.start_ref, bf16[8,64,512]{2,1,0:T(8,128)(2,1)S(1)} %bitcast.34, f32[8,512]{1,0:T(8,128)S(1)} %reshape.70.gain_ref, s32[64,1]{1,0:T(8,128)S(1)} %reshape.75.target_ref, bf16[4096,128]{1,0:T(8,128)(2,1)S(1)} %copy-done.1, ...), custom_call_target="tpu_custom_call" | custom-call | flops 536870912 | bytes 9437184 | tf_op jit(solution)/shard_map/pallas_call | solution.py:342
  152.5 17.5 %all_to_all.30 = f32[64,1,256]{2,1,0:T(1,128)S(1)} all-to-all(f32[64,1,256]{2,1,0:T(1,128)S(1)} %broadcast_in_dim.13), channel_id=1, replica_groups=mesh['z'=8,'x'=4,'core'=2,'tp'=8] {'z','tp'}, dimensions={0} | all-to-all | bytes 131072 | tf_op jit(solution)/shard_map/all_to_all | solution.py:23
  170.0 0.2 reduce.3
  170.2 0.1 reshape.73
  170.6 11.2 %all_to_all.31 = f32[8,8,8]{2,1,0:T(8,128)S(1)} all-to-all(f32[8,8,8]{2,1,0:T(8,128)S(1)} %broadcast_in_dim.14), channel_id=1, replica_groups=mesh['z'=8,'x'=4,'core'=2,'tp'=8] {'x','core'}, dimensions={0} | all-to-all | bytes 4096 | tf_op jit(solution)/shard_map/all_to_all | solution.py:23
  181.8 0.1 reshape.74
  181.9 0.6 copy-done.8
  182.5 0.6 multiply_multiply_fusion
  (54 shorter events, 0.9 us)
Async XLA Ops:
  0.6 17.3 %copy-start = (bf16[128,512]{1,0:T(8,128)(2,1)S(1)}, bf16[128,512]{1,0:T(8,128)(2,1)}, u32[]{:S(2)}) copy-start(bf16[128,512]{1,0:T(8,128)(2,1)} %param.28) | copy-start | bytes 393220
  0.6 54.5 %collective-permute-start.3 = (bf16[4096,128]{1,0:T(8,128)(2,1)}, bf16[4096,128]{1,0:T(8,128)(2,1)S(1)}, u32[]{:S(2)}, u32[]{:S(2)}) collective-permute-start(bf16[4096,128]{1,0:T(8,128)(2,1)} %refs_0_.1), channel_id=1, source_target_pairs={{0,16},{16,32},{32,48},{48,0},{1,17},{17,33},{33,49},{49,1},{2,18}... | collective-permute-start | bytes 3145736 | tf_op jit(solution)/shard_map/ppermute | solution.py:364
  4.7 50.4 %collective-permute-start.4 = (bf16[4096,128]{1,0:T(8,128)(2,1)}, bf16[4096,128]{1,0:T(8,128)(2,1)}, u32[]{:S(2)}, u32[]{:S(2)}) collective-permute-start(bf16[4096,128]{1,0:T(8,128)(2,1)} %refs_0_.1), channel_id=1, source_target_pairs={{0,48},{16,0},{32,16},{48,32},{1,49},{17,1},{33,17},{49,33},{2,50}... | collective-permute-start | bytes 3145736 | tf_op jit(solution)/shard_map/ppermute | solution.py:364
  9.4 0.8 slice-start
  10.1 13.6 %collective-permute-start = (bf16[16,1408]{1,0:T(8,128)(2,1)S(1)}, bf16[16,1408]{1,0:T(8,128)(2,1)S(1)}, u32[]{:S(2)}, u32[]{:S(2)}) collective-permute-start(bf16[16,1408]{1,0:T(8,128)(2,1)S(1)} %pad_maximum_fusion.1), channel_id=1, source_target_pairs={{0,8},{8,16},{16,24},{24,32},{32,40},{40,48},{48,56},{56,64},{64,7... | collective-permute-start | bytes 135176 | tf_op jit(solution)/shard_map/ppermute | solution.py:401
  17.3 0.7 copy-start.11
  18.1 0.7 copy-start.9
  18.1 0.7 copy-start.10
  23.8 0.6 copy-start.4
  24.4 22.3 %copy-start.1 = (bf16[4096,128]{1,0:T(8,128)(2,1)S(1)}, bf16[4096,128]{1,0:T(8,128)(2,1)}, u32[]{:S(2)}) copy-start(bf16[4096,128]{1,0:T(8,128)(2,1)} %refs_0_.1) | copy-start | bytes 3145732
  27.9 23.6 %copy-start.3 = (bf16[1024,64]{0,1:T(8,128)(2,1)S(1)}, bf16[1024,64]{0,1:T(8,128)(2,1)}, u32[]{:S(2)}) copy-start(bf16[1024,64]{0,1:T(8,128)(2,1)} %param.27) | copy-start | bytes 393220
  27.9 36.6 %all-to-all-start = ((s16[64,32,128]{2,1,0:T(8,128)(2,1)}), s16[64,32,128]{2,1,0:T(8,128)(2,1)S(1)}, u32[]{:S(2)}, u32[]{:S(2)}) async-start(s16[64,32,128]{2,1,0:T(8,128)(2,1)} %shard_map.176), calls=%async_computation | async-start | bytes 1048576 | tf_op jit(solution)/shard_map/all_to_all | solution.py:23
  46.7 45.2 %collective-permute-start.8 = (bf16[4096,128]{1,0:T(8,128)(2,1)S(1)}, bf16[4096,128]{1,0:T(8,128)(2,1)}, u32[]{:S(2)}, u32[]{:S(2)}) collective-permute-start(bf16[4096,128]{1,0:T(8,128)(2,1)S(1)} %copy-done.1), channel_id=1, source_target_pairs={{0,32},{16,48},{32,0},{48,16},{1,33},{17,49},{33,1},{49,17},{2,34}... | collective-permute-start | bytes 3145736 | tf_op jit(solution)/shard_map/ppermute | solution.py:364
  51.5 3.5 %collective-permute-start.2 = (bf16[64,1024]{1,0:T(8,128)(2,1)S(1)}, bf16[64,1024]{1,0:T(8,128)(2,1)S(1)}, u32[]{:S(2)}, u32[]{:S(2)}) collective-permute-start(bf16[64,1024]{1,0:T(8,128)(2,1)S(1)} %bitcast.40), channel_id=1, source_target_pairs={{0,8},{8,0},{1,9},{9,1},{2,10},{10,2},{3,11},{11,3},{4,12},{12,4},... | collective-permute-start | bytes 393224 | tf_op jit(solution)/shard_map/ppermute | solution.py:364
  54.1 1.0 collective-permute-start.1
  66.8 31.3 %all-to-all-start.1 = ((f32[64,8,128]{2,1,0:T(8,128)}), f32[64,8,128]{2,1,0:T(8,128)S(1)}, u32[]{:S(2)}, u32[]{:S(2)}) async-start(f32[64,8,128]{2,1,0:T(8,128)} %shard_map.177), calls=%async_computation.1 | async-start | bytes 524288 | tf_op jit(solution)/shard_map/all_to_all | solution.py:23
  78.5 13.4 %collective-permute-start.5 = (bf16[128,1024]{1,0:T(8,128)(2,1)S(1)}, bf16[128,1024]{1,0:T(8,128)(2,1)S(1)}, u32[]{:S(2)}, u32[]{:S(2)}) collective-permute-start(bf16[128,1024]{1,0:T(8,128)(2,1)S(1)} %pad_maximum_fusion.refs_0_), channel_id=1, source_target_pairs={{0,16},{16,32},{32,48},{48,0},{1,17},{17,33},{33,49},{49,1},{2,18}... | collective-permute-start | bytes 786440 | tf_op jit(solution)/shard_map/ppermute | solution.py:364
  81.9 10.3 %collective-permute-start.6 = (bf16[128,1024]{1,0:T(8,128)(2,1)S(1)}, bf16[128,1024]{1,0:T(8,128)(2,1)S(1)}, u32[]{:S(2)}, u32[]{:S(2)}) collective-permute-start(bf16[128,1024]{1,0:T(8,128)(2,1)S(1)} %pad_maximum_fusion.refs_0_), channel_id=1, source_target_pairs={{0,48},{16,0},{32,16},{48,32},{1,49},{17,1},{33,17},{49,33},{2,50}... | collective-permute-start | bytes 786440 | tf_op jit(solution)/shard_map/ppermute | solution.py:364
  85.1 13.1 %collective-permute-start.7 = (bf16[128,1024]{1,0:T(8,128)(2,1)S(1)}, bf16[128,1024]{1,0:T(8,128)(2,1)S(1)}, u32[]{:S(2)}, u32[]{:S(2)}) collective-permute-start(bf16[128,1024]{1,0:T(8,128)(2,1)S(1)} %pad_maximum_fusion.refs_0_), channel_id=1, source_target_pairs={{0,32},{16,48},{32,0},{48,16},{1,33},{17,49},{33,1},{49,17},{2,34}... | collective-permute-start | bytes 786440 | tf_op jit(solution)/shard_map/ppermute | solution.py:364
  88.7 17.7 %collective-permute-start.9 = (bf16[4096,128]{1,0:T(8,128)(2,1)S(1)}, bf16[4096,128]{1,0:T(8,128)(2,1)}, u32[]{:S(2)}, u32[]{:S(2)}) collective-permute-start(bf16[4096,128]{1,0:T(8,128)(2,1)S(1)} %copy-done.1), channel_id=1, source_target_pairs={{0,8},{8,0},{1,9},{9,1},{2,10},{10,2},{3,11},{11,3},{4,12},{12,4},... | collective-permute-start | bytes 3145736 | tf_op jit(solution)/shard_map/ppermute | solution.py:364
  91.8 6.3 %copy-start.2 = (f32[1024]{0:T(1024)S(1)}, f32[1024]{0:T(1024)}, u32[]{:S(2)}) copy-start(f32[1024]{0:T(1024)} %param.26) | copy-start | bytes 12292
  100.1 15.7 %collective-permute-start.10 = (bf16[4096,128]{1,0:T(8,128)(2,1)S(1)}, bf16[4096,128]{1,0:T(8,128)(2,1)}, u32[]{:S(2)}, u32[]{:S(2)}) collective-permute-start(bf16[4096,128]{1,0:T(8,128)(2,1)S(1)} %collective-permute-done.3.refs_1_), channel_id=1, source_target_pairs={{0,8},{8,0},{1,9},{9,1},{2,10},{10,2},{3,11},{11,3},{4,12},{12,4},... | collective-permute-start | bytes 3145736 | tf_op jit(solution)/shard_map/ppermute | solution.py:364
  103.0 12.8 %all-to-all-start.2 = ((f32[8,8,512]{2,1,0:T(8,128)}), f32[8,8,512]{2,1,0:T(8,128)S(1)}, u32[]{:S(2)}, u32[]{:S(2)}) async-start(f32[8,8,512]{2,1,0:T(8,128)} %bitcast.21), calls=%async_computation.2 | async-start | bytes 262144 | tf_op jit(solution)/shard_map/all_to_all | solution.py:23
  115.8 29.5 %collective-permute-start.11 = (bf16[4096,128]{1,0:T(8,128)(2,1)}, bf16[4096,128]{1,0:T(8,128)(2,1)}, u32[]{:S(2)}, u32[]{:S(2)}) collective-permute-start(bf16[4096,128]{1,0:T(8,128)(2,1)} %collective-permute-done.4.refs_2_), channel_id=1, source_target_pairs={{0,8},{8,0},{1,9},{9,1},{2,10},{10,2},{3,11},{11,3},{4,12},{12,4},... | collective-permute-start | bytes 3145736 | tf_op jit(solution)/shard_map/ppermute | solution.py:364
  118.2 27.0 %collective-permute-start.12 = (bf16[4096,128]{1,0:T(8,128)(2,1)}, bf16[4096,128]{1,0:T(8,128)(2,1)}, u32[]{:S(2)}, u32[]{:S(2)}) collective-permute-start(bf16[4096,128]{1,0:T(8,128)(2,1)} %collective-permute-done.8.refs_3_), channel_id=1, source_target_pairs={{0,8},{8,0},{1,9},{9,1},{2,10},{10,2},{3,11},{11,3},{4,12},{12,4},... | collective-permute-start | bytes 3145736 | tf_op jit(solution)/shard_map/ppermute | solution.py:364
  121.0 24.3 %all-to-all-start.3 = ((bf16[64,8,512]{2,1,0:T(8,128)(2,1)}), bf16[64,8,512]{2,1,0:T(8,128)(2,1)S(1)}, u32[]{:S(2)}, u32[]{:S(2)}) async-start(bf16[64,8,512]{2,1,0:T(8,128)(2,1)} %broadcast_in_dim.11), calls=%async_computation.3 | async-start | bytes 1048576 | tf_op jit(solution)/shard_map/all_to_all | solution.py:23
  127.7 0.7 copy-start.5
  128.4 0.7 copy-start.7
  181.8 0.7 copy-start.8
  182.5 0.6 copy-start.6

commit v4 on v2

--- a/solution.py
+++ b/solution.py
@@ -58,24 +58,63 @@
     return jnp.where(high < -32767.5, blocked, high / 2048.0 + low * 2.0**-26)
 
 
+def tail_kernel(stream_ref, state_ref, reset_ref, out_ref):
+    channels, states = stream_ref.shape[1], state_ref.shape[2]
+    out_ref[:, :channels] = stream_ref[...]
+    out_ref[:, channels : channels + states] = state_ref[0]
+    out_ref[:, channels + states : channels + 2 * states] = state_ref[1]
+    flags = jnp.broadcast_to(reset_ref[...].astype(f32), (out_ref.shape[0], reset_ref.shape[1]))
+    out_ref[:, channels + 2 * states :] = flags.astype(bf16)
+
+
+def last_rows(stream, states, resets, margin):
+    rows, channels = stream.shape
+    at = rows // margin - 1
+    width = states.shape[2]
+    return pl.pallas_call(
+        tail_kernel,
+        grid=(1,),
+        out_shape=jax.ShapeDtypeStruct((margin, channels + 2 * width + rows), bf16),
+        in_specs=[
+            pl.BlockSpec((margin, channels), lambda k: (at, 0)),
+            pl.BlockSpec((2, margin, width), lambda k: (0, at, 0)),
+            pl.BlockSpec((1, rows), lambda k: (0, 0)),
+        ],
+        out_specs=pl.BlockSpec((margin, channels + 2 * width + rows), lambda k: (0, 0)),
+        compiler_params=pltpu.CompilerParams(vmem_limit_bytes=58 * 2**20),
+    )(stream, states, resets)
+
+
 def local_kernel(
-    place_ref, stream_ref, state_ref, tail_ref, gate_ref, step_ref, reset_ref, head_ref, taps_ref, state_taps_ref, out_ref, pad_ref
+    base_ref,
+    scored_ref,
+    rate_ref,
+    skip_ref,
+    stream_ref,
+    state_ref,
+    tail_ref,
+    gate_ref,
+    step_ref,
+    reset_ref,
+    taps_ref,
+    state_taps_ref,
+    out_ref,
+    pad_ref,
 ):
     rows, channels = stream_ref.shape
     states = state_ref.shape[2]
     heads = step_ref.shape[0]
     margin = tail_ref.shape[0]
     width = tail_ref.shape[1] - 128
-    count = place_ref.shape[0]
+    count = scored_ref.shape[0]
     lane = lax.broadcasted_iota(jnp.int32, (8, 128), 1)
     line = lax.broadcasted_iota(jnp.int32, (8, 128), 0)
 
     flag = jnp.broadcast_to(reset_ref[...].astype(f32), (8, rows))
     free = 1.0 - flag
-    earlier = 1.0 - tail_ref[:, width:].astype(f32)
-    one, two = earlier[margin - 1 :], earlier[margin - 2 : margin - 1]
-    second = free * jnp.where(lane == 0, one, pltpu.roll(free, 1, 1))
-    third = second * jnp.where(lane == 0, two, jnp.where(lane == 1, one, pltpu.roll(free, 2, 1)))
+    earlier = 1.0 - tail_ref[:, width:].astype(f32)[:8]
+    second = free * pltpu.roll(jnp.where(lane == rows - 1, earlier, free), 1, 1)
+    third = second * pltpu.roll(jnp.where(lane >= rows - 2, earlier, free), 2, 1)
     turned = jnp.where(line == 0, free, jnp.where(line == 1, second, third)).T
     keeping = [jnp.broadcast_to(turned[:, k : k + 1], (rows, 128)) for k in range(3)]
 
@@ -90,25 +129,34 @@
     writes = filtered(state_ref[0], tail_ref[:, channels : channels + states], state_taps_ref[0])
     reads = filtered(state_ref[1], tail_ref[:, channels + states : width], state_taps_ref[1])
 
-    chosen = lane == place_ref[...]
+    place = jnp.zeros((8, 128), jnp.int32)
+    for k in range(count):
+        place = jnp.where(line == k, scored_ref[k] - base_ref[0], place)
+    rate = jnp.zeros((heads, rows), f32)
+    skip = jnp.zeros((heads, rows), f32)
+    head = lax.broadcasted_iota(jnp.int32, (heads, rows), 0)
+    for k in range(heads):
+        rate = jnp.where(head == k, rate_ref[k], rate)
+        skip = jnp.where(head == k, skip_ref[k], skip)
+    chosen = lane == place
     pick = chosen.astype(bf16)
     rows_reads = jnp.dot(pick, reads, preferred_element_type=f32)
     first = lax.broadcasted_iota(jnp.int32, (rows, rows), 0)
     upto = (first <= lax.broadcasted_iota(jnp.int32, (rows, rows), 1)).astype(bf16)
     step = step_ref[...]
-    drift = jnp.concatenate(split(-head_ref[:, 0:1] * step, 3), axis=0)
+    drift = jnp.concatenate(split(-rate * step, 3), axis=0)
     summed = jnp.dot(drift, upto, preferred_element_type=f32)
     cumulated = summed[:heads] + summed[heads : 2 * heads] + summed[2 * heads :]
     segment = jnp.dot(flag.astype(bf16), upto, preferred_element_type=f32)
     rows_segment = jnp.sum(jnp.where(chosen, segment, 0.0), axis=1, keepdims=True)
     rows_log = jnp.sum(jnp.where(chosen[None], cumulated[:, None, :], 0.0), axis=2, keepdims=True)
-    causal = (lane <= place_ref[...]) & (segment == rows_segment)
+    causal = (lane <= place) & (segment == rows_segment)
     scores = lax.dot_general(
         rows_reads.astype(bf16), writes, (((1,), (1,)), ((), ())), preferred_element_type=f32
     )
     gaps = jnp.where(causal[None], rows_log - cumulated[:, None, :], 0.0)
     mixing = jnp.where(causal[None], jnp.exp(gaps), 0.0) * scores[None] * step[:, None, :]
-    mixing = mixing + jnp.where(chosen[None], head_ref[:, 1:2][:, :, None], 0.0)
+    mixing = mixing + jnp.where(chosen[None], skip[:, None, :], 0.0)
     mixing = split(mixing.reshape(heads * count, rows), 3)
 
     end_segment = segment[0:1, rows - 1 :]
@@ -161,17 +209,17 @@
             out_ref[8 * b : 8 * b + 8, at : at + 16, :] = part.astype(jnp.int16)
 
 
-def local_part(place, stream, states, tail, gate, step, resets, by_head, taps, state_taps):
+def local_part(base, scored, rate, skip, stream, states, tail, gate, step, resets, taps, state_taps):
     channels = stream.shape[1]
     return pl.pallas_call(
         local_kernel,
         out_shape=jax.ShapeDtypeStruct((channels // 16, 32, 128), jnp.int16),
-        in_specs=[whole] * 10,
+        in_specs=[pl.BlockSpec(memory_space=pltpu.SMEM)] * 4 + [whole] * 8,
         out_specs=whole,
         scratch_shapes=[pltpu.VMEM((tail.shape[0] + stream.shape[0], 128), f32)],
         compiler_params=pltpu.CompilerParams(vmem_limit_bytes=58 * 2**20),
         cost_estimate=pl.CostEstimate(flops=1 << 27, bytes_accessed=2 << 20, transcendentals=1 << 18),
-    )(place, stream, states, tail, gate, step, resets, by_head, taps, state_taps)
+    )(base, scored, rate, skip, stream, states, tail, gate, step, resets, taps, state_taps)
 
 
 def carry_kernel(came_ref, out_ref, side_ref, met_ref, weight_ref, *, planes, subs):
@@ -293,62 +341,67 @@
     )(gated, gain, weight)
 
 
-def logits_kernel(start_ref, chosen_ref, gain_ref, target_ref, weight_ref, out_ref, total_ref, inverse_ref, *, steps, stride):
-    step = pl.program_id(0)
+def spread_kernel(partial_ref, residual_ref, out_ref):
+    total = residual_ref[...].astype(f32)
+    summed = partial_ref[0]
+    for k in range(1, partial_ref.shape[0]):
+        summed = summed + partial_ref[k]
+    out_ref[...] = jnp.broadcast_to((summed + total).astype(bf16)[None], out_ref.shape)
+
+
+def spread(partial, residual, copies):
+    return pl.pallas_call(
+        spread_kernel,
+        out_shape=jax.ShapeDtypeStruct((copies, *residual.shape), bf16),
+        in_specs=[whole] * 2,
+        out_specs=whole,
+        compiler_params=pltpu.CompilerParams(vmem_limit_bytes=8 * 2**20),
+        cost_estimate=pl.CostEstimate(flops=1 << 16, bytes_accessed=1 << 20, transcendentals=0),
+    )(partial, residual)
+
+
+def logits_kernel(start_ref, chosen_ref, gain_ref, target_ref, from_ref, out_ref, weight_ref, sems, *, stride):
     slabs, group, width = chosen_ref.shape
     subs, _, columns = weight_ref.shape
-
-    @pl.when(step == 0)
-    def _():
-        squares = jnp.zeros((group, 1), f32)
-        for k in range(slabs):
-            slab = chosen_ref[k].astype(f32)
-            squares = squares + jnp.sum(slab * slab, axis=1, keepdims=True)
-        inverse_ref[...] = jnp.broadcast_to(lax.rsqrt(squares / (slabs * width) + epsilon), inverse_ref.shape)
-        total_ref[...] = jnp.zeros_like(total_ref)
-
-    features = chosen_ref[step].astype(f32) * inverse_ref[:, :1] * gain_ref[pl.ds(step, 1), :]
-    weight = jnp.concatenate([weight_ref[k] for k in range(subs)], axis=1)
-    total_ref[...] += jnp.dot(features.astype(bf16), weight, preferred_element_type=f32)
-
-    @pl.when(step == steps - 1)
-    def _():
-        logits = total_ref[...]
-        top = jnp.max(logits, axis=1, keepdims=True)
-        summed = jnp.sum(jnp.exp(logits - top), axis=1, keepdims=True)
-        picked = jnp.zeros((group, 1), f32)
-        lane = lax.broadcasted_iota(jnp.int32, (group, columns), 1)
-        for k in range(subs):
-            own = lane + (start_ref[0] + k * stride) == target_ref[...]
-            picked = picked + jnp.sum(
-                jnp.where(own, logits[:, k * columns : (k + 1) * columns], 0.0), axis=1, keepdims=True
-            )
-        place = lax.broadcasted_iota(jnp.int32, (group, 128), 1)
-        found = jnp.where(place == 0, top, jnp.where(place == 1, summed, picked)).T
-        pair = jnp.concatenate([found[0:1], found[1:2], found[2:3], found[2:3]], axis=1)
-        out_ref[...] = pair
+    fetches = []
+    for k in range(slabs):
+        block = (slice(None), slice(k * width, (k + 1) * width), slice(None))
+        fetches.append(pltpu.make_async_copy(from_ref.at[block], weight_ref.at[block], sems.at[k]))
+        fetches[k].start()
+    squares = jnp.zeros((group, 1), f32)
+    for k in range(slabs):
+        slab = chosen_ref[k].astype(f32)
+        squares = squares + jnp.sum(slab * slab, axis=1, keepdims=True)
+    inverse = lax.rsqrt(squares / (slabs * width) + epsilon)
+    logits = jnp.zeros((group, subs * columns), f32)
+    for k in range(slabs):
+        features = chosen_ref[k].astype(f32) * inverse * gain_ref[k : k + 1, :]
+        fetches[k].wait()
+        weight = jnp.concatenate([weight_ref[j, k * width : (k + 1) * width, :] for j in range(subs)], axis=1)
+        logits = logits + jnp.dot(features.astype(bf16), weight, preferred_element_type=f32)
+    top = jnp.max(logits, axis=1, keepdims=True)
+    summed = jnp.sum(jnp.exp(logits - top), axis=1, keepdims=True)
+    picked = jnp.zeros((group, 1), f32)
+    lane = lax.broadcasted_iota(jnp.int32, (group, columns), 1)
+    for k in range(subs):
+        own = lane + (start_ref[0] + k * stride) == target_ref[...]
+        picked = picked + jnp.sum(
+            jnp.where(own, logits[:, k * columns : (k + 1) * columns], 0.0), axis=1, keepdims=True
+        )
+    place = lax.broadcasted_iota(jnp.int32, (group, 128), 1)
+    found = jnp.where(place == 0, top, jnp.where(place == 1, summed, picked)).T
+    out_ref[...] = jnp.concatenate([found[0:1], found[1:2], found[2:3], found[2:3]], axis=1)
 
 
 def score(start, chosen, gain, target, weight, stride):
     slabs, group, width = chosen.shape
-    subs, _, columns = weight.shape
-    fixed = lambda *shape: pl.BlockSpec(shape, lambda k: (0,) * len(shape))
-    return pl.pallas_call(
-        functools.partial(logits_kernel, steps=slabs, stride=stride),
-        grid=(slabs,),
+    return pl.pallas_call(
+        functools.partial(logits_kernel, stride=stride),
         out_shape=jax.ShapeDtypeStruct((1, 4 * group), f32),
-        in_specs=[
-            pl.BlockSpec(memory_space=pltpu.SMEM),
-            fixed(slabs, group, width),
-            fixed(slabs, width),
-            fixed(group, 1),
-            pl.BlockSpec((subs, width, columns), lambda k: (0, k, 0)),
-        ],
-        out_specs=fixed(1, 4 * group),
-        scratch_shapes=[pltpu.VMEM((group, subs * columns), f32), pltpu.VMEM((group, 128), f32)],
-        compiler_params=pltpu.CompilerParams(
-            dimension_semantics=("arbitrary",), vmem_limit_bytes=58 * 2**20
-        ),
+        in_specs=[pl.BlockSpec(memory_space=pltpu.SMEM), whole, whole, whole, pl.BlockSpec(memory_space=pl.ANY)],
+        out_specs=whole,
+        scratch_shapes=[pltpu.VMEM(weight.shape, bf16), pltpu.SemaphoreType.DMA((slabs,))],
+        compiler_params=pltpu.CompilerParams(vmem_limit_bytes=54 * 2**20),
         cost_estimate=pl.CostEstimate(flops=2 * 64 * 4096 * 1024, bytes_accessed=9 << 20, transcendentals=0),
     )(start, chosen, gain, target, weight)
 
@@ -381,10 +434,9 @@
     total = chunks * count
     local_rows = scored - lax.axis_index(CTX) * rows
 
-    margin = 16
-    flags = jnp.broadcast_to(resets[rows - margin :, None].astype(bf16), (margin, 128))
-    tail = [inner_input[rows - margin :], state_inputs[0, rows - margin :], state_inputs[1, rows - margin :], flags]
-    tail = lax.ppermute(jnp.concatenate(tail, axis=1), CTX, [(i, i + 1) for i in range(chunks - 1)])
+    flags = resets.reshape(1, rows)
+    tail = last_rows(inner_input, state_inputs, flags, 16)
+    tail = lax.ppermute(tail, CTX, [(i, i + 1) for i in range(chunks - 1)])
 
     out_full = lax.all_gather(out_weight.T, SUB, axis=0, tiled=True)
     head_full = lax.all_gather(head_weight, SUB, axis=0)
@@ -392,9 +444,9 @@
     rows_residual = jnp.dot(pick, residual, preferred_element_type=f32).astype(bf16)
     own = lax.dynamic_index_in_dim(targets.reshape(planes, subs, count), lax.axis_index(SUB), 1, False).reshape(group, 1)
 
-    by_head = jnp.stack([decay_rate, skip_gain], axis=1)
+    base = (lax.axis_index(CTX) * rows).reshape(1)
     message = local_part(
-        local_rows.reshape(-1, 1), inner_input, state_inputs, tail, gate_input, step_size, resets.reshape(1, rows), by_head, conv_inner, conv_state
+        base, scored, decay_rate, skip_gain, inner_input, state_inputs, tail, gate_input, step_size, flags, conv_inner, conv_state
     )
     message, rows_residual = lax.optimization_barrier((message, rows_residual))
     came = exchange(message, CTX)
@@ -406,9 +458,7 @@
     gated = exchange(gated, CTX).reshape(channels // 2, 2 * group)
 
     partial = exchange(project(gated, norm_gain.reshape(1, -1), out_full).reshape(planes, count, -1), "tp")
-    chosen = (jnp.sum(partial, axis=0) + rows_residual.astype(f32)).astype(bf16)
-
-    chosen = to_everyone(chosen, PLANE).reshape(planes, group, -1)
+    chosen = exchange(spread(partial, rows_residual, chunks), PLANE).reshape(planes, group, -1)
     columns = head_weight.shape[1]
     ways = lax.axis_size("tp")
     start = (lax.axis_index("z") * subs * ways + lax.axis_index("tp")) * columns

time: 161 us -> 158 us (0.981)
  local copies, waits for them, and re-layouts: 9.71 us -> 5.87 us
  waiting for transfers between devices: 33.7 us -> 36.3 us
  other arithmetic: 3.52 us -> 1.5 us
    ppermute x1, waiting for transfers between devices: 0.8 us -> 3.71 us  [body(): tail = lax.ppermute(tail, CTX, [(i, i + 1) for i in range(chunks - 1)])]
    pallas_call x1 -> x3, Pallas kernels: 8.2 us -> 7.97 us  [the longest x1 5.71 us: score(): pl.pallas_call(functools.partial(logits_kernel, stride=stride), out_shape...]
  transfers between devices with their start and end apart: 6 -> 6, of which waited for: 3 -> 3; matrix products, arithmetic and copies ran while one was open for 5% -> 1% of each run, Pallas kernels for 4% -> 5%
where the time goes in v4:
time: 158 us; the launch traced here: 157 us
  blocking collectives  63.4 us (40%)
  waiting for transfers between devices  36.3 us (23%)
  starting transfers between devices  22 us (14%)
  between operations  14.2 us (9%)
  Pallas kernels  13.7 us (9%)
  local copies, waits for them, and re-layouts  5.87 us (4%)
    all_to_all x4, blocking collectives, exchange(): return lax.all_to_all(blocks, axes, 0, 0, tiled=True)  63.4 us
    all_to_all x2, waiting for transfers between devices, exchange(): return lax.all_to_all(blocks, axes, 0, 0, tiled=True)  31.2 us
    all_to_all x2, starting transfers between devices, exchange(): return lax.all_to_all(blocks, axes, 0, 0, tiled=True)  16.8 us
    pallas_call x1, Pallas kernels, score(): pl.pallas_call(functools.partial(logits_kernel, stride=stride), out_shape...  5.71 us
    ppermute x1, starting transfers between devices, body(): tail = lax.ppermute(tail, CTX, [(i, i + 1) for i in range(chunks - 1)])  4.5 us
    ppermute x1, waiting for transfers between devices, body(): tail = lax.ppermute(tail, CTX, [(i, i + 1) for i in range(chunks - 1)])  3.71 us
    pallas_call x1, Pallas kernels, local_part(): pl.pallas_call(local_kernel, out_shape=jax.ShapeDtypeStruct((channels //...  3.46 us
    unnamed x18, local copies, waits for them, and re-layouts  3.41 us
  transfers between devices with their start and end apart: 6, of which 3 were waited for; matrix products, arithmetic and copies ran while one was open for 1% of the time, Pallas kernels for 5%

profile of v4, /device:TPU:1, one launch (start us, length us, event | category | flops | bytes accessed | tf_op | source)
XLA Modules:
  0.0 157.2 jit_solution(17130365287046072106)
XLA Ops:
  7.2 0.0 copy-start
  7.2 0.0 copy-start.7
  7.2 0.0 copy-start.5
  7.2 0.0 all-gather.4.cloned.1.call-start
  7.2 0.7 all-gather.4.cloned.1.call-update
  7.9 0.0 all-gather.6.cloned.1.call-start
  8.0 0.7 all-gather.6.cloned.1.call-update
  8.7 1.4 shard_map.176
  10.1 4.5 %collective-permute-start = (bf16[16,1408]{1,0:T(8,128)(2,1)}, bf16[16,1408]{1,0:T(8,128)(2,1)S(1)}, u32[]{:S(2)}, u32[]{:S(2)}) collective-permute-start(bf16[16,1408]{1,0:T(8,128)(2,1)} %shard_map.176), channel_id=1, source_target_pairs={{0,8},{8,16},{16,24},{24,32},{32,40},{40,48},{48,56},{56,64},{64,7... | collective-permute-start | bytes 135176 | tf_op jit(solution)/shard_map/ppermute | solution.py:439
  14.6 0.7 broadcast_subtract_fusion
  15.2 0.0 copy-done
  15.2 0.2 convolution_convert_fusion
  15.4 3.7 %collective-permute-done.tail_ref = bf16[16,1408]{1,0:T(8,128)(2,1)S(1)} collective-permute-done((bf16[16,1408]{1,0:T(8,128)(2,1)}, bf16[16,1408]{1,0:T(8,128)(2,1)S(1)}, u32[]{:S(2)}, u32[]{:S(2)}) %collective-permute-start) | collective-permute-done | bytes 45088 | tf_op jit(solution)/shard_map/ppermute | solution.py:439
  19.1 0.6 copy-done.4
  19.8 3.5 %shard_map.177 = s16[64,32,128]{2,1,0:T(8,128)(2,1)} custom-call(s32[1]{0:T(128)} %bitcast.1.base_ref, s32[8]{0:T(128)} %scored_ref.1, f32[16]{0:T(128)} %rate_ref.1, f32[16]{0:T(128)} %skip_ref.1, bf16[128,1024]{1,0:T(8,128)(2,1)} %stream_ref.3, bf16[2,128,128]{2,1,0:T(8,128)(2,1)} %state_ref.3, bf16[16,1408]{1,0:T(8,128)(2,1)} %copy-done.4, ...), custom_call_target="tpu_custom_call" | custom-call | flops 134217728 | bytes 2097152 | tf_op jit(solution)/shard_map/pallas_call | solution.py:214
  23.2 12.2 %all-to-all-start = ((s16[64,32,128]{2,1,0:T(8,128)(2,1)}), s16[64,32,128]{2,1,0:T(8,128)(2,1)S(1)}, u32[]{:S(2)}, u32[]{:S(2)}) async-start(s16[64,32,128]{2,1,0:T(8,128)(2,1)} %shard_map.177), calls=%async_computation | async-start | bytes 1048576 | tf_op jit(solution)/shard_map/all_to_all | solution.py:23
  35.4 0.7 collective-permute-start.1
  36.1 0.0 collective-permute-done.1.residual_ref
  36.1 17.0 %all-to-all-done.came_ref = s16[64,32,128]{2,1,0:T(8,128)(2,1)S(1)} async-done(((s16[64,32,128]{2,1,0:T(8,128)(2,1)}), s16[64,32,128]{2,1,0:T(8,128)(2,1)S(1)}, u32[]{:S(2)}, u32[]{:S(2)}) %all-to-all-start) | async-done | bytes 524320 | tf_op jit(solution)/shard_map/all_to_all | solution.py:23
  53.1 1.5 shard_map.178
  54.6 0.0 all-gather.4.cloned.1.call-done.weight_ref
  54.7 19.9 %all_to_all.30 = f32[64,8,128]{2,1,0:T(8,128)S(1)} all-to-all(f32[64,8,128]{2,1,0:T(8,128)S(1)} %shard_map.178), channel_id=1, replica_groups=mesh['z'=8,'x'=4,'core'=2,'tp'=8] {'z','x','core'}, dimensions={0} | all-to-all | bytes 524288 | tf_op jit(solution)/shard_map/all_to_all | solution.py:23
  74.5 1.2 copy-done.1
  75.8 0.7 copy-done.2
  76.5 0.7 shard_map.179
  77.2 14.0 %all_to_all.31.partial_ref = f32[8,8,512]{2,1,0:T(8,128)S(1)} all-to-all(f32[8,8,512]{2,1,0:T(8,128)S(1)} %bitcast.18), channel_id=1, replica_groups=mesh['z'=8,'x'=4,'core'=2,'tp'=8] {'tp'}, dimensions={0} | all-to-all | bytes 262144 | tf_op jit(solution)/shard_map/all_to_all | solution.py:23
  91.2 0.9 shard_map.180
  92.1 4.6 %all-to-all-start.3 = ((bf16[64,8,512]{2,1,0:T(8,128)(2,1)}), bf16[64,8,512]{2,1,0:T(8,128)(2,1)S(1)}, u32[]{:S(2)}, u32[]{:S(2)}) async-start(bf16[64,8,512]{2,1,0:T(8,128)(2,1)} %shard_map.180), calls=%async_computation.3 | async-start | bytes 1048576 | tf_op jit(solution)/shard_map/all_to_all | solution.py:23
  96.7 0.0 copy-done.7
  96.7 0.1 reshape.72
  96.9 0.7 reshape.77.target_ref
  97.5 0.0 copy-done.5
  97.5 0.6 reshape.71.gain_ref
  98.1 14.2 %all-to-all-done.3 = bf16[64,8,512]{2,1,0:T(8,128)(2,1)S(1)} async-done(((bf16[64,8,512]{2,1,0:T(8,128)(2,1)}), bf16[64,8,512]{2,1,0:T(8,128)(2,1)S(1)}, u32[]{:S(2)}, u32[]{:S(2)}) %all-to-all-start.3) | async-done | bytes 524320 | tf_op jit(solution)/shard_map/all_to_all | solution.py:23
  112.3 0.8 copy-done.3
  113.1 5.7 %shard_map.181 = f32[1,256]{1,0:T(1,128)} custom-call(s32[1]{0:T(128)} %bitcast.start_ref, bf16[8,64,512]{2,1,0:T(8,128)(2,1)} %bitcast.21, f32[8,512]{1,0:T(8,128)} %reshape.71.gain_ref, s32[64,1]{1,0:T(8,128)} %reshape.77.target_ref, bf16[8,4096,128]{2,1,0:T(8,128)(2,1)} %bitcast.20), custom_call_target="tpu_custom_call" | custom-call | flops 536870912 | bytes 9437184 | tf_op jit(solution)/shard_map/pallas_call | solution.py:398
  118.8 0.7 broadcast_in_dim.7
  119.6 18.6 %all_to_all.32 = f32[64,1,256]{2,1,0:T(1,128)S(1)} all-to-all(f32[64,1,256]{2,1,0:T(1,128)S(1)} %broadcast_in_dim.7), channel_id=1, replica_groups=mesh['z'=8,'x'=4,'core'=2,'tp'=8] {'z','tp'}, dimensions={0} | all-to-all | bytes 131072 | tf_op jit(solution)/shard_map/all_to_all | solution.py:23
  138.2 0.2 reduce.3
  138.3 0.1 reshape.74
  138.4 0.1 fusion.1
  138.6 0.1 sub.41
  138.7 10.9 %all_to_all.33 = f32[8,8,8]{2,1,0:T(8,128)S(1)} all-to-all(f32[8,8,8]{2,1,0:T(8,128)S(1)} %broadcast_in_dim.8), channel_id=1, replica_groups=mesh['z'=8,'x'=4,'core'=2,'tp'=8] {'x','core'}, dimensions={0} | all-to-all | bytes 4096 | tf_op jit(solution)/shard_map/all_to_all | solution.py:23
  149.6 0.1 reshape.75
  149.7 0.0 copy-done.8
  149.7 0.0 copy-start.6
  149.7 0.6 multiply_multiply_fusion
  150.3 0.0 copy-done.6
  (13 shorter events, 0.1 us)
Async XLA Ops:
  7.2 8.1 %copy-start = (bf16[128,512]{1,0:T(8,128)(2,1)S(1)}, bf16[128,512]{1,0:T(8,128)(2,1)}, u32[]{:S(2)}) copy-start(bf16[128,512]{1,0:T(8,128)(2,1)} %param.28) | copy-start | bytes 393220
  7.2 89.5 %copy-start.7 = (s32[512]{0:T(512)S(1)}, s32[512]{0:T(512)}, u32[]{:S(2)}) copy-start(s32[512]{0:T(512)} %param.32) | copy-start | bytes 6148
  7.2 90.3 %copy-start.5 = (f32[4096]{0:T(1024)S(1)}, f32[4096]{0:T(1024)}, u32[]{:S(2)}) copy-start(f32[4096]{0:T(1024)} %param.29) | copy-start | bytes 49156
  7.2 47.5 %all-gather.4.cloned.1.call-start = ((), (), s32[]{:S(2)}) async-start(), calls=%async_computation.6 | async-start | bytes 1179648 | tf_op jit(solution)/shard_map/all_gather | solution.py:441
  7.9 104.4 %all-gather.6.cloned.1.call-start = ((), (), s32[]{:S(2)}) async-start(), calls=%async_computation.7 | async-start | bytes 9437184 | tf_op jit(solution)/shard_map/all_gather | solution.py:442
  10.1 9.1 %collective-permute-start = (bf16[16,1408]{1,0:T(8,128)(2,1)}, bf16[16,1408]{1,0:T(8,128)(2,1)S(1)}, u32[]{:S(2)}, u32[]{:S(2)}) collective-permute-start(bf16[16,1408]{1,0:T(8,128)(2,1)} %shard_map.176), channel_id=1, source_target_pairs={{0,8},{8,16},{16,24},{24,32},{32,40},{40,48},{48,56},{56,64},{64,7... | collective-permute-start | bytes 135176 | tf_op jit(solution)/shard_map/ppermute | solution.py:439
  19.1 0.6 copy-start.4
  19.8 130.0 %copy-start.8 = (f32[512]{0:T(512)S(1)}, f32[512]{0:T(512)}, u32[]{:S(2)}) copy-start(f32[512]{0:T(512)} %param.33) | copy-start | bytes 6148
  23.2 29.9 %all-to-all-start = ((s16[64,32,128]{2,1,0:T(8,128)(2,1)}), s16[64,32,128]{2,1,0:T(8,128)(2,1)S(1)}, u32[]{:S(2)}, u32[]{:S(2)}) async-start(s16[64,32,128]{2,1,0:T(8,128)(2,1)} %shard_map.177), calls=%async_computation | async-start | bytes 1048576 | tf_op jit(solution)/shard_map/all_to_all | solution.py:23
  35.4 0.7 collective-permute-start.1
  74.5 1.2 copy-start.1
  75.8 0.7 copy-start.2
  92.1 20.2 %all-to-all-start.3 = ((bf16[64,8,512]{2,1,0:T(8,128)(2,1)}), bf16[64,8,512]{2,1,0:T(8,128)(2,1)S(1)}, u32[]{:S(2)}, u32[]{:S(2)}) async-start(bf16[64,8,512]{2,1,0:T(8,128)(2,1)} %shard_map.180), calls=%async_computation.3 | async-start | bytes 1048576 | tf_op jit(solution)/shard_map/all_to_all | solution.py:23
  112.3 0.8 copy-start.3
  149.7 0.6 copy-start.6
Sparse Core Ops, SparseCore 0:
  10.2 35.2 all-gather.3
  47.7 59.0 all-gather.5

commit v5 on v4

--- a/solution.py
+++ b/solution.py
@@ -315,6 +315,26 @@
     )(came)
 
 
+def fetch_kernel(full_ref, gain_ref, after_ref, full_out_ref, gain_out_ref, sem):
+    fetch = pltpu.make_async_copy(full_ref, full_out_ref, sem)
+    fetch.start()
+    gain_out_ref[...] = gain_ref[...]
+    fetch.wait()
+
+
+def fetched(full, gain, after):
+    anywhere = pl.BlockSpec(memory_space=pl.ANY)
+    return pl.pallas_call(
+        fetch_kernel,
+        out_shape=[pltpu.VMEM(full.shape, full.dtype), pltpu.VMEM(gain.shape, gain.dtype)],
+        in_specs=[anywhere, whole, anywhere],
+        out_specs=[whole] * 2,
+        scratch_shapes=[pltpu.SemaphoreType.DMA],
+        compiler_params=pltpu.CompilerParams(vmem_limit_bytes=4 * 2**20),
+        cost_estimate=pl.CostEstimate(flops=0, bytes_accessed=2 << 20, transcendentals=0),
+    )(full, gain, after)
+
+
 def project_kernel(gated_ref, gain_ref, weight_ref, out_ref):
     gated = gated_ref[...]
     depth, lanes = gated.shape
@@ -390,18 +410,20 @@
         )
     place = lax.broadcasted_iota(jnp.int32, (group, 128), 1)
     found = jnp.where(place == 0, top, jnp.where(place == 1, summed, picked)).T
-    out_ref[...] = jnp.concatenate([found[0:1], found[1:2], found[2:3], found[2:3]], axis=1)
-
-
-def score(start, chosen, gain, target, weight, stride):
+    row = jnp.concatenate([found[0:1], found[1:2], found[2:3], found[2:3]], axis=1)
+    for k in range(out_ref.shape[0]):
+        out_ref[k] = row
+
+
+def score(start, chosen, gain, target, weight, stride, copies):
     slabs, group, width = chosen.shape
     return pl.pallas_call(
         functools.partial(logits_kernel, stride=stride),
-        out_shape=jax.ShapeDtypeStruct((1, 4 * group), f32),
+        out_shape=jax.ShapeDtypeStruct((copies, 1, 4 * group), f32),
         in_specs=[pl.BlockSpec(memory_space=pltpu.SMEM), whole, whole, whole, pl.BlockSpec(memory_space=pl.ANY)],
         out_specs=whole,
         scratch_shapes=[pltpu.VMEM(weight.shape, bf16), pltpu.SemaphoreType.DMA((slabs,))],
-        compiler_params=pltpu.CompilerParams(vmem_limit_bytes=54 * 2**20),
+        compiler_params=pltpu.CompilerParams(vmem_limit_bytes=52 * 2**20),
         cost_estimate=pl.CostEstimate(flops=2 * 64 * 4096 * 1024, bytes_accessed=9 << 20, transcendentals=0),
     )(start, chosen, gain, target, weight)
 
@@ -452,19 +474,19 @@
     came = exchange(message, CTX)
     swap = [(i * planes + k, k * planes + i) for i in range(planes) for k in range(planes)]
     rows_residual = lax.ppermute(rows_residual, PLANE, swap)
-    came, rows_residual = lax.optimization_barrier((came, rows_residual))
-
-    gated, out_full = lax.optimization_barrier((carry(came, planes, subs), out_full))
-    gated = exchange(gated, CTX).reshape(channels // 2, 2 * group)
-
-    partial = exchange(project(gated, norm_gain.reshape(1, -1), out_full).reshape(planes, count, -1), "tp")
+    out_full, gain = fetched(out_full, norm_gain.reshape(1, -1), rows_residual)
+    came, rows_residual, out_full, gain = lax.optimization_barrier((came, rows_residual, out_full, gain))
+
+    gated = exchange(carry(came, planes, subs), CTX).reshape(channels // 2, 2 * group)
+
+    partial = exchange(project(gated, gain, out_full).reshape(planes, count, -1), "tp")
     chosen = exchange(spread(partial, rows_residual, chunks), PLANE).reshape(planes, group, -1)
     columns = head_weight.shape[1]
     ways = lax.axis_size("tp")
     start = (lax.axis_index("z") * subs * ways + lax.axis_index("tp")) * columns
-    found = score(start.reshape(1), chosen, final_gain.reshape(planes, -1), own, head_full, ways * columns)
-
-    found = to_everyone(found, PLANE).reshape(chunks, 4, group)
+    found = score(start.reshape(1), chosen, final_gain.reshape(planes, -1), own, head_full, ways * columns, chunks)
+
+    found = exchange(found, PLANE).reshape(chunks, 4, group)
     top = jnp.max(found[:, 0], axis=0)
     summed = jnp.sum(found[:, 1] * jnp.exp(found[:, 0] - top[None, :]), axis=0)
     ref = jnp.sum(found[:, 2], axis=0) - top - jnp.log(summed)

time: 158 us -> 153 us (0.968)
  local copies, waits for them, and re-layouts: 5.87 us -> 3.03 us
    all_to_all x2, waiting for transfers between devices: 31.2 us -> 21.5 us  [exchange(): return lax.all_to_all(blocks, axes, 0, 0, tiled=True)]
    all_gather x1, waiting for transfers between devices: 0.01 us -> 9.12 us  [body(): out_full = lax.all_gather(out_weight.T, SUB, axis=0, tiled=True)]
    pallas_call x1, Pallas kernels: 5.71 us -> 4.1 us  [score(): pl.pallas_call(functools.partial(logits_kernel, stride=stride), out_shape...]
    unnamed x18 -> x16, local copies, waits for them, and re-layouts: 3.41 us -> 2.55 us
  transfers between devices with their start and end apart: 6 -> 6, of which waited for: 3 -> 4; matrix products, arithmetic and copies ran while one was open for 1% -> 1% of each run, Pallas kernels for 5% -> 5%
where the time goes in v5:
time: 153 us; the launch traced here: 152 us
  blocking collectives  63.1 us (41%)
  waiting for transfers between devices  35.7 us (23%)
  starting transfers between devices  22.2 us (15%)
  between operations  14.2 us (9%)
  Pallas kernels  12.2 us (8%)
  local copies, waits for them, and re-layouts  3.03 us (2%)
  other arithmetic  1.57 us (1%)
    all_to_all x4, blocking collectives, exchange(): return lax.all_to_all(blocks, axes, 0, 0, tiled=True)  63.1 us
    all_to_all x2, waiting for transfers between devices, exchange(): return lax.all_to_all(blocks, axes, 0, 0, tiled=True)  21.5 us
    all_to_all x2, starting transfers between devices, exchange(): return lax.all_to_all(blocks, axes, 0, 0, tiled=True)  16.9 us
    all_gather x1, waiting for transfers between devices, body(): out_full = lax.all_gather(out_weight.T, SUB, axis=0, tiled=True)  9.12 us
    ppermute x1, starting transfers between devices, body(): tail = lax.ppermute(tail, CTX, [(i, i + 1) for i in range(chunks - 1)])  4.5 us
    pallas_call x1, Pallas kernels, score(): pl.pallas_call(functools.partial(logits_kernel, stride=stride), out_shape...  4.1 us
    ppermute x1, waiting for transfers between devices, body(): tail = lax.ppermute(tail, CTX, [(i, i + 1) for i in range(chunks - 1)])  3.71 us
    pallas_call x1, Pallas kernels, local_part(): pl.pallas_call(local_kernel, out_shape=jax.ShapeDtypeStruct((channels //...  3.45 us
  transfers between devices with their start and end apart: 6, of which 4 were waited for; matrix products, arithmetic and copies ran while one was open for 1% of the time, Pallas kernels for 5%

profile of v5, /device:TPU:1, one launch (start us, length us, event | category | flops | bytes accessed | tf_op | source)
XLA Modules:
  0.0 152.2 jit_solution(10531476070078316988)
XLA Ops:
  7.2 0.0 copy-start
  7.2 0.0 copy-start.6
  7.2 0.0 copy-start.4
  7.2 0.0 all-gather.4.cloned.1.call-start
  7.2 0.7 all-gather.4.cloned.1.call-update
  7.9 0.0 all-gather.6.cloned.1.call-start
  8.0 0.7 all-gather.6.cloned.1.call-update
  8.7 1.4 shard_map.176
  10.1 4.5 %collective-permute-start = (bf16[16,1408]{1,0:T(8,128)(2,1)}, bf16[16,1408]{1,0:T(8,128)(2,1)S(1)}, u32[]{:S(2)}, u32[]{:S(2)}) collective-permute-start(bf16[16,1408]{1,0:T(8,128)(2,1)} %shard_map.176), channel_id=1, source_target_pairs={{0,8},{8,16},{16,24},{24,32},{32,40},{40,48},{48,56},{56,64},{64,7... | collective-permute-start | bytes 135176 | tf_op jit(solution)/shard_map/ppermute | solution.py:461
  14.6 0.7 broadcast_subtract_fusion
  15.2 0.0 copy-done
  15.2 0.2 convolution_convert_fusion
  15.4 3.7 %collective-permute-done.tail_ref = bf16[16,1408]{1,0:T(8,128)(2,1)S(1)} collective-permute-done((bf16[16,1408]{1,0:T(8,128)(2,1)}, bf16[16,1408]{1,0:T(8,128)(2,1)S(1)}, u32[]{:S(2)}, u32[]{:S(2)}) %collective-permute-start) | collective-permute-done | bytes 45088 | tf_op jit(solution)/shard_map/ppermute | solution.py:461
  19.1 0.0 copy-start.3
  19.1 0.6 copy-done.3
  19.8 3.5 %shard_map.177 = s16[64,32,128]{2,1,0:T(8,128)(2,1)} custom-call(s32[1]{0:T(128)} %bitcast.1.base_ref, s32[8]{0:T(128)} %scored_ref.1, f32[16]{0:T(128)} %rate_ref.1, f32[16]{0:T(128)} %skip_ref.1, bf16[128,1024]{1,0:T(8,128)(2,1)} %stream_ref.3, bf16[2,128,128]{2,1,0:T(8,128)(2,1)} %state_ref.3, bf16[16,1408]{1,0:T(8,128)(2,1)} %copy-done.3, ...), custom_call_target="tpu_custom_call" | custom-call | flops 134217728 | bytes 2097152 | tf_op jit(solution)/shard_map/pallas_call | solution.py:214
  23.2 0.0 copy-start.7
  23.2 12.3 %all-to-all-start = ((s16[64,32,128]{2,1,0:T(8,128)(2,1)}), s16[64,32,128]{2,1,0:T(8,128)(2,1)S(1)}, u32[]{:S(2)}, u32[]{:S(2)}) async-start(s16[64,32,128]{2,1,0:T(8,128)(2,1)} %shard_map.177), calls=%async_computation | async-start | bytes 1048576 | tf_op jit(solution)/shard_map/all_to_all | solution.py:23
  35.5 0.7 collective-permute-start.1
  36.2 0.0 collective-permute-done.1.after_ref.residual_ref
  36.2 9.1 %all-gather.4.cloned.1.call-done.full_ref = bf16[512,1024]{1,0:T(8,128)(2,1)} async-done(((bf16[64,1024]{1,0:T(8,128)(2,1)}), bf16[512,1024]{1,0:T(8,128)(2,1)}) %all-gather.4.cloned.1.call-update) | async-done | bytes 1048592 | tf_op jit(solution)/shard_map/all_gather | solution.py:463
  45.3 1.2 copy-done.1
  46.5 0.7 copy-done.2
  47.2 0.1 shard_map.178
  47.3 5.9 %all-to-all-done.came_ref = s16[64,32,128]{2,1,0:T(8,128)(2,1)S(1)} async-done(((s16[64,32,128]{2,1,0:T(8,128)(2,1)}), s16[64,32,128]{2,1,0:T(8,128)(2,1)S(1)}, u32[]{:S(2)}, u32[]{:S(2)}) %all-to-all-start) | async-done | bytes 524320 | tf_op jit(solution)/shard_map/all_to_all | solution.py:23
  53.2 1.5 %shard_map.179 = f32[64,8,128]{2,1,0:T(8,128)S(1)} custom-call(s16[64,32,128]{2,1,0:T(8,128)(2,1)S(1)} %all-to-all-done.came_ref), custom_call_target="tpu_custom_call" | custom-call | flops 268435456 | bytes 1048576 | tf_op jit(solution)/shard_map/pallas_call | solution.py:303
  54.8 21.9 %all_to_all.30 = f32[64,8,128]{2,1,0:T(8,128)S(1)} all-to-all(f32[64,8,128]{2,1,0:T(8,128)S(1)} %shard_map.179), channel_id=1, replica_groups=mesh['z'=8,'x'=4,'core'=2,'tp'=8] {'z','x','core'}, dimensions={0} | all-to-all | bytes 524288 | tf_op jit(solution)/shard_map/all_to_all | solution.py:23
  76.6 0.7 shard_map.180
  77.4 12.2 %all_to_all.31.partial_ref = f32[8,8,512]{2,1,0:T(8,128)S(1)} all-to-all(f32[8,8,512]{2,1,0:T(8,128)S(1)} %bitcast.17), channel_id=1, replica_groups=mesh['z'=8,'x'=4,'core'=2,'tp'=8] {'tp'}, dimensions={0} | all-to-all | bytes 262144 | tf_op jit(solution)/shard_map/all_to_all | solution.py:23
  89.6 0.9 shard_map.181
  90.5 4.6 %all-to-all-start.3 = ((bf16[64,8,512]{2,1,0:T(8,128)(2,1)}), bf16[64,8,512]{2,1,0:T(8,128)(2,1)S(1)}, u32[]{:S(2)}, u32[]{:S(2)}) async-start(bf16[64,8,512]{2,1,0:T(8,128)(2,1)} %shard_map.181), calls=%async_computation.3 | async-start | bytes 1048576 | tf_op jit(solution)/shard_map/all_to_all | solution.py:23
  95.1 0.0 copy-done.6
  95.1 0.1 reshape.69
  95.2 0.1 reshape.74.target_ref
  95.3 0.0 copy-done.4
  95.3 15.6 %all-to-all-done.3 = bf16[64,8,512]{2,1,0:T(8,128)(2,1)S(1)} async-done(((bf16[64,8,512]{2,1,0:T(8,128)(2,1)}), bf16[64,8,512]{2,1,0:T(8,128)(2,1)S(1)}, u32[]{:S(2)}, u32[]{:S(2)}) %all-to-all-start.3) | async-done | bytes 524320 | tf_op jit(solution)/shard_map/all_to_all | solution.py:23
  110.9 4.1 %shard_map.182 = f32[64,1,256]{2,1,0:T(1,128)S(1)} custom-call(s32[1]{0:T(128)} %bitcast.start_ref, bf16[8,64,512]{2,1,0:T(8,128)(2,1)S(1)} %bitcast.15, f32[8,512]{1,0:T(8,128)S(1)} %reshape.68.gain_ref, s32[64,1]{1,0:T(8,128)S(1)} %reshape.74.target_ref, bf16[8,4096,128]{2,1,0:T(8,128)(2,1)} %bitcast.19), custom_call_target="tpu_custom_call" | custom-call | flops 536870912 | bytes 9437184 | tf_op jit(solution)/shard_map/pallas_call | solution.py:420
  115.0 18.4 %all_to_all.32 = f32[64,1,256]{2,1,0:T(1,128)S(1)} all-to-all(f32[64,1,256]{2,1,0:T(1,128)S(1)} %shard_map.182), channel_id=1, replica_groups=mesh['z'=8,'x'=4,'core'=2,'tp'=8] {'z','tp'}, dimensions={0} | all-to-all | bytes 131072 | tf_op jit(solution)/shard_map/all_to_all | solution.py:23
  133.4 0.2 reduce.3
  133.6 0.1 reshape.71
  133.7 0.1 slice_reduce_fusion
  133.9 0.1 sub.41
  134.0 10.7 %all_to_all.33 = f32[8,8,8]{2,1,0:T(8,128)S(1)} all-to-all(f32[8,8,8]{2,1,0:T(8,128)S(1)} %broadcast_in_dim.2), channel_id=1, replica_groups=mesh['z'=8,'x'=4,'core'=2,'tp'=8] {'x','core'}, dimensions={0} | all-to-all | bytes 4096 | tf_op jit(solution)/shard_map/all_to_all | solution.py:23
  144.6 0.1 reshape.72
  144.7 0.0 copy-done.7
  144.7 0.0 copy-start.5
  144.8 0.6 multiply_multiply_fusion
  145.3 0.0 copy-done.5
  (10 shorter events, 0.1 us)
Async XLA Ops:
  7.2 8.1 %copy-start = (bf16[128,512]{1,0:T(8,128)(2,1)S(1)}, bf16[128,512]{1,0:T(8,128)(2,1)}, u32[]{:S(2)}) copy-start(bf16[128,512]{1,0:T(8,128)(2,1)} %param.28) | copy-start | bytes 393220
  7.2 87.9 %copy-start.6 = (s32[512]{0:T(512)S(1)}, s32[512]{0:T(512)}, u32[]{:S(2)}) copy-start(s32[512]{0:T(512)} %param.32) | copy-start | bytes 6148
  7.2 88.1 %copy-start.4 = (f32[4096]{0:T(1024)S(1)}, f32[4096]{0:T(1024)}, u32[]{:S(2)}) copy-start(f32[4096]{0:T(1024)} %param.29) | copy-start | bytes 49156
  7.2 38.1 %all-gather.4.cloned.1.call-start = ((), (), s32[]{:S(2)}) async-start(), calls=%async_computation.6 | async-start | bytes 1179648 | tf_op jit(solution)/shard_map/all_gather | solution.py:463
  7.9 103.0 %all-gather.6.cloned.1.call-start = ((), (), s32[]{:S(2)}) async-start(), calls=%async_computation.7 | async-start | bytes 9437184 | tf_op jit(solution)/shard_map/all_gather | solution.py:464
  10.1 9.1 %collective-permute-start = (bf16[16,1408]{1,0:T(8,128)(2,1)}, bf16[16,1408]{1,0:T(8,128)(2,1)S(1)}, u32[]{:S(2)}, u32[]{:S(2)}) collective-permute-start(bf16[16,1408]{1,0:T(8,128)(2,1)} %shard_map.176), channel_id=1, source_target_pairs={{0,8},{8,16},{16,24},{24,32},{32,40},{40,48},{48,56},{56,64},{64,7... | collective-permute-start | bytes 135176 | tf_op jit(solution)/shard_map/ppermute | solution.py:461
  19.1 0.6 copy-start.3
  23.2 121.5 %copy-start.7 = (f32[512]{0:T(512)S(1)}, f32[512]{0:T(512)}, u32[]{:S(2)}) copy-start(f32[512]{0:T(512)} %param.33) | copy-start | bytes 6148
  23.2 30.0 %all-to-all-start = ((s16[64,32,128]{2,1,0:T(8,128)(2,1)}), s16[64,32,128]{2,1,0:T(8,128)(2,1)S(1)}, u32[]{:S(2)}, u32[]{:S(2)}) async-start(s16[64,32,128]{2,1,0:T(8,128)(2,1)} %shard_map.177), calls=%async_computation | async-start | bytes 1048576 | tf_op jit(solution)/shard_map/all_to_all | solution.py:23
  35.5 0.7 collective-permute-start.1
  45.3 1.2 copy-start.1
  46.5 0.7 copy-start.2
  90.5 20.5 %all-to-all-start.3 = ((bf16[64,8,512]{2,1,0:T(8,128)(2,1)}), bf16[64,8,512]{2,1,0:T(8,128)(2,1)S(1)}, u32[]{:S(2)}, u32[]{:S(2)}) async-start(bf16[64,8,512]{2,1,0:T(8,128)(2,1)} %shard_map.181), calls=%async_computation.3 | async-start | bytes 1048576 | tf_op jit(solution)/shard_map/all_to_all | solution.py:23
  144.7 0.6 copy-start.5
Sparse Core Ops, SparseCore 0:
  10.2 35.0 all-gather.3
  47.5 59.9 all-gather.5

commit v6 on v5

--- a/solution.py
+++ b/solution.py
@@ -85,49 +85,69 @@
     )(stream, states, resets)
 
 
-def local_kernel(
+def silu_filter(pad_ref, keeping, taps, rows, margin):
+    summed = taps[0:1] * pad_ref[margin : margin + rows]
+    for k in range(1, 4):
+        summed = summed + keeping[k - 1] * taps[k : k + 1] * pad_ref[margin - k : margin - k + rows]
+    return (summed * jax.nn.sigmoid(summed)).astype(bf16)
+
+
+def kept(free, second, third, rows):
+    line = lax.broadcasted_iota(jnp.int32, free.shape, 0)
+    turned = jnp.where(line == 0, free, jnp.where(line == 1, second, third)).T
+    return [jnp.broadcast_to(turned[:rows, k : k + 1], (rows, 128)) for k in range(3)]
+
+
+def ready_kernel(
     base_ref,
     scored_ref,
     rate_ref,
     skip_ref,
     stream_ref,
     state_ref,
-    tail_ref,
     gate_ref,
     step_ref,
     reset_ref,
     taps_ref,
     state_taps_ref,
-    out_ref,
+    values_ref,
+    lead_ref,
+    taps_out_ref,
+    free_ref,
+    gates_ref,
+    mixing_ref,
+    own_ref,
+    to_end_ref,
+    logs_ref,
+    ends_ref,
+    pick_ref,
     pad_ref,
 ):
     rows, channels = stream_ref.shape
     states = state_ref.shape[2]
     heads = step_ref.shape[0]
-    margin = tail_ref.shape[0]
-    width = tail_ref.shape[1] - 128
+    margin = lead_ref.shape[0]
     count = scored_ref.shape[0]
     lane = lax.broadcasted_iota(jnp.int32, (8, 128), 1)
     line = lax.broadcasted_iota(jnp.int32, (8, 128), 0)
-
     flag = jnp.broadcast_to(reset_ref[...].astype(f32), (8, rows))
     free = 1.0 - flag
-    earlier = 1.0 - tail_ref[:, width:].astype(f32)[:8]
-    second = free * pltpu.roll(jnp.where(lane == rows - 1, earlier, free), 1, 1)
-    third = second * pltpu.roll(jnp.where(lane >= rows - 2, earlier, free), 2, 1)
-    turned = jnp.where(line == 0, free, jnp.where(line == 1, second, third)).T
-    keeping = [jnp.broadcast_to(turned[:, k : k + 1], (rows, 128)) for k in range(3)]
-
-    def filtered(block, tail, taps):
-        pad_ref[:margin] = tail.astype(f32)
-        pad_ref[margin:] = block.astype(f32)
-        summed = taps[0:1] * pad_ref[margin:]
-        for k in range(1, 4):
-            summed = summed + keeping[k - 1] * taps[k : k + 1] * pad_ref[margin - k : margin - k + rows]
-        return (summed * jax.nn.sigmoid(summed)).astype(bf16)
-
-    writes = filtered(state_ref[0], tail_ref[:, channels : channels + states], state_taps_ref[0])
-    reads = filtered(state_ref[1], tail_ref[:, channels + states : width], state_taps_ref[1])
+    free_ref[...] = free
+    second = free * pltpu.roll(free, 1, 1)
+    keeping = kept(free, second, second * pltpu.roll(free, 2, 1), rows)
+    lead_ref[:, :channels] = stream_ref[:margin]
+    taps_out_ref[:, :channels] = taps_ref[...]
+    for k in range(2):
+        span = slice(channels + k * states, channels + (k + 1) * states)
+        lead_ref[:, span] = state_ref[k, :margin]
+        taps_out_ref[:, span] = state_taps_ref[k]
+    pad_ref[:margin] = jnp.zeros((margin, 128), f32)
+    for b in range(channels // 128 + 2):
+        span = slice(b * 128, (b + 1) * 128)
+        k = b - channels // 128
+        pad_ref[margin:] = (stream_ref[:, span] if k < 0 else state_ref[k]).astype(f32)
+        taps = taps_ref[:, span] if k < 0 else state_taps_ref[k]
+        values_ref[:, span] = silu_filter(pad_ref, keeping, taps, rows, margin)
 
     place = jnp.zeros((8, 128), jnp.int32)
     for k in range(count):
@@ -139,8 +159,7 @@
         rate = jnp.where(head == k, rate_ref[k], rate)
         skip = jnp.where(head == k, skip_ref[k], skip)
     chosen = lane == place
-    pick = chosen.astype(bf16)
-    rows_reads = jnp.dot(pick, reads, preferred_element_type=f32)
+    pick_ref[...] = chosen.astype(f32)
     first = lax.broadcasted_iota(jnp.int32, (rows, rows), 0)
     upto = (first <= lax.broadcasted_iota(jnp.int32, (rows, rows), 1)).astype(bf16)
     step = step_ref[...]
@@ -151,19 +170,98 @@
     rows_segment = jnp.sum(jnp.where(chosen, segment, 0.0), axis=1, keepdims=True)
     rows_log = jnp.sum(jnp.where(chosen[None], cumulated[:, None, :], 0.0), axis=2, keepdims=True)
     causal = (lane <= place) & (segment == rows_segment)
+    gaps = jnp.where(causal[None], rows_log - cumulated[:, None, :], 0.0)
+    mixing = jnp.where(causal[None], jnp.exp(gaps), 0.0) * step[:, None, :]
+    mixing_ref[...] = mixing.reshape(heads * count, rows)
+    own_ref[...] = jnp.where(chosen[None], skip[:, None, :], 0.0).reshape(heads * count, rows)
+
+    end_segment = segment[0:1, rows - 1 :]
+    end_log = cumulated[:, rows - 1 :]
+    to_end_ref[...] = jnp.where(segment[0:1] == end_segment, jnp.exp(end_log - cumulated) * step, 0.0)
+    end_high, end_low = coded_log(end_log, jnp.broadcast_to(end_segment == 0.0, end_log.shape))
+    log_high, log_low = coded_log(rows_log, jnp.broadcast_to((rows_segment == 0.0)[None], rows_log.shape))
+    ends_ref[0] = jnp.broadcast_to(end_high, (heads, 128))
+    ends_ref[1] = jnp.broadcast_to(end_low, (heads, 128))
+    logs_ref[0] = jnp.broadcast_to(log_high, (heads, 8, 128))
+    logs_ref[1] = jnp.broadcast_to(log_low, (heads, 8, 128))
+    gate = jnp.dot(chosen.astype(bf16), gate_ref[...], preferred_element_type=f32)
+    power = exponent(gate, 0)
+    gates_ref[:8] = coded(gate, power)
+    gates_ref[8:] = jnp.broadcast_to(power, gate.shape)
+
+
+def ready(base, scored, rate, skip, stream, states, gate, step, resets, taps, state_taps, margin):
+    rows, channels = stream.shape
+    heads = step.shape[0]
+    width = channels + 2 * states.shape[2]
+    shapes = [
+        ((rows, width), bf16),
+        ((margin, width), bf16),
+        ((4, width), f32),
+        ((8, rows), f32),
+        ((16, channels), f32),
+        ((heads * 8, rows), f32),
+        ((heads * 8, rows), f32),
+        ((heads, rows), f32),
+        ((2, heads, 8, 128), f32),
+        ((2, heads, 128), f32),
+        ((8, rows), f32),
+    ]
+    return pl.pallas_call(
+        ready_kernel,
+        out_shape=[pltpu.VMEM(*shape) for shape in shapes],
+        in_specs=[pl.BlockSpec(memory_space=pltpu.SMEM)] * 4 + [whole] * 7,
+        out_specs=[whole] * len(shapes),
+        scratch_shapes=[pltpu.VMEM((margin + rows, 128), f32)],
+        compiler_params=pltpu.CompilerParams(vmem_limit_bytes=54 * 2**20),
+        cost_estimate=pl.CostEstimate(flops=1 << 24, bytes_accessed=2 << 20, transcendentals=1 << 18),
+    )(base, scored, rate, skip, stream, states, gate, step, resets, taps, state_taps)
+
+
+def local_kernel(
+    values_ref,
+    lead_ref,
+    taps_ref,
+    free_ref,
+    gates_ref,
+    mixing_ref,
+    own_ref,
+    to_end_ref,
+    logs_ref,
+    ends_ref,
+    pick_ref,
+    tail_ref,
+    out_ref,
+    pad_ref,
+):
+    rows, width = values_ref.shape
+    margin = lead_ref.shape[0]
+    channels = gates_ref.shape[1]
+    lane = lax.broadcasted_iota(jnp.int32, (8, 128), 1)
+    line = lax.broadcasted_iota(jnp.int32, (8, 128), 0)
+    free = free_ref[...]
+    earlier = 1.0 - tail_ref[:, width:].astype(f32)[:8]
+    second = free * pltpu.roll(jnp.where(lane == rows - 1, earlier, free), 1, 1)
+    third = second * pltpu.roll(jnp.where(lane >= rows - 2, earlier, free), 2, 1)
+    keeping = kept(free, second, third, margin)
+
+    def filtered(span):
+        pad_ref[:margin] = tail_ref[:, span].astype(f32)
+        pad_ref[margin:] = lead_ref[:, span].astype(f32)
+        start = silu_filter(pad_ref, keeping, taps_ref[:, span], margin, margin)
+        return jnp.concatenate([start, values_ref[margin:, span]], axis=0)
+
+    writes = filtered(slice(channels, channels + 128))
+    reads = filtered(slice(channels + 128, width))
+    rows_reads = jnp.dot(pick_ref[...].astype(bf16), reads, preferred_element_type=f32)
     scores = lax.dot_general(
         rows_reads.astype(bf16), writes, (((1,), (1,)), ((), ())), preferred_element_type=f32
     )
-    gaps = jnp.where(causal[None], rows_log - cumulated[:, None, :], 0.0)
-    mixing = jnp.where(causal[None], jnp.exp(gaps), 0.0) * scores[None] * step[:, None, :]
-    mixing = mixing + jnp.where(chosen[None], skip[:, None, :], 0.0)
-    mixing = split(mixing.reshape(heads * count, rows), 3)
-
-    end_segment = segment[0:1, rows - 1 :]
-    end_log = cumulated[:, rows - 1 :]
-    to_end = jnp.where(segment[0:1] == end_segment, jnp.exp(end_log - cumulated) * step, 0.0)
-    end_high, end_low = coded_log(end_log, jnp.broadcast_to(end_segment == 0.0, end_log.shape))
-    log_high, log_low = coded_log(rows_log, jnp.broadcast_to((rows_segment == 0.0)[None], rows_log.shape))
+    heads = to_end_ref.shape[0]
+    scores = jnp.broadcast_to(scores[None], (heads, 8, rows)).reshape(heads * 8, rows)
+    mixing = split(mixing_ref[...] * scores + own_ref[...], 3)
+    to_end = to_end_ref[...]
+    end_high, end_low = ends_ref[0], ends_ref[1]
 
     power = exponent(rows_reads, 1)
     rows_reads = coded(rows_reads, power)
@@ -176,7 +274,7 @@
     for b in range(channels // 128):
         span = slice(b * 128, (b + 1) * 128)
         p, q = 2 * b, 2 * b + 1
-        values = filtered(stream_ref[:, span], tail_ref[:, span], taps_ref[:, span])
+        values = filtered(span)
         ends = jnp.concatenate(
             [jnp.broadcast_to(to_end[p : p + 1], (64, rows)), jnp.broadcast_to(to_end[q : q + 1], (64, rows))], axis=0
         )
@@ -186,17 +284,16 @@
         met = jnp.dot(both, values, preferred_element_type=f32)
         met = met[:16] + met[16:32] + met[32:]
         local = jnp.where(left, met[:8], met[8:])
-        gate = jnp.dot(pick, gate_ref[:, span], preferred_element_type=f32)
-        local_power, gate_power, state_power = exponent(local, 0), exponent(gate, 0), exponent(state, 1)
-        others = jnp.where(line == 2, local_power, jnp.where(line == 3, gate_power, 0.0))
+        local_power, state_power = exponent(local, 0), exponent(state, 1)
+        others = jnp.where(line == 2, local_power, jnp.where(line == 3, gates_ref[8:, span], 0.0))
         others = jnp.where(line == 1, jnp.where(left, end_low[p : p + 1], end_low[q : q + 1]), others)
         others = jnp.where(line == 0, jnp.where(left, end_high[p : p + 1], end_high[q : q + 1]), others)
         side = jnp.concatenate(
             [
                 coded(local, local_power),
-                coded(gate, gate_power),
-                jnp.where(left, log_high[p], log_high[q]),
-                jnp.where(left, log_low[p], log_low[q]),
+                gates_ref[:8, span],
+                jnp.where(left, logs_ref[0, p], logs_ref[0, q]),
+                jnp.where(left, logs_ref[1, p], logs_ref[1, q]),
                 others,
                 powers,
                 empty,
@@ -209,17 +306,17 @@
             out_ref[8 * b : 8 * b + 8, at : at + 16, :] = part.astype(jnp.int16)
 
 
-def local_part(base, scored, rate, skip, stream, states, tail, gate, step, resets, taps, state_taps):
-    channels = stream.shape[1]
+def local_part(made, tail):
+    channels = made[4].shape[1]
     return pl.pallas_call(
         local_kernel,
         out_shape=jax.ShapeDtypeStruct((channels // 16, 32, 128), jnp.int16),
-        in_specs=[pl.BlockSpec(memory_space=pltpu.SMEM)] * 4 + [whole] * 8,
+        in_specs=[whole] * (len(made) + 1),
         out_specs=whole,
-        scratch_shapes=[pltpu.VMEM((tail.shape[0] + stream.shape[0], 128), f32)],
-        compiler_params=pltpu.CompilerParams(vmem_limit_bytes=58 * 2**20),
+        scratch_shapes=[pltpu.VMEM((2 * tail.shape[0], 128), f32)],
+        compiler_params=pltpu.CompilerParams(vmem_limit_bytes=12 * 2**20),
         cost_estimate=pl.CostEstimate(flops=1 << 27, bytes_accessed=2 << 20, transcendentals=1 << 18),
-    )(base, scored, rate, skip, stream, states, tail, gate, step, resets, taps, state_taps)
+    )(*made, tail)
 
 
 def carry_kernel(came_ref, out_ref, side_ref, met_ref, weight_ref, *, planes, subs):
@@ -467,9 +564,10 @@
     own = lax.dynamic_index_in_dim(targets.reshape(planes, subs, count), lax.axis_index(SUB), 1, False).reshape(group, 1)
 
     base = (lax.axis_index(CTX) * rows).reshape(1)
-    message = local_part(
-        base, scored, decay_rate, skip_gain, inner_input, state_inputs, tail, gate_input, step_size, flags, conv_inner, conv_state
+    made = ready(
+        base, scored, decay_rate, skip_gain, inner_input, state_inputs, gate_input, step_size, flags, conv_inner, conv_state, tail.shape[0]
     )
+    message = local_part(made, tail)
     message, rows_residual = lax.optimization_barrier((message, rows_residual))
     came = exchange(message, CTX)
     swap = [(i * planes + k, k * planes + i) for i in range(planes) for k in range(planes)]

time: 153 us -> 152 us (level)
  waiting for transfers between devices: 35.7 us -> 33.8 us
    all_to_all x2, waiting for transfers between devices: 21.5 us -> 18.6 us  [exchange(): return lax.all_to_all(blocks, axes, 0, 0, tiled=True)]
    all_gather x1, waiting for transfers between devices: 9.12 us -> 12 us  [body(): out_full = lax.all_gather(out_weight.T, SUB, axis=0, tiled=True)]
    ppermute x1, waiting for transfers between devices: 3.71 us -> 1.8 us  [body(): tail = lax.ppermute(tail, CTX, [(i, i + 1) for i in range(chunks - 1)])]
    pallas_call x0 -> x1, Pallas kernels: none -> 1.9 us  [ready(): pl.pallas_call(ready_kernel, out_shape=[pltpu.VMEM(*shape) for shape in s...]
    pallas_call x1, Pallas kernels: 3.45 us -> 1.86 us  [local_part(): pl.pallas_call(local_kernel, out_shape=jax.ShapeDtypeStruct((channels //...]
  transfers between devices with their start and end apart: 6 -> 6, of which waited for: 4 -> 4; matrix products, arithmetic and copies ran while one was open for 1% -> 1% of each run, Pallas kernels for 5% -> 6%
where the time goes in v6:
time: 152 us; the launch traced here: 151 us
  blocking collectives  64.1 us (42%)
  waiting for transfers between devices  33.8 us (22%)
  starting transfers between devices  22.2 us (15%)
  between operations  14.2 us (9%)
  Pallas kernels  12.5 us (8%)
  local copies, waits for them, and re-layouts  2.42 us (2%)
  other arithmetic  1.57 us (1%)
    all_to_all x4, blocking collectives, exchange(): return lax.all_to_all(blocks, axes, 0, 0, tiled=True)  64.1 us
    all_to_all x2, waiting for transfers between devices, exchange(): return lax.all_to_all(blocks, axes, 0, 0, tiled=True)  18.6 us
    all_to_all x2, starting transfers between devices, exchange(): return lax.all_to_all(blocks, axes, 0, 0, tiled=True)  16.9 us
    all_gather x1, waiting for transfers between devices, body(): out_full = lax.all_gather(out_weight.T, SUB, axis=0, tiled=True)  12 us
    ppermute x1, starting transfers between devices, body(): tail = lax.ppermute(tail, CTX, [(i, i + 1) for i in range(chunks - 1)])  4.5 us
    pallas_call x1, Pallas kernels, score(): pl.pallas_call(functools.partial(logits_kernel, stride=stride), out_shape...  4.1 us
  transfers between devices with their start and end apart: 6, of which 4 were waited for; matrix products, arithmetic and copies ran while one was open for 1% of the time, Pallas kernels for 6%

profile of v6, /device:TPU:1, one launch (start us, length us, event | category | flops | bytes accessed | tf_op | source)
XLA Modules:
  0.0 150.9 jit_solution(8805722466234737867)
XLA Ops:
  7.2 0.0 copy-start
  7.2 0.0 copy-start.5
  7.2 0.0 copy-start.3
  7.2 0.0 all-gather.4.cloned.1.call-start
  7.2 0.7 all-gather.4.cloned.1.call-update
  7.9 0.0 all-gather.6.cloned.1.call-start
  8.0 0.7 all-gather.6.cloned.1.call-update
  8.7 1.4 shard_map.177
  10.1 4.5 %collective-permute-start = (bf16[16,1408]{1,0:T(8,128)(2,1)}, bf16[16,1408]{1,0:T(8,128)(2,1)S(1)}, u32[]{:S(2)}, u32[]{:S(2)}) collective-permute-start(bf16[16,1408]{1,0:T(8,128)(2,1)} %shard_map.177), channel_id=1, source_target_pairs={{0,8},{8,16},{16,24},{24,32},{32,40},{40,48},{48,56},{56,64},{64,7... | collective-permute-start | bytes 135176 | tf_op jit(solution)/shard_map/ppermute | solution.py:558
  14.6 0.7 broadcast_subtract_fusion
  15.2 0.0 copy-done
  15.2 0.2 convolution_convert_fusion
  15.4 1.9 %shard_map.176 = (bf16[128,1280]{1,0:T(8,128)(2,1)S(1)}, bf16[16,1280]{1,0:T(8,128)(2,1)S(1)}, f32[4,1280]{1,0:T(4,128)S(1)}, f32[8,128]{1,0:T(8,128)S(1)}, f32[...) custom-call(s32[1]{0:T(128)} %bitcast.1.base_ref, ...), custom_call_target="tpu_custom_call" | custom-call | flops 16777216 | bytes 2097152 | tf_op jit(solution)/shard_map/pallas_call | solution.py:210
  17.3 1.8 %collective-permute-done.tail_ref = bf16[16,1408]{1,0:T(8,128)(2,1)S(1)} collective-permute-done((bf16[16,1408]{1,0:T(8,128)(2,1)}, bf16[16,1408]{1,0:T(8,128)(2,1)S(1)}, u32[]{:S(2)}, u32[]{:S(2)}) %collective-permute-start) | collective-permute-done | bytes 45088 | tf_op jit(solution)/shard_map/ppermute | solution.py:558
  19.1 1.9 %shard_map.178 = s16[64,32,128]{2,1,0:T(8,128)(2,1)} custom-call(bf16[128,1280]{1,0:T(8,128)(2,1)S(1)} %get-tuple-element.21.values_ref, bf16[16,1280]{1,0:T(8,128)(2,1)S(1)} %get-tuple-element.22.lead_ref, f32[4,1280]{1,0:T(4,128)S(1)} %get-tuple-element.23.taps_ref, f32[8,128]{1,0:T(8,128)S(1)} %get-tuple-element.24.free_ref, ...), custom_call_target="tpu_custom_call" | custom-call | flops 134217728 | bytes 2097152 | tf_op jit(solution)/shard_map/pallas_call | solution.py:311
  21.0 0.0 copy-start.6
  21.0 12.3 %all-to-all-start = ((s16[64,32,128]{2,1,0:T(8,128)(2,1)}), s16[64,32,128]{2,1,0:T(8,128)(2,1)S(1)}, u32[]{:S(2)}, u32[]{:S(2)}) async-start(s16[64,32,128]{2,1,0:T(8,128)(2,1)} %shard_map.178), calls=%async_computation | async-start | bytes 1048576 | tf_op jit(solution)/shard_map/all_to_all | solution.py:23
  33.3 0.7 collective-permute-start.1
  34.0 0.0 collective-permute-done.1.after_ref.residual_ref
  34.0 12.0 %all-gather.4.cloned.1.call-done.full_ref = bf16[512,1024]{1,0:T(8,128)(2,1)} async-done(((bf16[64,1024]{1,0:T(8,128)(2,1)}), bf16[512,1024]{1,0:T(8,128)(2,1)}) %all-gather.4.cloned.1.call-update) | async-done | bytes 1048592 | tf_op jit(solution)/shard_map/all_gather | solution.py:560
  46.0 0.0 copy-start.1
  46.0 1.2 copy-done.1
  47.2 0.7 copy-done.2
  47.9 0.1 shard_map.179
  48.0 3.0 %all-to-all-done.came_ref = s16[64,32,128]{2,1,0:T(8,128)(2,1)S(1)} async-done(((s16[64,32,128]{2,1,0:T(8,128)(2,1)}), s16[64,32,128]{2,1,0:T(8,128)(2,1)S(1)}, u32[]{:S(2)}, u32[]{:S(2)}) %all-to-all-start) | async-done | bytes 524320 | tf_op jit(solution)/shard_map/all_to_all | solution.py:23
  51.0 1.5 %shard_map.180 = f32[64,8,128]{2,1,0:T(8,128)S(1)} custom-call(s16[64,32,128]{2,1,0:T(8,128)(2,1)S(1)} %all-to-all-done.came_ref), custom_call_target="tpu_custom_call" | custom-call | flops 268435456 | bytes 1048576 | tf_op jit(solution)/shard_map/pallas_call | solution.py:400
  52.6 21.9 %all_to_all.30 = f32[64,8,128]{2,1,0:T(8,128)S(1)} all-to-all(f32[64,8,128]{2,1,0:T(8,128)S(1)} %shard_map.180), channel_id=1, replica_groups=mesh['z'=8,'x'=4,'core'=2,'tp'=8] {'z','x','core'}, dimensions={0} | all-to-all | bytes 524288 | tf_op jit(solution)/shard_map/all_to_all | solution.py:23
  74.4 0.7 shard_map.181
  75.2 13.2 %all_to_all.31.partial_ref = f32[8,8,512]{2,1,0:T(8,128)S(1)} all-to-all(f32[8,8,512]{2,1,0:T(8,128)S(1)} %bitcast.17), channel_id=1, replica_groups=mesh['z'=8,'x'=4,'core'=2,'tp'=8] {'tp'}, dimensions={0} | all-to-all | bytes 262144 | tf_op jit(solution)/shard_map/all_to_all | solution.py:23
  88.3 0.9 shard_map.182
  89.2 4.6 %all-to-all-start.3 = ((bf16[64,8,512]{2,1,0:T(8,128)(2,1)}), bf16[64,8,512]{2,1,0:T(8,128)(2,1)S(1)}, u32[]{:S(2)}, u32[]{:S(2)}) async-start(bf16[64,8,512]{2,1,0:T(8,128)(2,1)} %shard_map.182), calls=%async_computation.3 | async-start | bytes 1048576 | tf_op jit(solution)/shard_map/all_to_all | solution.py:23
  93.8 0.0 copy-done.5
  93.9 0.1 reshape.69
  94.0 0.1 reshape.74.target_ref
  94.0 0.0 copy-done.3
  94.1 15.6 %all-to-all-done.3 = bf16[64,8,512]{2,1,0:T(8,128)(2,1)S(1)} async-done(((bf16[64,8,512]{2,1,0:T(8,128)(2,1)}), bf16[64,8,512]{2,1,0:T(8,128)(2,1)S(1)}, u32[]{:S(2)}, u32[]{:S(2)}) %all-to-all-start.3) | async-done | bytes 524320 | tf_op jit(solution)/shard_map/all_to_all | solution.py:23
  109.7 4.1 %shard_map.183 = f32[64,1,256]{2,1,0:T(1,128)S(1)} custom-call(s32[1]{0:T(128)} %bitcast.start_ref, bf16[8,64,512]{2,1,0:T(8,128)(2,1)S(1)} %bitcast.15, f32[8,512]{1,0:T(8,128)S(1)} %reshape.68.gain_ref, s32[64,1]{1,0:T(8,128)S(1)} %reshape.74.target_ref, bf16[8,4096,128]{2,1,0:T(8,128)(2,1)} %bitcast.19), custom_call_target="tpu_custom_call" | custom-call | flops 536870912 | bytes 9437184 | tf_op jit(solution)/shard_map/pallas_call | solution.py:517
  113.8 18.8 %all_to_all.32 = f32[64,1,256]{2,1,0:T(1,128)S(1)} all-to-all(f32[64,1,256]{2,1,0:T(1,128)S(1)} %shard_map.183), channel_id=1, replica_groups=mesh['z'=8,'x'=4,'core'=2,'tp'=8] {'z','tp'}, dimensions={0} | all-to-all | bytes 131072 | tf_op jit(solution)/shard_map/all_to_all | solution.py:23
  132.6 0.2 reduce.3
  132.8 0.1 reshape.71
  132.9 0.1 slice_reduce_fusion
  133.1 0.1 sub.41
  133.1 10.2 %all_to_all.33 = f32[8,8,8]{2,1,0:T(8,128)S(1)} all-to-all(f32[8,8,8]{2,1,0:T(8,128)S(1)} %broadcast_in_dim.2), channel_id=1, replica_groups=mesh['z'=8,'x'=4,'core'=2,'tp'=8] {'x','core'}, dimensions={0} | all-to-all | bytes 4096 | tf_op jit(solution)/shard_map/all_to_all | solution.py:23
  143.4 0.1 reshape.72
  143.5 0.0 copy-done.6
  143.5 0.0 copy-start.4
  143.5 0.6 multiply_multiply_fusion
  144.1 0.0 copy-done.4
  (9 shorter events, 0.1 us)
Async XLA Ops:
  7.2 8.1 %copy-start = (bf16[128,512]{1,0:T(8,128)(2,1)S(1)}, bf16[128,512]{1,0:T(8,128)(2,1)}, u32[]{:S(2)}) copy-start(bf16[128,512]{1,0:T(8,128)(2,1)} %param.28) | copy-start | bytes 393220
  7.2 86.7 %copy-start.5 = (s32[512]{0:T(512)S(1)}, s32[512]{0:T(512)}, u32[]{:S(2)}) copy-start(s32[512]{0:T(512)} %param.32) | copy-start | bytes 6148
  7.2 86.9 %copy-start.3 = (f32[4096]{0:T(1024)S(1)}, f32[4096]{0:T(1024)}, u32[]{:S(2)}) copy-start(f32[4096]{0:T(1024)} %param.29) | copy-start | bytes 49156
  7.2 38.8 %all-gather.4.cloned.1.call-start = ((), (), s32[]{:S(2)}) async-start(), calls=%async_computation.6 | async-start | bytes 1179648 | tf_op jit(solution)/shard_map/all_gather | solution.py:560
  7.9 101.8 %all-gather.6.cloned.1.call-start = ((), (), s32[]{:S(2)}) async-start(), calls=%async_computation.7 | async-start | bytes 9437184 | tf_op jit(solution)/shard_map/all_gather | solution.py:561
  10.1 9.1 %collective-permute-start = (bf16[16,1408]{1,0:T(8,128)(2,1)}, bf16[16,1408]{1,0:T(8,128)(2,1)S(1)}, u32[]{:S(2)}, u32[]{:S(2)}) collective-permute-start(bf16[16,1408]{1,0:T(8,128)(2,1)} %shard_map.177), channel_id=1, source_target_pairs={{0,8},{8,16},{16,24},{24,32},{32,40},{40,48},{48,56},{56,64},{64,7... | collective-permute-start | bytes 135176 | tf_op jit(solution)/shard_map/ppermute | solution.py:558
  21.0 122.5 %copy-start.6 = (f32[512]{0:T(512)S(1)}, f32[512]{0:T(512)}, u32[]{:S(2)}) copy-start(f32[512]{0:T(512)} %param.33) | copy-start | bytes 6148
  21.0 30.0 %all-to-all-start = ((s16[64,32,128]{2,1,0:T(8,128)(2,1)}), s16[64,32,128]{2,1,0:T(8,128)(2,1)S(1)}, u32[]{:S(2)}, u32[]{:S(2)}) async-start(s16[64,32,128]{2,1,0:T(8,128)(2,1)} %shard_map.178), calls=%async_computation | async-start | bytes 1048576 | tf_op jit(solution)/shard_map/all_to_all | solution.py:23
  33.3 0.7 collective-permute-start.1
  46.0 1.2 copy-start.1
  47.2 0.7 copy-start.2
  89.2 20.5 %all-to-all-start.3 = ((bf16[64,8,512]{2,1,0:T(8,128)(2,1)}), bf16[64,8,512]{2,1,0:T(8,128)(2,1)S(1)}, u32[]{:S(2)}, u32[]{:S(2)}) async-start(bf16[64,8,512]{2,1,0:T(8,128)(2,1)} %shard_map.182), calls=%async_computation.3 | async-start | bytes 1048576 | tf_op jit(solution)/shard_map/all_to_all | solution.py:23
  143.5 0.6 copy-start.4
Sparse Core Ops, SparseCore 0:
  10.2 35.7 all-gather.3
  48.2 58.0 all-gather.5

commit v7 on v6

--- a/solution.py
+++ b/solution.py
@@ -572,10 +572,12 @@
     came = exchange(message, CTX)
     swap = [(i * planes + k, k * planes + i) for i in range(planes) for k in range(planes)]
     rows_residual = lax.ppermute(rows_residual, PLANE, swap)
-    out_full, gain = fetched(out_full, norm_gain.reshape(1, -1), rows_residual)
-    came, rows_residual, out_full, gain = lax.optimization_barrier((came, rows_residual, out_full, gain))
-
-    gated = exchange(carry(came, planes, subs), CTX).reshape(channels // 2, 2 * group)
+    came, rows_residual = lax.optimization_barrier((came, rows_residual))
+
+    gated = carry(came, planes, subs)
+    out_full, gain = fetched(out_full, norm_gain.reshape(1, -1), gated)
+    gated, out_full, gain = lax.optimization_barrier((exchange(gated, CTX), out_full, gain))
+    gated = gated.reshape(channels // 2, 2 * group)
 
     partial = exchange(project(gated, gain, out_full).reshape(planes, count, -1), "tp")
     chosen = exchange(spread(partial, rows_residual, chunks), PLANE).reshape(planes, group, -1)

time: 152 us -> 151 us (level)
  blocking collectives: 64.1 us -> 43.2 us
  waiting for transfers between devices: 33.8 us -> 47 us
  starting transfers between devices: 22.2 us -> 28.9 us
    all_to_all x2 -> x3, waiting for transfers between devices: 18.6 us -> 43.8 us  [exchange(): return lax.all_to_all(blocks, axes, 0, 0, tiled=True)]
    all_to_all x4 -> x3, blocking collectives: 64.1 us -> 43.2 us  [exchange(): return lax.all_to_all(blocks, axes, 0, 0, tiled=True)]
    all_gather x1, waiting for transfers between devices: 12 us -> 0.02 us  [body(): out_full = lax.all_gather(out_weight.T, SUB, axis=0, tiled=True)]
    all_to_all x2 -> x3, starting transfers between devices: 16.9 us -> 23.7 us  [exchange(): return lax.all_to_all(blocks, axes, 0, 0, tiled=True)]
  transfers between devices with their start and end apart: 6 -> 7, of which waited for: 4 -> 4; matrix products, arithmetic and copies ran while one was open for 1% -> 1% of each run, Pallas kernels for 6% -> 6%
where the time goes in v7:
time: 151 us
  waiting for transfers between devices  47 us (31%)
  blocking collectives  43.2 us (29%)
  starting transfers between devices  28.9 us (19%)
  between operations  14.2 us (9%)
  Pallas kernels  13.2 us (9%)
  local copies, waits for them, and re-layouts  2.41 us (2%)
  other arithmetic  1.57 us (1%)
    all_to_all x3, waiting for transfers between devices, exchange(): return lax.all_to_all(blocks, axes, 0, 0, tiled=True)  43.8 us
    all_to_all x3, blocking collectives, exchange(): return lax.all_to_all(blocks, axes, 0, 0, tiled=True)  43.2 us
    all_to_all x3, starting transfers between devices, exchange(): return lax.all_to_all(blocks, axes, 0, 0, tiled=True)  23.7 us
    ppermute x1, starting transfers between devices, body(): tail = lax.ppermute(tail, CTX, [(i, i + 1) for i in range(chunks - 1)])  4.5 us
    pallas_call x1, Pallas kernels, score(): pl.pallas_call(functools.partial(logits_kernel, stride=stride), out_shape...  4.1 us
  transfers between devices with their start and end apart: 7, of which 4 were waited for; matrix products, arithmetic and copies ran while one was open for 1% of the time, Pallas kernels for 6%

profile of v7, /device:TPU:1, one launch (start us, length us, event | category | flops | bytes accessed | tf_op | source)
XLA Modules:
  0.0 150.8 jit_solution(15539547839583643370)
XLA Ops:
  7.2 0.0 copy-start
  7.2 0.0 copy-start.5
  7.2 0.0 copy-start.3
  7.2 0.0 all-gather.4.cloned.1.call-start
  7.2 0.7 all-gather.4.cloned.1.call-update
  7.9 0.0 all-gather.6.cloned.1.call-start
  8.0 0.7 all-gather.6.cloned.1.call-update
  8.7 1.4 shard_map.177
  10.1 4.5 %collective-permute-start = (bf16[16,1408]{1,0:T(8,128)(2,1)}, bf16[16,1408]{1,0:T(8,128)(2,1)S(1)}, u32[]{:S(2)}, u32[]{:S(2)}) collective-permute-start(bf16[16,1408]{1,0:T(8,128)(2,1)} %shard_map.177), channel_id=1, source_target_pairs={{0,8},{8,16},{16,24},{24,32},{32,40},{40,48},{48,56},{56,64},{64,7... | collective-permute-start | bytes 135176 | tf_op jit(solution)/shard_map/ppermute | solution.py:558
  14.6 0.7 broadcast_subtract_fusion
  15.2 0.0 copy-done
  15.3 0.2 convolution_convert_fusion
  15.4 1.9 %shard_map.176 = (bf16[128,1280]{1,0:T(8,128)(2,1)S(1)}, bf16[16,1280]{1,0:T(8,128)(2,1)S(1)}, f32[4,1280]{1,0:T(4,128)S(1)}, f32[8,128]{1,0:T(8,128)S(1)}, f32[...) custom-call(s32[1]{0:T(128)} %bitcast.1.base_ref, ...), custom_call_target="tpu_custom_call" | custom-call | flops 16777216 | bytes 2097152 | tf_op jit(solution)/shard_map/pallas_call | solution.py:210
  17.3 1.8 %collective-permute-done.tail_ref = bf16[16,1408]{1,0:T(8,128)(2,1)S(1)} collective-permute-done((bf16[16,1408]{1,0:T(8,128)(2,1)}, bf16[16,1408]{1,0:T(8,128)(2,1)S(1)}, u32[]{:S(2)}, u32[]{:S(2)}) %collective-permute-start) | collective-permute-done | bytes 45088 | tf_op jit(solution)/shard_map/ppermute | solution.py:558
  19.1 1.9 %shard_map.178 = s16[64,32,128]{2,1,0:T(8,128)(2,1)} custom-call(bf16[128,1280]{1,0:T(8,128)(2,1)S(1)} %get-tuple-element.22.values_ref, bf16[16,1280]{1,0:T(8,128)(2,1)S(1)} %get-tuple-element.23.lead_ref, f32[4,1280]{1,0:T(4,128)S(1)} %get-tuple-element.24.taps_ref, f32[8,128]{1,0:T(8,128)S(1)} %get-tuple-element.25.free_ref, ...), custom_call_target="tpu_custom_call" | custom-call | flops 134217728 | bytes 2097152 | tf_op jit(solution)/shard_map/pallas_call | solution.py:311
  21.0 12.2 %all-to-all-start = ((s16[64,32,128]{2,1,0:T(8,128)(2,1)}), s16[64,32,128]{2,1,0:T(8,128)(2,1)S(1)}, u32[]{:S(2)}, u32[]{:S(2)}) async-start(s16[64,32,128]{2,1,0:T(8,128)(2,1)} %shard_map.178), calls=%async_computation | async-start | bytes 1048576 | tf_op jit(solution)/shard_map/all_to_all | solution.py:23
  33.2 0.0 copy-start.6
  33.2 0.7 collective-permute-start.1
  33.9 0.0 collective-permute-done.1.residual_ref
  33.9 17.0 %all-to-all-done.came_ref = s16[64,32,128]{2,1,0:T(8,128)(2,1)S(1)} async-done(((s16[64,32,128]{2,1,0:T(8,128)(2,1)}), s16[64,32,128]{2,1,0:T(8,128)(2,1)S(1)}, u32[]{:S(2)}, u32[]{:S(2)}) %all-to-all-start) | async-done | bytes 524320 | tf_op jit(solution)/shard_map/all_to_all | solution.py:23
  50.9 2.2 %shard_map.179.after_ref = f32[64,8,128]{2,1,0:T(8,128)} custom-call(s16[64,32,128]{2,1,0:T(8,128)(2,1)S(1)} %all-to-all-done.came_ref), custom_call_target="tpu_custom_call" | custom-call | flops 268435456 | bytes 1048576 | tf_op jit(solution)/shard_map/pallas_call | solution.py:400
  53.1 6.9 %all-to-all-start.1 = ((f32[64,8,128]{2,1,0:T(8,128)}), f32[64,8,128]{2,1,0:T(8,128)S(1)}, u32[]{:S(2)}, u32[]{:S(2)}) async-start(f32[64,8,128]{2,1,0:T(8,128)} %shard_map.179.after_ref), calls=%async_computation.1 | async-start | bytes 524288 | tf_op jit(solution)/shard_map/all_to_all | solution.py:23
  60.1 0.0 all-gather.4.cloned.1.call-done.full_ref
  60.1 0.0 copy-start.1
  60.1 1.2 copy-done.1
  61.3 0.7 copy-done.2
  62.0 0.1 shard_map.180
  62.1 11.1 %all-to-all-done.1 = f32[64,8,128]{2,1,0:T(8,128)S(1)} async-done(((f32[64,8,128]{2,1,0:T(8,128)}), f32[64,8,128]{2,1,0:T(8,128)S(1)}, u32[]{:S(2)}, u32[]{:S(2)}) %all-to-all-start.1) | async-done | bytes 262176 | tf_op jit(solution)/shard_map/all_to_all | solution.py:23
  73.2 0.7 shard_map.181
  74.0 14.2 %all_to_all.30.partial_ref = f32[8,8,512]{2,1,0:T(8,128)S(1)} all-to-all(f32[8,8,512]{2,1,0:T(8,128)S(1)} %bitcast.17), channel_id=1, replica_groups=mesh['z'=8,'x'=4,'core'=2,'tp'=8] {'tp'}, dimensions={0} | all-to-all | bytes 262144 | tf_op jit(solution)/shard_map/all_to_all | solution.py:23
  88.2 0.9 shard_map.182
  89.0 4.6 %all-to-all-start.3 = ((bf16[64,8,512]{2,1,0:T(8,128)(2,1)}), bf16[64,8,512]{2,1,0:T(8,128)(2,1)S(1)}, u32[]{:S(2)}, u32[]{:S(2)}) async-start(bf16[64,8,512]{2,1,0:T(8,128)(2,1)} %shard_map.182), calls=%async_computation.3 | async-start | bytes 1048576 | tf_op jit(solution)/shard_map/all_to_all | solution.py:23
  93.7 0.0 copy-done.5
  93.7 0.1 reshape.69
  93.8 0.1 reshape.74.target_ref
  93.9 0.0 copy-done.3
  93.9 15.6 %all-to-all-done.3 = bf16[64,8,512]{2,1,0:T(8,128)(2,1)S(1)} async-done(((bf16[64,8,512]{2,1,0:T(8,128)(2,1)}), bf16[64,8,512]{2,1,0:T(8,128)(2,1)S(1)}, u32[]{:S(2)}, u32[]{:S(2)}) %all-to-all-start.3) | async-done | bytes 524320 | tf_op jit(solution)/shard_map/all_to_all | solution.py:23
  109.5 4.1 %shard_map.183 = f32[64,1,256]{2,1,0:T(1,128)S(1)} custom-call(s32[1]{0:T(128)} %bitcast.start_ref, bf16[8,64,512]{2,1,0:T(8,128)(2,1)S(1)} %bitcast.15, f32[8,512]{1,0:T(8,128)S(1)} %reshape.68.gain_ref, s32[64,1]{1,0:T(8,128)S(1)} %reshape.74.target_ref, bf16[8,4096,128]{2,1,0:T(8,128)(2,1)} %bitcast.19), custom_call_target="tpu_custom_call" | custom-call | flops 536870912 | bytes 9437184 | tf_op jit(solution)/shard_map/pallas_call | solution.py:517
  113.6 18.8 %all_to_all.31 = f32[64,1,256]{2,1,0:T(1,128)S(1)} all-to-all(f32[64,1,256]{2,1,0:T(1,128)S(1)} %shard_map.183), channel_id=1, replica_groups=mesh['z'=8,'x'=4,'core'=2,'tp'=8] {'z','tp'}, dimensions={0} | all-to-all | bytes 131072 | tf_op jit(solution)/shard_map/all_to_all | solution.py:23
  132.4 0.2 reduce.3
  132.6 0.1 reshape.71
  132.7 0.1 slice_reduce_fusion
  132.9 0.1 sub.41
  133.0 10.2 %all_to_all.32 = f32[8,8,8]{2,1,0:T(8,128)S(1)} all-to-all(f32[8,8,8]{2,1,0:T(8,128)S(1)} %broadcast_in_dim.2), channel_id=1, replica_groups=mesh['z'=8,'x'=4,'core'=2,'tp'=8] {'x','core'}, dimensions={0} | all-to-all | bytes 4096 | tf_op jit(solution)/shard_map/all_to_all | solution.py:23
  143.2 0.1 reshape.72
  143.3 0.0 copy-done.6
  143.3 0.0 copy-start.4
  143.3 0.6 multiply_multiply_fusion
  (10 shorter events, 0.1 us)
Async XLA Ops:
  7.2 8.1 %copy-start = (bf16[128,512]{1,0:T(8,128)(2,1)S(1)}, bf16[128,512]{1,0:T(8,128)(2,1)}, u32[]{:S(2)}) copy-start(bf16[128,512]{1,0:T(8,128)(2,1)} %param.28) | copy-start | bytes 393220
  7.2 86.5 %copy-start.5 = (s32[512]{0:T(512)S(1)}, s32[512]{0:T(512)}, u32[]{:S(2)}) copy-start(s32[512]{0:T(512)} %param.32) | copy-start | bytes 6148
  7.2 86.7 %copy-start.3 = (f32[4096]{0:T(1024)S(1)}, f32[4096]{0:T(1024)}, u32[]{:S(2)}) copy-start(f32[4096]{0:T(1024)} %param.29) | copy-start | bytes 49156
  7.2 52.9 %all-gather.4.cloned.1.call-start = ((), (), s32[]{:S(2)}) async-start(), calls=%async_computation.6 | async-start | bytes 1179648 | tf_op jit(solution)/shard_map/all_gather | solution.py:560
  7.9 101.6 %all-gather.6.cloned.1.call-start = ((), (), s32[]{:S(2)}) async-start(), calls=%async_computation.7 | async-start | bytes 9437184 | tf_op jit(solution)/shard_map/all_gather | solution.py:561
  10.1 9.1 %collective-permute-start = (bf16[16,1408]{1,0:T(8,128)(2,1)}, bf16[16,1408]{1,0:T(8,128)(2,1)S(1)}, u32[]{:S(2)}, u32[]{:S(2)}) collective-permute-start(bf16[16,1408]{1,0:T(8,128)(2,1)} %shard_map.177), channel_id=1, source_target_pairs={{0,8},{8,16},{16,24},{24,32},{32,40},{40,48},{48,56},{56,64},{64,7... | collective-permute-start | bytes 135176 | tf_op jit(solution)/shard_map/ppermute | solution.py:558
  21.0 29.9 %all-to-all-start = ((s16[64,32,128]{2,1,0:T(8,128)(2,1)}), s16[64,32,128]{2,1,0:T(8,128)(2,1)S(1)}, u32[]{:S(2)}, u32[]{:S(2)}) async-start(s16[64,32,128]{2,1,0:T(8,128)(2,1)} %shard_map.178), calls=%async_computation | async-start | bytes 1048576 | tf_op jit(solution)/shard_map/all_to_all | solution.py:23
  33.2 110.1 %copy-start.6 = (f32[512]{0:T(512)S(1)}, f32[512]{0:T(512)}, u32[]{:S(2)}) copy-start(f32[512]{0:T(512)} %param.33) | copy-start | bytes 6148
  33.2 0.7 collective-permute-start.1
  53.1 20.1 %all-to-all-start.1 = ((f32[64,8,128]{2,1,0:T(8,128)}), f32[64,8,128]{2,1,0:T(8,128)S(1)}, u32[]{:S(2)}, u32[]{:S(2)}) async-start(f32[64,8,128]{2,1,0:T(8,128)} %shard_map.179.after_ref), calls=%async_computation.1 | async-start | bytes 524288 | tf_op jit(solution)/shard_map/all_to_all | solution.py:23
  60.1 1.2 copy-start.1
  61.3 0.7 copy-start.2
  89.0 20.5 %all-to-all-start.3 = ((bf16[64,8,512]{2,1,0:T(8,128)(2,1)}), bf16[64,8,512]{2,1,0:T(8,128)(2,1)S(1)}, u32[]{:S(2)}, u32[]{:S(2)}) async-start(bf16[64,8,512]{2,1,0:T(8,128)(2,1)} %shard_map.182), calls=%async_computation.3 | async-start | bytes 1048576 | tf_op jit(solution)/shard_map/all_to_all | solution.py:23
  143.3 0.6 copy-start.4
Sparse Core Ops, SparseCore 0:
  10.2 35.2 all-gather.3
  47.7 57.9 all-gather.5

commit v8 on v6

--- a/solution.py
+++ b/solution.py
@@ -506,8 +506,8 @@
             jnp.where(own, logits[:, k * columns : (k + 1) * columns], 0.0), axis=1, keepdims=True
         )
     place = lax.broadcasted_iota(jnp.int32, (group, 128), 1)
-    found = jnp.where(place == 0, top, jnp.where(place == 1, summed, picked)).T
-    row = jnp.concatenate([found[0:1], found[1:2], found[2:3], found[2:3]], axis=1)
+    found = jnp.where(place == 0, top + jnp.log(summed), picked).T
+    row = jnp.concatenate([found[0:1], found[1:2]], axis=1)
     for k in range(out_ref.shape[0]):
         out_ref[k] = row
 
@@ -516,7 +516,7 @@
     slabs, group, width = chosen.shape
     return pl.pallas_call(
         functools.partial(logits_kernel, stride=stride),
-        out_shape=jax.ShapeDtypeStruct((copies, 1, 4 * group), f32),
+        out_shape=jax.ShapeDtypeStruct((copies, 1, 2 * group), f32),
         in_specs=[pl.BlockSpec(memory_space=pltpu.SMEM), whole, whole, whole, pl.BlockSpec(memory_space=pl.ANY)],
         out_specs=whole,
         scratch_shapes=[pltpu.VMEM(weight.shape, bf16), pltpu.SemaphoreType.DMA((slabs,))],
@@ -584,10 +584,10 @@
     start = (lax.axis_index("z") * subs * ways + lax.axis_index("tp")) * columns
     found = score(start.reshape(1), chosen, final_gain.reshape(planes, -1), own, head_full, ways * columns, chunks)
 
-    found = exchange(found, PLANE).reshape(chunks, 4, group)
+    found = exchange(found, PLANE).reshape(chunks, 2, group)
     top = jnp.max(found[:, 0], axis=0)
-    summed = jnp.sum(found[:, 1] * jnp.exp(found[:, 0] - top[None, :]), axis=0)
-    ref = jnp.sum(found[:, 2], axis=0) - top - jnp.log(summed)
+    summed = jnp.sum(jnp.exp(found[:, 0] - top[None, :]), axis=0)
+    ref = jnp.sum(found[:, 1], axis=0) - top - jnp.log(summed)
     ref = to_everyone(ref.reshape(planes, count), SUB)
     ref_logprob = ref.swapaxes(0, 1).reshape(total)
     token_kl = 0.5 * jnp.square(ref_logprob - policy_logprob)

time: 152 us -> 152 us (level)
  no operation moved by 1% of the time
where the time goes in v8:
time: 152 us
  blocking collectives  63.8 us (42%)
  waiting for transfers between devices  33.8 us (22%)
  starting transfers between devices  22.2 us (15%)
  between operations  14.2 us (9%)
  Pallas kernels  12.5 us (8%)
  local copies, waits for them, and re-layouts  2.91 us (2%)
  other arithmetic  2.1 us (1%)
    all_to_all x4, blocking collectives, exchange(): return lax.all_to_all(blocks, axes, 0, 0, tiled=True)  63.8 us
    all_to_all x2, waiting for transfers between devices, exchange(): return lax.all_to_all(blocks, axes, 0, 0, tiled=True)  18.6 us
    all_to_all x2, starting transfers between devices, exchange(): return lax.all_to_all(blocks, axes, 0, 0, tiled=True)  16.9 us
    all_gather x1, waiting for transfers between devices, body(): out_full = lax.all_gather(out_weight.T, SUB, axis=0, tiled=True)  12 us
    ppermute x1, starting transfers between devices, body(): tail = lax.ppermute(tail, CTX, [(i, i + 1) for i in range(chunks - 1)])  4.5 us
    pallas_call x1, Pallas kernels, score(): pl.pallas_call(functools.partial(logits_kernel, stride=stride), out_shape...  4.11 us
  transfers between devices with their start and end apart: 6, of which 4 were waited for; matrix products, arithmetic and copies ran while one was open for 1% of the time, Pallas kernels for 6%

profile of v8, /device:TPU:1, one launch (start us, length us, event | category | flops | bytes accessed | tf_op | source)
XLA Modules:
  0.0 151.7 jit_solution(16969640331173772000)
XLA Ops:
  7.2 0.0 copy-start
  7.2 0.0 copy-start.5
  7.2 0.0 copy-start.3
  7.2 0.0 all-gather.4.cloned.1.call-start
  7.2 0.7 all-gather.4.cloned.1.call-update
  7.9 0.0 all-gather.6.cloned.1.call-start
  8.0 0.7 all-gather.6.cloned.1.call-update
  8.7 1.4 shard_map.177
  10.1 4.5 %collective-permute-start = (bf16[16,1408]{1,0:T(8,128)(2,1)}, bf16[16,1408]{1,0:T(8,128)(2,1)S(1)}, u32[]{:S(2)}, u32[]{:S(2)}) collective-permute-start(bf16[16,1408]{1,0:T(8,128)(2,1)} %shard_map.177), channel_id=1, source_target_pairs={{0,8},{8,16},{16,24},{24,32},{32,40},{40,48},{48,56},{56,64},{64,7... | collective-permute-start | bytes 135176 | tf_op jit(solution)/shard_map/ppermute | solution.py:558
  14.6 0.7 broadcast_subtract_fusion
  15.2 0.0 copy-done
  15.3 0.2 convolution_convert_fusion
  15.4 1.9 %shard_map.176 = (bf16[128,1280]{1,0:T(8,128)(2,1)S(1)}, bf16[16,1280]{1,0:T(8,128)(2,1)S(1)}, f32[4,1280]{1,0:T(4,128)S(1)}, f32[8,128]{1,0:T(8,128)S(1)}, f32[...) custom-call(s32[1]{0:T(128)} %bitcast.1.base_ref, ...), custom_call_target="tpu_custom_call" | custom-call | flops 16777216 | bytes 2097152 | tf_op jit(solution)/shard_map/pallas_call | solution.py:210
  17.3 1.8 %collective-permute-done.tail_ref = bf16[16,1408]{1,0:T(8,128)(2,1)S(1)} collective-permute-done((bf16[16,1408]{1,0:T(8,128)(2,1)}, bf16[16,1408]{1,0:T(8,128)(2,1)S(1)}, u32[]{:S(2)}, u32[]{:S(2)}) %collective-permute-start) | collective-permute-done | bytes 45088 | tf_op jit(solution)/shard_map/ppermute | solution.py:558
  19.1 1.9 %shard_map.178 = s16[64,32,128]{2,1,0:T(8,128)(2,1)} custom-call(bf16[128,1280]{1,0:T(8,128)(2,1)S(1)} %get-tuple-element.21.values_ref, bf16[16,1280]{1,0:T(8,128)(2,1)S(1)} %get-tuple-element.22.lead_ref, f32[4,1280]{1,0:T(4,128)S(1)} %get-tuple-element.23.taps_ref, f32[8,128]{1,0:T(8,128)S(1)} %get-tuple-element.24.free_ref, ...), custom_call_target="tpu_custom_call" | custom-call | flops 134217728 | bytes 2097152 | tf_op jit(solution)/shard_map/pallas_call | solution.py:311
  21.0 0.0 copy-start.6
  21.0 12.3 %all-to-all-start = ((s16[64,32,128]{2,1,0:T(8,128)(2,1)}), s16[64,32,128]{2,1,0:T(8,128)(2,1)S(1)}, u32[]{:S(2)}, u32[]{:S(2)}) async-start(s16[64,32,128]{2,1,0:T(8,128)(2,1)} %shard_map.178), calls=%async_computation | async-start | bytes 1048576 | tf_op jit(solution)/shard_map/all_to_all | solution.py:23
  33.3 0.7 collective-permute-start.1
  34.0 0.0 collective-permute-done.1.after_ref.residual_ref
  34.0 12.0 %all-gather.4.cloned.1.call-done.full_ref = bf16[512,1024]{1,0:T(8,128)(2,1)} async-done(((bf16[64,1024]{1,0:T(8,128)(2,1)}), bf16[512,1024]{1,0:T(8,128)(2,1)}) %all-gather.4.cloned.1.call-update) | async-done | bytes 1048592 | tf_op jit(solution)/shard_map/all_gather | solution.py:560
  46.0 1.2 copy-done.1
  47.2 0.7 copy-done.2
  47.9 0.1 shard_map.179
  48.0 3.0 %all-to-all-done.came_ref = s16[64,32,128]{2,1,0:T(8,128)(2,1)S(1)} async-done(((s16[64,32,128]{2,1,0:T(8,128)(2,1)}), s16[64,32,128]{2,1,0:T(8,128)(2,1)S(1)}, u32[]{:S(2)}, u32[]{:S(2)}) %all-to-all-start) | async-done | bytes 524320 | tf_op jit(solution)/shard_map/all_to_all | solution.py:23
  51.0 1.5 %shard_map.180 = f32[64,8,128]{2,1,0:T(8,128)S(1)} custom-call(s16[64,32,128]{2,1,0:T(8,128)(2,1)S(1)} %all-to-all-done.came_ref), custom_call_target="tpu_custom_call" | custom-call | flops 268435456 | bytes 1048576 | tf_op jit(solution)/shard_map/pallas_call | solution.py:400
  52.6 21.9 %all_to_all.30 = f32[64,8,128]{2,1,0:T(8,128)S(1)} all-to-all(f32[64,8,128]{2,1,0:T(8,128)S(1)} %shard_map.180), channel_id=1, replica_groups=mesh['z'=8,'x'=4,'core'=2,'tp'=8] {'z','x','core'}, dimensions={0} | all-to-all | bytes 524288 | tf_op jit(solution)/shard_map/all_to_all | solution.py:23
  74.4 0.7 shard_map.181
  75.2 13.2 %all_to_all.31.partial_ref = f32[8,8,512]{2,1,0:T(8,128)S(1)} all-to-all(f32[8,8,512]{2,1,0:T(8,128)S(1)} %bitcast.14), channel_id=1, replica_groups=mesh['z'=8,'x'=4,'core'=2,'tp'=8] {'tp'}, dimensions={0} | all-to-all | bytes 262144 | tf_op jit(solution)/shard_map/all_to_all | solution.py:23
  88.3 0.9 shard_map.182
  89.2 4.6 %all-to-all-start.3 = ((bf16[64,8,512]{2,1,0:T(8,128)(2,1)}), bf16[64,8,512]{2,1,0:T(8,128)(2,1)S(1)}, u32[]{:S(2)}, u32[]{:S(2)}) async-start(bf16[64,8,512]{2,1,0:T(8,128)(2,1)} %shard_map.182), calls=%async_computation.3 | async-start | bytes 1048576 | tf_op jit(solution)/shard_map/all_to_all | solution.py:23
  93.8 0.0 copy-done.5
  93.9 0.1 reshape.69
  94.0 0.1 reshape.74.target_ref
  94.1 0.0 copy-done.3
  94.1 15.6 %all-to-all-done.3 = bf16[64,8,512]{2,1,0:T(8,128)(2,1)S(1)} async-done(((bf16[64,8,512]{2,1,0:T(8,128)(2,1)}), bf16[64,8,512]{2,1,0:T(8,128)(2,1)S(1)}, u32[]{:S(2)}, u32[]{:S(2)}) %all-to-all-start.3) | async-done | bytes 524320 | tf_op jit(solution)/shard_map/all_to_all | solution.py:23
  109.7 4.1 %shard_map.183 = f32[64,1,128]{2,1,0:T(1,128)S(1)} custom-call(s32[1]{0:T(128)} %bitcast.start_ref, bf16[8,64,512]{2,1,0:T(8,128)(2,1)S(1)} %bitcast.12, f32[8,512]{1,0:T(8,128)S(1)} %reshape.68.gain_ref, s32[64,1]{1,0:T(8,128)S(1)} %reshape.74.target_ref, bf16[8,4096,128]{2,1,0:T(8,128)(2,1)} %bitcast.16), custom_call_target="tpu_custom_call" | custom-call | flops 536870912 | bytes 9437184 | tf_op jit(solution)/shard_map/pallas_call | solution.py:517
  113.8 18.6 %all_to_all.32 = f32[64,1,128]{2,1,0:T(1,128)S(1)} all-to-all(f32[64,1,128]{2,1,0:T(1,128)S(1)} %shard_map.183), channel_id=1, replica_groups=mesh['z'=8,'x'=4,'core'=2,'tp'=8] {'z','tp'}, dimensions={0} | all-to-all | bytes 65536 | tf_op jit(solution)/shard_map/all_to_all | solution.py:23
  132.4 0.5 broadcast.8
  132.9 0.7 reduce.9
  133.6 0.1 reshape.71
  133.7 0.1 slice_reduce_fusion
  133.9 0.1 sub.41
  134.0 10.2 %all_to_all.33 = f32[8,8,8]{2,1,0:T(8,128)S(1)} all-to-all(f32[8,8,8]{2,1,0:T(8,128)S(1)} %broadcast_in_dim.2), channel_id=1, replica_groups=mesh['z'=8,'x'=4,'core'=2,'tp'=8] {'x','core'}, dimensions={0} | all-to-all | bytes 4096 | tf_op jit(solution)/shard_map/all_to_all | solution.py:23
  144.2 0.1 reshape.72
  144.3 0.0 copy-done.6
  144.3 0.0 copy-start.4
  144.3 0.6 multiply_multiply_fusion
  144.9 0.0 copy-done.4
  (9 shorter events, 0.1 us)
Async XLA Ops:
  7.2 8.1 %copy-start = (bf16[128,512]{1,0:T(8,128)(2,1)S(1)}, bf16[128,512]{1,0:T(8,128)(2,1)}, u32[]{:S(2)}) copy-start(bf16[128,512]{1,0:T(8,128)(2,1)} %param.28) | copy-start | bytes 393220
  7.2 86.7 %copy-start.5 = (s32[512]{0:T(512)S(1)}, s32[512]{0:T(512)}, u32[]{:S(2)}) copy-start(s32[512]{0:T(512)} %param.32) | copy-start | bytes 6148
  7.2 86.9 %copy-start.3 = (f32[4096]{0:T(1024)S(1)}, f32[4096]{0:T(1024)}, u32[]{:S(2)}) copy-start(f32[4096]{0:T(1024)} %param.29) | copy-start | bytes 49156
  7.2 38.8 %all-gather.4.cloned.1.call-start = ((), (), s32[]{:S(2)}) async-start(), calls=%async_computation.6 | async-start | bytes 1179648 | tf_op jit(solution)/shard_map/all_gather | solution.py:560
  7.9 101.8 %all-gather.6.cloned.1.call-start = ((), (), s32[]{:S(2)}) async-start(), calls=%async_computation.7 | async-start | bytes 9437184 | tf_op jit(solution)/shard_map/all_gather | solution.py:561
  10.1 9.1 %collective-permute-start = (bf16[16,1408]{1,0:T(8,128)(2,1)}, bf16[16,1408]{1,0:T(8,128)(2,1)S(1)}, u32[]{:S(2)}, u32[]{:S(2)}) collective-permute-start(bf16[16,1408]{1,0:T(8,128)(2,1)} %shard_map.177), channel_id=1, source_target_pairs={{0,8},{8,16},{16,24},{24,32},{32,40},{40,48},{48,56},{56,64},{64,7... | collective-permute-start | bytes 135176 | tf_op jit(solution)/shard_map/ppermute | solution.py:558
  21.0 123.3 %copy-start.6 = (f32[512]{0:T(512)S(1)}, f32[512]{0:T(512)}, u32[]{:S(2)}) copy-start(f32[512]{0:T(512)} %param.33) | copy-start | bytes 6148
  21.0 30.0 %all-to-all-start = ((s16[64,32,128]{2,1,0:T(8,128)(2,1)}), s16[64,32,128]{2,1,0:T(8,128)(2,1)S(1)}, u32[]{:S(2)}, u32[]{:S(2)}) async-start(s16[64,32,128]{2,1,0:T(8,128)(2,1)} %shard_map.178), calls=%async_computation | async-start | bytes 1048576 | tf_op jit(solution)/shard_map/all_to_all | solution.py:23
  33.3 0.7 collective-permute-start.1
  46.0 1.2 copy-start.1
  47.2 0.7 copy-start.2
  89.2 20.5 %all-to-all-start.3 = ((bf16[64,8,512]{2,1,0:T(8,128)(2,1)}), bf16[64,8,512]{2,1,0:T(8,128)(2,1)S(1)}, u32[]{:S(2)}, u32[]{:S(2)}) async-start(bf16[64,8,512]{2,1,0:T(8,128)(2,1)} %shard_map.182), calls=%async_computation.3 | async-start | bytes 1048576 | tf_op jit(solution)/shard_map/all_to_all | solution.py:23
  144.3 0.6 copy-start.4
Sparse Core Ops, SparseCore 0:
  10.2 35.7 all-gather.3
  48.2 58.0 all-gather.5
